TPU v7x, 32 devices: a whole 2x2x4 slice. The times are simulated.
32 devices in a mesh: seq: 8 (over z, y), uly: 4 (over x, core).
Axes of the slice: x: 2, y: 2, z: 4, core: 2. Of those that a mesh axis runs over, the one named last changes fastest.
Arguments:
- queries: bfloat16 [4096, 5120], P(('seq', 'uly')), may hold values from -27 to 27
- keys: bfloat16 [4096, 5120], P(('seq', 'uly')), may hold values from -9 to 9
- values: bfloat16 [4096, 5120], P(('seq', 'uly')), may hold values from -6 to 6
- block_lists: int32 [32, 12], P('seq'), may hold values from 0 to 31, as said below
- block_counts: int32 [32], P('seq'), may hold values from 4 to 12
Outputs:
- attended: bfloat16 [4096, 5120], P(('seq', 'uly'))
Inputs may be any that keep to these rules, and one draw needn't show every extreme that they name: `block_lists`: each row names 12 different blocks, its first entry being the query block itself; only the first block_counts entries of a row are used, the rest are block numbers too. Over the used entries of the 4 query blocks of one group (blocks g * 4 to (g + 1) * 4 - 1), at most 2 different blocks of any other group are named, and in every group exactly 2 of some other group.
All inputs are finite; a program needn't handle non-finite values.
Results may differ from a plain program's by a relative error of at most 0.003.
Values may be sent and summed in bfloat16 or wider, within the bound.
No kernel may reach another device: no remote copies, remote signals or barrier semaphores. Data moves between devices by JAX's collectives and lax.ppermute only.
A program may use at most 128 MiB of HBM per device.

v0:
```python
import jax
import jax.numpy as jnp
from jax import lax
from jax.sharding import PartitionSpec as P

HEAD_DIM = 128
BLOCK_LEN = 128
LIST_LEN = 12
PEER_SLOTS = 2


def finish(scores, value_part, block_count, entry_ids):
    live_keys = jnp.repeat(entry_ids < block_count, BLOCK_LEN)
    scores = jnp.where(live_keys[None, None, :], scores, -jnp.inf)
    row_max = jnp.max(scores, axis=2, keepdims=True)
    weights = jnp.exp(scores - row_max)
    weight_sum = jnp.sum(weights, axis=2)
    blended = jnp.einsum(
        "hqk,khd->qhd", weights.astype(jnp.bfloat16), value_part, preferred_element_type=jnp.float32
    )
    result = blended / jnp.transpose(weight_sum)[:, :, None]
    return result.astype(jnp.bfloat16)


def body(queries, keys, values, block_lists, block_counts):
    q_heads, k_heads, v_heads = (
        lax.all_to_all(queries, "uly", split_axis=1, concat_axis=0, tiled=True),
        lax.all_to_all(keys, "uly", split_axis=1, concat_axis=0, tiled=True),
        lax.all_to_all(values, "uly", split_axis=1, concat_axis=0, tiled=True),
    )
    row_count, feat_width = q_heads.shape
    group_blocks = row_count // BLOCK_LEN
    groups = lax.axis_size("seq")
    my_group = lax.axis_index("seq")
    head_count = feat_width // HEAD_DIM
    total_blocks = groups * group_blocks
    kv_pairs = jnp.concatenate([k_heads, v_heads], axis=1).reshape(
        group_blocks, BLOCK_LEN, 2 * feat_width
    )
    entry_ids = jnp.arange(LIST_LEN, dtype=jnp.int32)
    live_entry = entry_ids[None, :] < block_counts[:, None]
    block_ids = jnp.arange(total_blocks, dtype=jnp.int32)
    matches = block_lists[:, :, None] == block_ids[None, None, :]
    owners = block_ids // group_blocks
    remote = owners != my_group
    needed = (jnp.any(matches & live_entry[:, :, None], axis=(0, 1)) & remote).astype(jnp.int32)
    needed = needed.reshape(groups, group_blocks)
    asked_for = lax.all_to_all(needed, "seq", split_axis=0, concat_axis=0, tiled=True)
    ask_rank = jnp.cumsum(asked_for, axis=1) - 1
    slot_ids = jnp.arange(PEER_SLOTS, dtype=jnp.int32)
    chosen = (asked_for[:, None, :] == 1) & (ask_rank[:, None, :] == slot_ids[None, :, None])
    picked = jnp.sum(
        chosen.astype(jnp.int32) * jnp.arange(group_blocks, dtype=jnp.int32)[None, None, :], axis=2
    )
    outgoing = jnp.take(kv_pairs, picked.reshape(-1), axis=0).reshape(
        groups, PEER_SLOTS, BLOCK_LEN, 2 * feat_width
    )
    arrived = lax.all_to_all(outgoing, "seq", split_axis=0, concat_axis=0, tiled=True)
    pool = jnp.concatenate(
        [kv_pairs, arrived.reshape(groups * PEER_SLOTS, BLOCK_LEN, 2 * feat_width)], axis=0
    )
    need_rank = (jnp.cumsum(needed, axis=1) - 1).reshape(-1)
    slot_table = jnp.where(
        remote, group_blocks + owners * PEER_SLOTS + need_rank, block_ids % group_blocks
    )
    entry_slot = jnp.sum(matches.astype(jnp.int32) * slot_table[None, None, :], axis=2)
    entry_slot = jnp.clip(entry_slot, 0, pool.shape[0] - 1)
    q_blocks = q_heads.reshape(group_blocks, BLOCK_LEN, head_count, HEAD_DIM)
    score_scale = HEAD_DIM ** (-0.5)

    def attend(inputs):
        q_block, slot_list, block_count = inputs
        gathered = jnp.take(pool, slot_list, axis=0).reshape(
            LIST_LEN * BLOCK_LEN, 2, head_count, HEAD_DIM
        )
        scores = (
            jnp.einsum("qhd,khd->hqk", q_block, gathered[:, 0], preferred_element_type=jnp.float32)
            * score_scale
        )
        result = finish(scores, gathered[:, 1], block_count, entry_ids)
        return result.reshape(BLOCK_LEN, head_count * HEAD_DIM)

    attended = lax.map(attend, (q_blocks, entry_slot, block_counts))
    return lax.all_to_all(
        attended.reshape(row_count, feat_width), "uly", split_axis=0, concat_axis=1, tiled=True
    )


def solution(mesh):
    placed = (
        P(("seq", "uly"), None),
        P(("seq", "uly"), None),
        P(("seq", "uly"), None),
        P("seq", None),
        P("seq"),
    )
    return jax.shard_map(
        body, mesh=mesh, in_specs=placed, out_specs=P(("seq", "uly"), None), check_vma=False
    )
```

profile of v0, /device:TPU:0, one launch (start us, length us, event | category | flops | bytes accessed | tf_op | source)
XLA Modules:
  0.0 572.6 jit_solution(12595250846918938351)
XLA Ops:
  2.4 7.3 %all-to-all-start.2 = ((s32[8,1,4]{2,1,0:T(1,128)}), s32[8,1,4]{2,1,0:T(1,128)S(1)}, u32[]{:S(2)}, u32[]{:S(2)}) async-start(s32[8,1,4]{2,1,0:T(1,128)} %copy.69), calls=%async_computation.2 | async-start | bytes 8192 | tf_op jit(solution)/shard_map/all_to_all | solution.py:48
  22.2 14.7 %all-to-all-done = bf16[128,4,1280]{0,2,1:T(8,128)(2,1)S(1)} async-done(((bf16[128,4,1280]{0,2,1:T(8,128)(2,1)}), bf16[128,4,1280]{0,2,1:T(8,128)(2,1)S(1)}, u32[]{:S(2)}, u32[]{:S(2)}) %all-to-all-start) | async-done | bytes 1310752 | tf_op jit(solution)/shard_map/all_to_all | solution.py:28
  40.9 16.7 %all-to-all-done.1 = bf16[128,4,1280]{0,2,1:T(8,128)(2,1)S(1)} async-done(((bf16[128,4,1280]{0,2,1:T(8,128)(2,1)}), bf16[128,4,1280]{0,2,1:T(8,128)(2,1)S(1)}, u32[]{:S(2)}, u32[]{:S(2)}) %all-to-all-start.1) | async-done | bytes 1310752 | tf_op jit(solution)/shard_map/all_to_all | solution.py:29
  60.6 5.6 gather_fusion.1
  66.2 10.1 %broadcast_select_fusion = bf16[8,2,128,2560]{2,3,1,0:T(8,128)(2,1)} fusion(bf16[8,2,128,2560]{2,3,1,0:T(8,128)(2,1)} %bitcast.84, pred[8,2]{1,0:T(8,128)(4,1)S(1)} %copy.74), kind=kLoop, calls=%fused_computation.36 | loop fusion | flops 5242880 | bytes 20971536 | tf_op jit(solution)/shard_map/jit(_take)/select_n | solution.py:55
  76.3 5.1 all-to-all-start.3
  84.2 225.3 %all-to-all-done.3 = bf16[8,2,128,2560]{2,3,1,0:T(8,128)(2,1)} async-done(((bf16[8,2,128,2560]{2,3,1,0:T(8,128)(2,1)}), bf16[8,2,128,2560]{2,3,1,0:T(8,128)(2,1)}, u32[]{:S(2)}, u32[]{:S(2)}) %all-to-all-start.3) | async-done | bytes 10485792 | tf_op jit(solution)/shard_map/all_to_all | solution.py:58
  309.5 4.3 all-to-all-start.4
  316.9 14.0 %copy.76 = bf16[8,2,128,2560]{3,2,1,0:T(8,128)(2,1)} copy(bf16[8,2,128,2560]{2,3,1,0:T(8,128)(2,1)} %all-to-all-done.3) | data formatting | bytes 20971520 | tf_op jit(solution)/shard_map/all_to_all | solution.py:58
  330.9 11.6 %pad_maximum_fusion = bf16[20,128,2560]{2,1,0:T(8,128)(2,1)} fusion(bf16[16,128,2560]{2,1,0:T(8,128)(2,1)} %bitcast.83, bf16[4,128,2560]{2,1,0:T(8,128)(2,1)S(1)} %copy-done), kind=kLoop, calls=%fused_computation.35 | loop fusion | flops 6553600 | bytes 26214400 | tf_op jit(solution)/shard_map/concatenate | solution.py:59
  342.5 207.9 %while.11 = (s32[]{:T(128)}, bf16[4,128,1280]{1,2,0:T(8,128)(2,1)}, s32[4,12]{1,0:T(4,128)S(1)}, bf16[20,128,2560]{2,1,0:T(8,128)(2,1)}, s32[4]{0:T(128)S(1)}, /*index=5*/bf16[4,128,10,128]{1,3,2,0:T(8,128)(2,1)}, s32[]{:T(128)}) while((s32[]{:T(128)}, bf16[4,128,1280]{1,2,0:T(8,128)(2,1)}, s32[4,12]{1,0:T(4,128)S(1)}, ...), condition=%wide.region_8.9_spmd.clone, body=%wide.region_5.8_spmd.clone.sunk | while | flops 1032518272 | bytes 103593904 | solution.py:83
  342.5 9.5 %gather_fusion = bf16[12,128,2560]{2,1,0:T(8,128)(2,1)} fusion(bf16[20,128,2560]{2,1,0:T(8,128)(2,1)} %get-tuple-element.153, s32[1024]{0:T(1024)S(1)} %pad_clamp_fusion.3), kind=kCustom, calls=%fused_computation.clone.clone.1 | custom fusion | bytes 15728688 | tf_op jit(solution)/shard_map/while/body/eval_jaxpr/jit(_take)/gather | solution.py:73
  352.1 16.1 %reshape.292 = bf16[1536,2,10,128]{3,2,1,0:T(8,128)(2,1)} reshape(bf16[12,128,2560]{2,1,0:T(8,128)(2,1)} %gather_fusion) | data formatting | bytes 15728640 | tf_op jit(solution)/shard_map/while/body/eval_jaxpr/jit(_take)/gather | solution.py:73
  368.3 15.9 %copy_select_fusion.2 = bf16[1536,2,10,128]{3,0,2,1:T(8,128)(2,1)} fusion(bf16[1536,2,10,128]{3,2,1,0:T(8,128)(2,1)} %reshape.292, pred[1536]{0:T(1024)(128)(4,1)S(1)} %broadcast_bitcast_fusion.5), kind=kLoop, calls=%fused_computation.3.clone.1 | loop fusion | flops 3932160 | bytes 15730176 | tf_op jit(solution)/shard_map/while/body/eval_jaxpr/jit(_take)/select_n | solution.py:73
  394.5 9.5 %gather_fusion = bf16[12,128,2560]{2,1,0:T(8,128)(2,1)} fusion(bf16[20,128,2560]{2,1,0:T(8,128)(2,1)} %get-tuple-element.153, s32[1024]{0:T(1024)S(1)} %pad_clamp_fusion.3), kind=kCustom, calls=%fused_computation.clone.clone.1 | custom fusion | bytes 15728688 | tf_op jit(solution)/shard_map/while/body/eval_jaxpr/jit(_take)/gather | solution.py:73
  404.0 16.1 %reshape.292 = bf16[1536,2,10,128]{3,2,1,0:T(8,128)(2,1)} reshape(bf16[12,128,2560]{2,1,0:T(8,128)(2,1)} %gather_fusion) | data formatting | bytes 15728640 | tf_op jit(solution)/shard_map/while/body/eval_jaxpr/jit(_take)/gather | solution.py:73
  420.2 15.9 %copy_select_fusion.2 = bf16[1536,2,10,128]{3,0,2,1:T(8,128)(2,1)} fusion(bf16[1536,2,10,128]{3,2,1,0:T(8,128)(2,1)} %reshape.292, pred[1536]{0:T(1024)(128)(4,1)S(1)} %broadcast_bitcast_fusion.5), kind=kLoop, calls=%fused_computation.3.clone.1 | loop fusion | flops 3932160 | bytes 15730176 | tf_op jit(solution)/shard_map/while/body/eval_jaxpr/jit(_take)/select_n | solution.py:73
  446.4 9.5 %gather_fusion = bf16[12,128,2560]{2,1,0:T(8,128)(2,1)} fusion(bf16[20,128,2560]{2,1,0:T(8,128)(2,1)} %get-tuple-element.153, s32[1024]{0:T(1024)S(1)} %pad_clamp_fusion.3), kind=kCustom, calls=%fused_computation.clone.clone.1 | custom fusion | bytes 15728688 | tf_op jit(solution)/shard_map/while/body/eval_jaxpr/jit(_take)/gather | solution.py:73
  456.0 16.1 %reshape.292 = bf16[1536,2,10,128]{3,2,1,0:T(8,128)(2,1)} reshape(bf16[12,128,2560]{2,1,0:T(8,128)(2,1)} %gather_fusion) | data formatting | bytes 15728640 | tf_op jit(solution)/shard_map/while/body/eval_jaxpr/jit(_take)/gather | solution.py:73
  472.1 15.9 %copy_select_fusion.2 = bf16[1536,2,10,128]{3,0,2,1:T(8,128)(2,1)} fusion(bf16[1536,2,10,128]{3,2,1,0:T(8,128)(2,1)} %reshape.292, pred[1536]{0:T(1024)(128)(4,1)S(1)} %broadcast_bitcast_fusion.5), kind=kLoop, calls=%fused_computation.3.clone.1 | loop fusion | flops 3932160 | bytes 15730176 | tf_op jit(solution)/shard_map/while/body/eval_jaxpr/jit(_take)/select_n | solution.py:73
  498.4 9.5 %gather_fusion = bf16[12,128,2560]{2,1,0:T(8,128)(2,1)} fusion(bf16[20,128,2560]{2,1,0:T(8,128)(2,1)} %get-tuple-element.153, s32[1024]{0:T(1024)S(1)} %pad_clamp_fusion.3), kind=kCustom, calls=%fused_computation.clone.clone.1 | custom fusion | bytes 15728688 | tf_op jit(solution)/shard_map/while/body/eval_jaxpr/jit(_take)/gather | solution.py:73
  507.9 16.1 %reshape.292 = bf16[1536,2,10,128]{3,2,1,0:T(8,128)(2,1)} reshape(bf16[12,128,2560]{2,1,0:T(8,128)(2,1)} %gather_fusion) | data formatting | bytes 15728640 | tf_op jit(solution)/shard_map/while/body/eval_jaxpr/jit(_take)/gather | solution.py:73
  524.1 15.9 %copy_select_fusion.2 = bf16[1536,2,10,128]{3,0,2,1:T(8,128)(2,1)} fusion(bf16[1536,2,10,128]{3,2,1,0:T(8,128)(2,1)} %reshape.292, pred[1536]{0:T(1024)(128)(4,1)S(1)} %broadcast_bitcast_fusion.5), kind=kLoop, calls=%fused_computation.3.clone.1 | loop fusion | flops 3932160 | bytes 15730176 | tf_op jit(solution)/shard_map/while/body/eval_jaxpr/jit(_take)/select_n | solution.py:73
  550.4 20.8 %all_to_all.75 = bf16[4,128,1280]{1,2,0:T(8,128)(2,1)S(1)} all-to-all(bf16[4,128,1280]{1,2,0:T(8,128)(2,1)} %get-tuple-element.42), channel_id=1, replica_groups=mesh['seq'=8,'uly'=4] {'uly'}, dimensions={0} | all-to-all | bytes 2621440 | tf_op jit(solution)/shard_map/all_to_all | solution.py:84
  (111 shorter events, 70.6 us)
Async XLA Ops:
  2.4 13.7 %all-to-all-start.2 = ((s32[8,1,4]{2,1,0:T(1,128)}), s32[8,1,4]{2,1,0:T(1,128)S(1)}, u32[]{:S(2)}, u32[]{:S(2)}) async-start(s32[8,1,4]{2,1,0:T(1,128)} %copy.69), calls=%async_computation.2 | async-start | bytes 8192 | tf_op jit(solution)/shard_map/all_to_all | solution.py:48
  16.1 20.8 %all-to-all-start = ((bf16[128,4,1280]{0,2,1:T(8,128)(2,1)}), bf16[128,4,1280]{0,2,1:T(8,128)(2,1)S(1)}, u32[]{:S(2)}, u32[]{:S(2)}) async-start(bf16[128,4,1280]{0,2,1:T(8,128)(2,1)} %bitcast), calls=%async_computation | async-start | bytes 2621440 | tf_op jit(solution)/shard_map/all_to_all | solution.py:28
  36.9 20.8 %copy-start.1 = (bf16[128,4,1280]{0,2,1:T(8,128)(2,1)}, bf16[128,4,1280]{0,2,1:T(8,128)(2,1)S(1)}, u32[]{:S(2)}) copy-start(bf16[128,4,1280]{0,2,1:T(8,128)(2,1)S(1)} %all-to-all-done) | copy-start | bytes 3932164
  36.9 20.8 %all-to-all-start.1 = ((bf16[128,4,1280]{0,2,1:T(8,128)(2,1)}), bf16[128,4,1280]{0,2,1:T(8,128)(2,1)S(1)}, u32[]{:S(2)}, u32[]{:S(2)}) async-start(bf16[128,4,1280]{0,2,1:T(8,128)(2,1)} %bitcast.88), calls=%async_computation.1 | async-start | bytes 2621440 | tf_op jit(solution)/shard_map/all_to_all | solution.py:29
  57.7 1.1 copy-start.2
  76.3 233.2 %all-to-all-start.3 = ((bf16[8,2,128,2560]{2,3,1,0:T(8,128)(2,1)}), bf16[8,2,128,2560]{2,3,1,0:T(8,128)(2,1)}, u32[]{:S(2)}, u32[]{:S(2)}) async-start(bf16[8,2,128,2560]{2,3,1,0:T(8,128)(2,1)} %broadcast_select_fusion), calls=%async_computation.3 | async-start | bytes 20971520 | tf_op jit(solution)/shard_map/all_to_all | solution.py:58
  309.5 33.0 %all-to-all-start.4 = ((bf16[128,4,1280]{0,2,1:T(8,128)(2,1)}), bf16[128,4,1280]{0,2,1:T(8,128)(2,1)}, u32[]{:S(2)}, u32[]{:S(2)}) async-start(bf16[128,4,1280]{0,2,1:T(8,128)(2,1)} %bitcast.89), calls=%async_computation.4 | async-start | bytes 2621440 | tf_op jit(solution)/shard_map/all_to_all | solution.py:27
  316.9 14.0 %copy-start = (bf16[4,128,2560]{2,1,0:T(8,128)(2,1)S(1)}, bf16[4,128,2560]{2,1,0:T(8,128)(2,1)}, u32[]{:S(2)}) copy-start(bf16[4,128,2560]{2,1,0:T(8,128)(2,1)} %copy.77) | copy-start | bytes 7864324
  330.9 11.6 %copy-start.3 = (s32[4]{0:T(128)S(1)}, s32[4]{0:T(128)}, u32[]{:S(2)}) copy-start(s32[4]{0:T(128)} %param.11) | copy-start | bytes 52
  385.5 5.6 slice-start
  385.5 5.6 slice-start.1
  437.4 5.6 slice-start
  437.4 5.6 slice-start.1
  489.4 5.6 slice-start
  489.4 5.6 slice-start.1
  541.4 5.6 slice-start
  541.4 5.6 slice-start.1
where the time goes:
time: 576 us; the launch traced here: 573 us
  waiting for transfers between devices  261 us (45%)
  local copies, waits for them, and re-layouts  143 us (25%)
  other arithmetic  98.6 us (17%)
  matrix products  25.6 us (4%)
  starting transfers between devices  23.8 us (4%)
  blocking collectives  20.8 us (4%)
    all_to_all x1, waiting for transfers between devices, body(): lax.all_to_all(outgoing, 'seq', split_axis=0, concat_axis=0, tiled=True)  225 us
    gather x8, local copies, waits for them, and re-layouts, attend(): jnp.take(pool, slot_list, axis=0)  102 us
    select_n x8, other arithmetic, attend(): jnp.take(pool, slot_list, axis=0)  63.8 us
    all_to_all x1, blocking collectives, body(): lax.all_to_all(attended.reshape(row_count, feat_width), 'uly', split_axis...  20.8 us
    all_to_all x1, waiting for transfers between devices, body(): lax.all_to_all(values, 'uly', split_axis=1, concat_axis=0, tiled=True)  16.7 us
    dot_general x4, matrix products, attend(): jnp.einsum('qhd,khd->hqk', q_block, gathered[:, 0], preferred_element_typ...  15.2 us
    all_to_all x1, waiting for transfers between devices, body(): lax.all_to_all(keys, 'uly', split_axis=1, concat_axis=0, tiled=True)  14.7 us
    all_to_all x1, local copies, waits for them, and re-layouts, body(): lax.all_to_all(outgoing, 'seq', split_axis=0, concat_axis=0, tiled=True)  14 us
  transfers between devices with their start and end apart: 5, of which 4 were waited for; matrix products, arithmetic and copies ran while one was open for 6% of the time, Pallas kernels for 0%

commit v1 on v0

v1 whole, which is shorter than its diff:
```python
import functools
import math

import jax
import jax.numpy as jnp
from jax import lax
from jax.experimental import pallas as pl
from jax.experimental.pallas import tpu as pltpu
from jax.sharding import PartitionSpec as P

HEAD_DIM = 128
BLOCK_LEN = 128
LIST_LEN = 12
MIN_COUNT = 4
ROW = LIST_LEN + 1
VMEM_LIMIT = 56 * 1024 * 1024
CHUNK = 2
SCORE_FACTOR = HEAD_DIM**-0.5 * math.log2(math.e)
ANY = pl.BlockSpec(memory_space=pl.ANY)
SMEM = pl.BlockSpec(memory_space=pltpu.SMEM)
DEVICES = ("seq", "uly")


def swap(x, axis, bit):
    return lax.ppermute(x, axis, [(i, i ^ bit) for i in range(lax.axis_size(axis))])


def gather_all(x, axis):
    parts = {0: x}
    bit = lax.axis_size(axis) // 2
    while bit:
        parts.update({rel | bit: swap(part, axis, bit) for rel, part in list(parts.items())})
        bit //= 2
    return [parts[rel] for rel in range(lax.axis_size(axis))]


def gather_tables(block_lists, block_counts):
    table = jnp.concatenate([block_lists, block_counts[:, None]], axis=1).reshape(-1)
    bit = 1
    while bit < lax.axis_size("seq"):
        table = jnp.concatenate([table, swap(table, "seq", bit)])
        bit *= 2
    return table


def table_row(block, group_blocks):
    group = block // group_blocks
    return ((group ^ lax.axis_index("seq")) * group_blocks + block % group_blocks) * ROW


def pack_all_kernel(full, step, k_ref, v_ref, q_ref, out_ref):
    for d in range(step):
        for part, src in enumerate((k_ref, v_ref, q_ref)):
            for i in range(full):
                col = (d * full + i) * HEAD_DIM
                row = (part * full + i) * BLOCK_LEN
                out_ref[d, row : row + BLOCK_LEN] = src[:, col : col + HEAD_DIM]


def pack_all(queries, keys, values, full, devices):
    step = devices // 4
    block = pl.BlockSpec((BLOCK_LEN, step * full * HEAD_DIM), lambda j: (0, j))
    rows = 3 * full * BLOCK_LEN
    return pl.pallas_call(
        functools.partial(pack_all_kernel, full, step),
        grid=(devices // step,),
        out_shape=jax.ShapeDtypeStruct((devices, rows, HEAD_DIM), queries.dtype),
        in_specs=[block] * 3,
        out_specs=pl.BlockSpec((step, rows, HEAD_DIM), lambda j: (j, 0, 0)),
        cost_estimate=pl.CostEstimate(
            flops=0, transcendentals=0, bytes_accessed=devices * rows * HEAD_DIM * 4
        ),
        compiler_params=pltpu.CompilerParams(vmem_limit_bytes=VMEM_LIMIT),
        name="pack_all",
    )(keys, values, queries)


def pack_rest_kernel(head_axis, start, each, first, count, peers, k_ref, v_ref, q_ref, *refs):
    outs, bufs, sem = refs[:peers], refs[peers : peers + 3], refs[peers + 3]
    me = lax.axis_index(head_axis)
    width = peers * each * HEAD_DIM
    copies = [
        pltpu.make_async_copy(src.at[:, pl.ds(start * HEAD_DIM, width)], buf, sem)
        for src, buf in zip((k_ref, v_ref, q_ref), bufs)
    ]
    for copy in copies:
        copy.start()
    for copy in copies:
        copy.wait()
    for rel in range(peers):
        for part, buf in enumerate(bufs):
            for i in range(count):
                col = pl.multiple_of(((me ^ rel) * each + first + i) * HEAD_DIM, HEAD_DIM)
                row = (part * count + i) * BLOCK_LEN
                outs[rel][row : row + BLOCK_LEN] = buf[:, pl.ds(col, HEAD_DIM)]


def pack_rest(queries, keys, values, head_axis, start, each, first, count):
    peers = lax.axis_size(head_axis)
    rows = 3 * count * BLOCK_LEN
    return pl.pallas_call(
        functools.partial(pack_rest_kernel, head_axis, start, each, first, count, peers),
        out_shape=[jax.ShapeDtypeStruct((rows, HEAD_DIM), queries.dtype)] * peers,
        in_specs=[ANY] * 3,
        out_specs=[pl.BlockSpec(memory_space=pltpu.VMEM)] * peers,
        scratch_shapes=[pltpu.VMEM((BLOCK_LEN, peers * each * HEAD_DIM), queries.dtype)] * 3
        + [pltpu.SemaphoreType.DMA],
        cost_estimate=pl.CostEstimate(
            flops=0, transcendentals=0, bytes_accessed=peers * rows * HEAD_DIM * 4
        ),
        compiler_params=pltpu.CompilerParams(vmem_limit_bytes=VMEM_LIMIT),
        name="pack_rest",
    )(keys, values, queries)


def attend_block(q, pairs, used, write):
    def run(entries):
        keys, values = pairs(entries)
        over = jnp.where(used >= entries, 0.0, -jnp.inf).astype(jnp.float32)
        s = [
            lax.dot_general(q, k_e, (((1,), (1,)), ((), ())), preferred_element_type=jnp.float32)
            for k_e in keys
        ]
        s[-1] = s[-1] + over
        top = jnp.max(functools.reduce(jnp.maximum, s), axis=1, keepdims=True)
        w = [jnp.exp2((s_e - top) * SCORE_FACTOR) for s_e in s]
        total = jnp.sum(functools.reduce(jnp.add, w), axis=1, keepdims=True)
        blended = jnp.dot(
            jnp.concatenate([w_e.astype(jnp.bfloat16) for w_e in w], axis=1),
            jnp.concatenate(values, axis=0),
            preferred_element_type=jnp.float32,
        )
        write((blended * (1.0 / total)).astype(jnp.bfloat16))

    for entries in range(MIN_COUNT, LIST_LEN + 1, 2):
        pl.when((used == entries) | (used == entries - 1))(functools.partial(run, entries))


def attend_all_kernel(full, group_blocks, table, in_ref, out_ref, buf, o_buf, in_sem, out_sem):
    devices = in_ref.shape[0]
    copy = pltpu.make_async_copy(in_ref, buf, in_sem)
    copy.start()
    copy.wait()

    def step(block, carry):
        row = table_row(block, group_blocks)
        used = table[row + LIST_LEN]
        for i in range(full):
            own = pl.ds(i * BLOCK_LEN, BLOCK_LEN)

            def pairs(entries):
                named = [table[row + e] for e in range(entries)]
                keys = [buf[b, own] for b in named]
                return keys, [buf[b, pl.ds((full + i) * BLOCK_LEN, BLOCK_LEN)] for b in named]

            def write(result):
                o_buf[block, own] = result

            attend_block(buf[block, pl.ds((2 * full + i) * BLOCK_LEN, BLOCK_LEN)], pairs, used, write)
        pltpu.make_async_copy(o_buf.at[block], out_ref.at[block], out_sem).start()
        return carry

    lax.fori_loop(0, devices, step, 0)
    pltpu.make_async_copy(o_buf, out_ref, out_sem).wait()


def attend_cost(blocks, heads, in_bytes):
    pairs = blocks * heads * LIST_LEN
    return pl.CostEstimate(
        flops=pairs * 4 * BLOCK_LEN * BLOCK_LEN * HEAD_DIM,
        transcendentals=pairs * BLOCK_LEN * BLOCK_LEN,
        bytes_accessed=in_bytes,
    )


def attend_all(table, arrived, full, group_blocks):
    devices = arrived.shape[0]
    shape = (devices, full * BLOCK_LEN, HEAD_DIM)
    return pl.pallas_call(
        functools.partial(attend_all_kernel, full, group_blocks),
        out_shape=jax.ShapeDtypeStruct(shape, jnp.bfloat16),
        in_specs=[SMEM, ANY],
        out_specs=ANY,
        scratch_shapes=[
            pltpu.VMEM(arrived.shape, jnp.bfloat16),
            pltpu.VMEM(shape, jnp.bfloat16),
            pltpu.SemaphoreType.DMA,
            pltpu.SemaphoreType.DMA,
        ],
        compiler_params=pltpu.CompilerParams(vmem_limit_bytes=VMEM_LIMIT),
        cost_estimate=attend_cost(devices, full, arrived.size * 2),
        name="attend_all",
    )(table, arrived)


def attend_rest_kernel(head_axis, gather_axis, count, peers, others, group_blocks, table, *refs):
    pieces, refs = refs[:peers], refs[peers:]
    gathered, refs = refs[:others], refs[others:]
    outs, refs = refs[:peers], refs[peers:]
    q_buf, kv_buf, o_buf, in_sem, out_sem = refs
    part_rows = count * BLOCK_LEN
    copies = [
        pltpu.make_async_copy(pieces[r].at[pl.ds(2 * part_rows, part_rows)], q_buf.at[r], in_sem)
        for r in range(peers)
    ]
    copies += [
        pltpu.make_async_copy(gathered[g], kv_buf.at[pl.ds(g * peers, peers)], in_sem)
        for g in range(others)
    ]
    for copy in copies:
        copy.start()
    for copy in copies:
        copy.wait()
    my_head, my_gather = lax.axis_index(head_axis), lax.axis_index(gather_axis)
    inner = lax.axis_size("uly")
    outer_heads = head_axis == "seq"

    def place(block):
        outer, low = block // inner, block % inner
        h, g = (outer, low) if outer_heads else (low, outer)
        return (g ^ my_gather) * peers + (h ^ my_head)

    def step(r, carry):
        h = my_head ^ r
        block = h * inner + my_gather if outer_heads else my_gather * inner + h
        row = table_row(block, group_blocks)
        used = table[row + LIST_LEN]
        for i in range(count):
            own = pl.ds(i * BLOCK_LEN, BLOCK_LEN)

            def pairs(entries):
                slots = [place(table[row + e]) for e in range(entries)]
                keys = [kv_buf[slot, own] for slot in slots]
                return keys, [kv_buf[slot, pl.ds((count + i) * BLOCK_LEN, BLOCK_LEN)] for slot in slots]

            def write(result):
                o_buf[r, own] = result

            attend_block(q_buf[r, own], pairs, used, write)
        return carry

    lax.fori_loop(0, peers, step, 0)
    copies = [pltpu.make_async_copy(o_buf.at[r], outs[r], out_sem) for r in range(peers)]
    for copy in copies:
        copy.start()
    for copy in copies:
        copy.wait()


def attend_rest(table, pieces, gathered, head_axis, gather_axis, count, group_blocks):
    peers, others = len(pieces), len(gathered)
    part_rows = count * BLOCK_LEN
    return pl.pallas_call(
        functools.partial(
            attend_rest_kernel, head_axis, gather_axis, count, peers, others, group_blocks
        ),
        out_shape=[jax.ShapeDtypeStruct((part_rows, HEAD_DIM), jnp.bfloat16)] * peers,
        in_specs=[SMEM] + [ANY] * (peers + others),
        out_specs=[ANY] * peers,
        scratch_shapes=[
            pltpu.VMEM((peers, part_rows, HEAD_DIM), jnp.bfloat16),
            pltpu.VMEM((others * peers, 2 * part_rows, HEAD_DIM), jnp.bfloat16),
            pltpu.VMEM((peers, part_rows, HEAD_DIM), jnp.bfloat16),
            pltpu.SemaphoreType.DMA,
            pltpu.SemaphoreType.DMA,
        ],
        compiler_params=pltpu.CompilerParams(vmem_limit_bytes=VMEM_LIMIT),
        cost_estimate=attend_cost(peers, count, peers * (others + 1) * 2 * part_rows * HEAD_DIM * 2),
        name="attend_rest",
    )(table, *pieces, *gathered)


def unpack_kernel(head_axis, start, each, full, chunks, peers, devices, *refs):
    has_main = 1 if full else 0
    n = has_main + len(chunks) * peers
    parts, out_ref, buf, in_sem, out_sem = refs[:n], refs[n], refs[n + 1], refs[n + 2], refs[n + 3]
    me = lax.axis_index(head_axis)
    copies = []
    for d in range(devices * has_main):
        for i in range(full):
            copies.append(
                pltpu.make_async_copy(
                    parts[0].at[d, pl.ds(i * BLOCK_LEN, BLOCK_LEN)],
                    buf.at[:, pl.ds((d * full + i) * HEAD_DIM, HEAD_DIM)],
                    in_sem,
                )
            )
    for j, (first, count) in enumerate(chunks):
        for rel in range(peers):
            for i in range(count):
                col = pl.multiple_of((start + (me ^ rel) * each + first + i) * HEAD_DIM, HEAD_DIM)
                copies.append(
                    pltpu.make_async_copy(
                        parts[has_main + j * peers + rel].at[pl.ds(i * BLOCK_LEN, BLOCK_LEN)],
                        buf.at[:, pl.ds(col, HEAD_DIM)],
                        in_sem,
                    )
                )
    for copy in copies:
        copy.start()
    for copy in copies:
        copy.wait()
    copy = pltpu.make_async_copy(buf, out_ref, out_sem)
    copy.start()
    copy.wait()


def unpack(parts, head_axis, start, each, full, chunks, devices, width):
    peers = lax.axis_size(head_axis)
    return pl.pallas_call(
        functools.partial(unpack_kernel, head_axis, start, each, full, chunks, peers, devices),
        out_shape=jax.ShapeDtypeStruct((BLOCK_LEN, width), jnp.bfloat16),
        in_specs=[ANY] * len(parts),
        out_specs=ANY,
        scratch_shapes=[
            pltpu.VMEM((BLOCK_LEN, width), jnp.bfloat16),
            pltpu.SemaphoreType.DMA,
            pltpu.SemaphoreType.DMA,
        ],
        cost_estimate=pl.CostEstimate(
            flops=0, transcendentals=0, bytes_accessed=2 * BLOCK_LEN * width * 2
        ),
        compiler_params=pltpu.CompilerParams(vmem_limit_bytes=VMEM_LIMIT),
        name="unpack",
    )(*parts)


def body(queries, keys, values, block_lists, block_counts):
    width = queries.shape[1]
    heads = width // HEAD_DIM
    devices = lax.axis_size(DEVICES)
    group_blocks = block_lists.shape[0]
    assert queries.shape[0] == BLOCK_LEN
    full = heads // devices
    start = full * devices
    head_axis, gather_axis = "seq", "uly"
    if (heads - start) % lax.axis_size(head_axis):
        head_axis, gather_axis = gather_axis, head_axis
    peers = lax.axis_size(head_axis)
    each = (heads - start) // peers
    chunks = tuple((first, min(CHUNK, each - first)) for first in range(0, each, CHUNK))
    half = peers // 2
    order = [rel for pair in zip(range(half, peers), range(half)) for rel in pair if rel]

    def exchange(parts):
        moved = {rel: swap(parts[rel], head_axis, rel) for rel in order}
        return [parts[0]] + [moved[rel] for rel in range(1, peers)]

    results = []
    if full:
        sent = pack_all(queries, keys, values, full, devices)
        arrived = lax.all_to_all(sent, DEVICES, split_axis=0, concat_axis=0, tiled=True)
    table = gather_tables(block_lists, block_counts)
    inputs = []
    for first, count in chunks:
        inputs.append(exchange(pack_rest(queries, keys, values, head_axis, start, each, first, count)))
    if full:
        blended = attend_all(table, arrived, full, group_blocks)
        results.append(lax.all_to_all(blended, DEVICES, split_axis=0, concat_axis=0, tiled=True))
    for (first, count), pieces in zip(chunks, inputs):
        kv = jnp.stack([piece[: 2 * count * BLOCK_LEN] for piece in pieces])
        gathered = gather_all(kv, gather_axis)
        outs = attend_rest(table, pieces, gathered, head_axis, gather_axis, count, group_blocks)
        results.extend(exchange(outs))
    return unpack(results, head_axis, start, each, full, chunks, devices, width)


def solution(mesh):
    rows = P(DEVICES, None)
    placed = (rows, rows, rows, P("seq", None), P("seq"))
    return jax.shard_map(body, mesh=mesh, in_specs=placed, out_specs=rows, check_vma=False)
```

time: 576 us -> 181 us (0.31)
  waiting for transfers between devices: 261 us -> 79 us
  local copies, waits for them, and re-layouts: 143 us -> 12 us
  other arithmetic: 98.6 us -> 0.88 us
  Pallas kernels: 0 us -> 39.5 us
  matrix products: 25.6 us -> 0 us
  starting transfers between devices: 23.8 us -> 48 us
  blocking collectives: 20.8 us -> 0 us
    all_to_all x5 -> x2, waiting for transfers between devices: 261 us -> 0.01 us  [the longest x1 0.01 us: body(): lax.all_to_all(sent, DEVICES, split_axis=0, concat_axis=0, tiled=True)]
    gather x9 -> x0, local copies, waits for them, and re-layouts: 108 us -> none  [the longest x8 102 us: attend(): jnp.take(pool, slot_list, axis=0)]
    ppermute x0 -> x20, waiting for transfers between devices: none -> 79 us  [swap(): lax.ppermute(x, axis, [(i, i ^ bit) for i in range(lax.axis_size(axis))])]
    select_n x11 -> x0, other arithmetic: 73.9 us -> none  [the longest x8 63.8 us: attend(): jnp.take(pool, slot_list, axis=0)]
    pallas_call x0 -> x5, Pallas kernels: none -> 39.5 us  [the longest x1 22.7 us: attend_all(): pl.pallas_call(functools.partial(attend_all_kernel, full, group_blocks),...]
    ppermute x0 -> x20, starting transfers between devices: none -> 36.8 us  [swap(): lax.ppermute(x, axis, [(i, i ^ bit) for i in range(lax.axis_size(axis))])]
    dot_general x8 -> x0, matrix products: 25.6 us -> none  [the longest x4 15.2 us: attend(): jnp.einsum('qhd,khd->hqk', q_block, gathered[:, 0], preferred_element_typ...]
    all_to_all x1 -> x0, blocking collectives: 20.8 us -> none  [body(): lax.all_to_all(attended.reshape(row_count, feat_width), 'uly', split_axis...]
  transfers between devices with their start and end apart: 5 -> 22, of which waited for: 4 -> 8; matrix products, arithmetic and copies ran while one was open for 6% -> 5% of each run, Pallas kernels for 0% -> 18%
where the time goes in v1:
time: 181 us; the launch traced here: 180 us
  waiting for transfers between devices  79 us (44%)
  starting transfers between devices  48 us (27%)
  Pallas kernels  39.5 us (22%)
  local copies, waits for them, and re-layouts  12 us (7%)
    ppermute x20, waiting for transfers between devices, swap(): lax.ppermute(x, axis, [(i, i ^ bit) for i in range(lax.axis_size(axis))])  79 us
    ppermute x20, starting transfers between devices, swap(): lax.ppermute(x, axis, [(i, i ^ bit) for i in range(lax.axis_size(axis))])  36.8 us
    pallas_call x1, Pallas kernels, attend_all(): pl.pallas_call(functools.partial(attend_all_kernel, full, group_blocks),...  22.7 us
    unnamed x43, local copies, waits for them, and re-layouts  10.4 us
    pallas_call x1, Pallas kernels, attend_rest(): pl.pallas_call(functools.partial(attend_rest_kernel, head_axis, gather_ax...  7.97 us
    all_to_all x1, starting transfers between devices, body(): lax.all_to_all(sent, DEVICES, split_axis=0, concat_axis=0, tiled=True)  7.3 us
    pallas_call x1, Pallas kernels, pack_all(): pl.pallas_call(functools.partial(pack_all_kernel, full, step), grid=(devi...  4.36 us
    all_to_all x1, starting transfers between devices, body(): lax.all_to_all(blended, DEVICES, split_axis=0, concat_axis=0, tiled=True)  3.85 us
  transfers between devices with their start and end apart: 22, of which 8 were waited for; matrix products, arithmetic and copies ran while one was open for 5% of the time, Pallas kernels for 18%

profile of v1, /device:TPU:0, one launch (start us, length us, event | category | flops | bytes accessed | tf_op | source)
XLA Modules:
  0.0 179.6 jit_solution(15870543105934968011)
XLA Ops:
  0.0 4.4 %pack_all.1 = bf16[32,384,128]{2,1,0:T(8,128)(2,1)} custom-call(bf16[128,5120]{1,0:T(8,128)(2,1)} %k_ref.3, bf16[128,5120]{1,0:T(8,128)(2,1)} %v_ref.3, bf16[128,5120]{1,0:T(8,128)(2,1)} %q_ref.3), custom_call_target="tpu_custom_call" | custom-call | bytes 6291456 | tf_op jit(solution)/shard_map/pack_all/pallas_call | solution.py:64
  4.4 7.3 %all-to-all-start = ((bf16[32,384,128]{2,1,0:T(8,128)(2,1)}), bf16[32,384,128]{2,1,0:T(8,128)(2,1)S(1)}, u32[]{:S(2)}, u32[]{:S(2)}) async-start(bf16[32,384,128]{2,1,0:T(8,128)(2,1)} %pack_all.1), calls=%async_computation | async-start | bytes 6291456 | tf_op jit(solution)/shard_map/all_to_all | solution.py:352
  11.9 1.8 collective-permute-start
  13.7 2.2 %pack_rest.1 = (bf16[384,128]{1,0:T(8,128)(2,1)}, bf16[384,128]{1,0:T(8,128)(2,1)}, bf16[384,128]{1,0:T(8,128)(2,1)}, bf16[384,128]{1,0:T(8,128)(2,1)}, bf16[384...) custom-call(bf16[128,5120]{1,0:T(8,128)(2,1)} %k_ref.3, ...), custom_call_target="tpu_custom_call" | custom-call | bytes 1572864 | tf_op jit(solution)/shard_map/pack_rest/pallas_call | solution.py:101
  15.9 9.9 %collective-permute-done = s32[52]{0:T(128)S(1)} collective-permute-done((s32[52]{0:T(128)S(1)}, s32[52]{0:T(128)S(1)}, u32[]{:S(2)}, u32[]{:S(2)}) %collective-permute-start) | collective-permute-done | bytes 240 | tf_op jit(solution)/shard_map/ppermute | solution.py:25
  25.8 2.6 %collective-permute-start.3 = (bf16[384,128]{1,0:T(8,128)(2,1)}, bf16[384,128]{1,0:T(8,128)(2,1)S(1)}, u32[]{:S(2)}, u32[]{:S(2)}) collective-permute-start(bf16[384,128]{1,0:T(8,128)(2,1)} %get-tuple-element.22), channel_id=1, source_target_pairs={{0,4},{4,0},{8,12},{12,8},{16,20},{20,16},{24,28},{28,24},{1,5},{5... | collective-permute-start | bytes 294920 | tf_op jit(solution)/shard_map/ppermute | solution.py:25
  28.4 1.9 %collective-permute-start.4 = (bf16[384,128]{1,0:T(8,128)(2,1)}, bf16[384,128]{1,0:T(8,128)(2,1)S(1)}, u32[]{:S(2)}, u32[]{:S(2)}) collective-permute-start(bf16[384,128]{1,0:T(8,128)(2,1)} %get-tuple-element.23), channel_id=1, source_target_pairs={{0,8},{4,12},{8,0},{12,4},{16,24},{20,28},{24,16},{28,20},{1,9},{5... | collective-permute-start | bytes 294920 | tf_op jit(solution)/shard_map/ppermute | solution.py:25
  30.4 8.9 %collective-permute-start.6 = (bf16[384,128]{1,0:T(8,128)(2,1)}, bf16[384,128]{1,0:T(8,128)(2,1)S(1)}, u32[]{:S(2)}, u32[]{:S(2)}) collective-permute-start(bf16[384,128]{1,0:T(8,128)(2,1)} %get-tuple-element.25), channel_id=1, source_target_pairs={{0,16},{4,20},{8,24},{12,28},{16,0},{20,4},{24,8},{28,12},{1,17},{... | collective-permute-start | bytes 294920 | tf_op jit(solution)/shard_map/ppermute | solution.py:25
  39.3 24.7 %collective-permute-done.1 = s32[104]{0:T(128)S(1)} collective-permute-done((s32[104]{0:T(128)S(1)}, s32[104]{0:T(128)S(1)}, u32[]{:S(2)}, u32[]{:S(2)}) %collective-permute-start.1) | collective-permute-done | bytes 448 | tf_op jit(solution)/shard_map/ppermute | solution.py:25
  64.1 4.3 %collective-permute-start.2 = (s32[208]{0:T(256)S(1)}, s32[208]{0:T(256)S(1)}, u32[]{:S(2)}, u32[]{:S(2)}) collective-permute-start(s32[208]{0:T(256)S(1)} %pad_add_fusion.2), channel_id=1, source_target_pairs={{0,16},{4,20},{8,24},{12,28},{16,0},{20,4},{24,8},{28,12},{1,17},{... | collective-permute-start | bytes 2504 | tf_op jit(solution)/shard_map/ppermute | solution.py:25
  69.8 17.7 %collective-permute-done.2 = s32[208]{0:T(256)S(1)} collective-permute-done((s32[208]{0:T(256)S(1)}, s32[208]{0:T(256)S(1)}, u32[]{:S(2)}, u32[]{:S(2)}) %collective-permute-start.2) | collective-permute-done | bytes 864 | tf_op jit(solution)/shard_map/ppermute | solution.py:25
  88.3 1.8 collective-permute-start.8
  90.7 2.5 %collective-permute-start.9 = (bf16[384,128]{1,0:T(8,128)(2,1)}, bf16[384,128]{1,0:T(8,128)(2,1)}, u32[]{:S(2)}, u32[]{:S(2)}) collective-permute-start(bf16[384,128]{1,0:T(8,128)(2,1)} %get-tuple-element.28), channel_id=1, source_target_pairs={{0,28},{4,24},{8,20},{12,16},{16,12},{20,8},{24,4},{28,0},{1,29},{... | collective-permute-start | bytes 294920 | tf_op jit(solution)/shard_map/ppermute | solution.py:25
  96.1 22.7 %attend_all.1 = bf16[32,128,128]{2,1,0:T(8,128)(2,1)} custom-call(s32[416]{0:T(512)} %pad_add_fusion.1.table, bf16[32,384,128]{2,1,0:T(8,128)(2,1)} %copy-done.1), custom_call_target="tpu_custom_call" | custom-call | flops 3221225472 | bytes 3145728 | tf_op jit(solution)/shard_map/attend_all/pallas_call | solution.py:179
  118.8 3.9 %all-to-all-start.1 = ((bf16[32,128,128]{2,1,0:T(8,128)(2,1)}), bf16[32,128,128]{2,1,0:T(8,128)(2,1)S(1)}, u32[]{:S(2)}, u32[]{:S(2)}) async-start(bf16[32,128,128]{2,1,0:T(8,128)(2,1)} %attend_all.1), calls=%async_computation.1 | async-start | bytes 2097152 | tf_op jit(solution)/shard_map/all_to_all | solution.py:359
  127.8 1.8 collective-permute-start.11
  129.6 18.8 %collective-permute-done.11.refs_10_ = bf16[8,256,128]{2,1,0:T(8,128)(2,1)S(1)} collective-permute-done((bf16[8,256,128]{2,1,0:T(8,128)(2,1)}, bf16[8,256,128]{2,1,0:T(8,128)(2,1)S(1)}, u32[]{:S(2)}, u32[]{:S(2)}) %collective-permute-start.11) | collective-permute-done | bytes 524320 | tf_op jit(solution)/shard_map/ppermute | solution.py:25
  148.4 1.9 %collective-permute-done.12.refs_11_ = bf16[8,256,128]{2,1,0:T(8,128)(2,1)S(1)} collective-permute-done((bf16[8,256,128]{2,1,0:T(8,128)(2,1)S(1)}, bf16[8,256,128]{2,1,0:T(8,128)(2,1)S(1)}, u32[]{:S(2)}, u32[]{:S(2)}) %collective-permute-start.12) | collective-permute-done | bytes 524320 | tf_op jit(solution)/shard_map/ppermute | solution.py:25
  151.1 8.0 %attend_rest.1 = (bf16[128,128]{1,0:T(8,128)(2,1)}, bf16[128,128]{1,0:T(8,128)(2,1)}, bf16[128,128]{1,0:T(8,128)(2,1)}, bf16[128,128]{1,0:T(8,128)(2,1)}, bf16[1...) custom-call(s32[416]{0:T(512)} %pad_add_fusion.1.table, ...), custom_call_target="tpu_custom_call" | custom-call | flops 805306368 | bytes 2621440 | tf_op jit(solution)/shard_map/attend_rest/pallas_call | solution.py:253
  160.3 2.1 %collective-permute-start.14 = (bf16[128,128]{1,0:T(8,128)(2,1)}, bf16[128,128]{1,0:T(8,128)(2,1)S(1)}, u32[]{:S(2)}, u32[]{:S(2)}) collective-permute-start(bf16[128,128]{1,0:T(8,128)(2,1)} %get-tuple-element.31), channel_id=1, source_target_pairs={{0,8},{4,12},{8,0},{12,4},{16,24},{20,28},{24,16},{28,20},{1,9},{5... | collective-permute-start | bytes 98312 | tf_op jit(solution)/shard_map/ppermute | solution.py:25
  162.6 2.4 %collective-permute-start.16 = (bf16[128,128]{1,0:T(8,128)(2,1)}, bf16[128,128]{1,0:T(8,128)(2,1)S(1)}, u32[]{:S(2)}, u32[]{:S(2)}) collective-permute-start(bf16[128,128]{1,0:T(8,128)(2,1)} %get-tuple-element.33), channel_id=1, source_target_pairs={{0,16},{4,20},{8,24},{12,28},{16,0},{20,4},{24,8},{28,12},{1,17},{... | collective-permute-start | bytes 98312 | tf_op jit(solution)/shard_map/ppermute | solution.py:25
  166.2 3.3 %collective-permute-start.18 = (bf16[128,128]{1,0:T(8,128)(2,1)}, bf16[128,128]{1,0:T(8,128)(2,1)S(1)}, u32[]{:S(2)}, u32[]{:S(2)}) collective-permute-start(bf16[128,128]{1,0:T(8,128)(2,1)} %get-tuple-element.35), channel_id=1, source_target_pairs={{0,24},{4,28},{8,16},{12,20},{16,8},{20,12},{24,0},{28,4},{1,25},{... | collective-permute-start | bytes 98312 | tf_op jit(solution)/shard_map/ppermute | solution.py:25
  172.1 4.1 %collective-permute-done.19.refs_8_ = bf16[128,128]{1,0:T(8,128)(2,1)S(1)} collective-permute-done((bf16[128,128]{1,0:T(8,128)(2,1)}, bf16[128,128]{1,0:T(8,128)(2,1)S(1)}, u32[]{:S(2)}, u32[]{:S(2)}) %collective-permute-start.19) | collective-permute-done | bytes 32800 | tf_op jit(solution)/shard_map/ppermute | solution.py:25
  177.3 2.3 %unpack.1 = bf16[128,5120]{1,0:T(8,128)(2,1)} custom-call(bf16[32,128,128]{2,1,0:T(8,128)(2,1)} %copy-done, bf16[128,128]{1,0:T(8,128)(2,1)} %get-tuple-element.29.refs_1_, bf16[128,128]{1,0:T(8,128)(2,1)} %copy-done.6, bf16[128,128]{1,0:T(8,128)(2,1)} %copy-done.7, bf16[128,128]{1,0:T(8,128)(2,1)} %copy-done.8, bf16[128,128]{1,0:T(8,128)(2,1)} %copy-done.9, ...), custom_call_target="tpu_custom_call" | custom-call | bytes 2621440 | tf_op jit(solution)/shard_map/unpack/pallas_call | solution.py:310
  (75 shorter events, 18.3 us)
Async XLA Ops:
  4.4 90.1 %all-to-all-start = ((bf16[32,384,128]{2,1,0:T(8,128)(2,1)}), bf16[32,384,128]{2,1,0:T(8,128)(2,1)S(1)}, u32[]{:S(2)}, u32[]{:S(2)}) async-start(bf16[32,384,128]{2,1,0:T(8,128)(2,1)} %pack_all.1), calls=%async_computation | async-start | bytes 6291456 | tf_op jit(solution)/shard_map/all_to_all | solution.py:352
  11.9 13.8 %collective-permute-start = (s32[52]{0:T(128)S(1)}, s32[52]{0:T(128)S(1)}, u32[]{:S(2)}, u32[]{:S(2)}) collective-permute-start(s32[52]{0:T(128)S(1)} %reshape.3), channel_id=1, source_target_pairs={{0,4},{4,0},{8,12},{12,8},{16,20},{20,16},{24,28},{28,24},{1,5},{5... | collective-permute-start | bytes 632 | tf_op jit(solution)/shard_map/ppermute | solution.py:25
  25.8 38.2 %collective-permute-start.1 = (s32[104]{0:T(128)S(1)}, s32[104]{0:T(128)S(1)}, u32[]{:S(2)}, u32[]{:S(2)}) collective-permute-start(s32[104]{0:T(128)S(1)} %pad_add_fusion.3), channel_id=1, source_target_pairs={{0,8},{4,12},{8,0},{12,4},{16,24},{20,28},{24,16},{28,20},{1,9},{5... | collective-permute-start | bytes 1256 | tf_op jit(solution)/shard_map/ppermute | solution.py:25
  25.8 62.5 %collective-permute-start.3 = (bf16[384,128]{1,0:T(8,128)(2,1)}, bf16[384,128]{1,0:T(8,128)(2,1)S(1)}, u32[]{:S(2)}, u32[]{:S(2)}) collective-permute-start(bf16[384,128]{1,0:T(8,128)(2,1)} %get-tuple-element.22), channel_id=1, source_target_pairs={{0,4},{4,0},{8,12},{12,8},{16,20},{20,16},{24,28},{28,24},{1,5},{5... | collective-permute-start | bytes 294920 | tf_op jit(solution)/shard_map/ppermute | solution.py:25
  28.4 62.3 %collective-permute-start.4 = (bf16[384,128]{1,0:T(8,128)(2,1)}, bf16[384,128]{1,0:T(8,128)(2,1)S(1)}, u32[]{:S(2)}, u32[]{:S(2)}) collective-permute-start(bf16[384,128]{1,0:T(8,128)(2,1)} %get-tuple-element.23), channel_id=1, source_target_pairs={{0,8},{4,12},{8,0},{12,4},{16,24},{20,28},{24,16},{28,20},{1,9},{5... | collective-permute-start | bytes 294920 | tf_op jit(solution)/shard_map/ppermute | solution.py:25
  30.4 63.4 %collective-permute-start.5 = (bf16[384,128]{1,0:T(8,128)(2,1)}, bf16[384,128]{1,0:T(8,128)(2,1)S(1)}, u32[]{:S(2)}, u32[]{:S(2)}) collective-permute-start(bf16[384,128]{1,0:T(8,128)(2,1)} %get-tuple-element.24), channel_id=1, source_target_pairs={{0,12},{4,8},{8,4},{12,0},{16,28},{20,24},{24,20},{28,16},{1,13},{... | collective-permute-start | bytes 294920 | tf_op jit(solution)/shard_map/ppermute | solution.py:25
  30.4 92.3 %collective-permute-start.6 = (bf16[384,128]{1,0:T(8,128)(2,1)}, bf16[384,128]{1,0:T(8,128)(2,1)S(1)}, u32[]{:S(2)}, u32[]{:S(2)}) collective-permute-start(bf16[384,128]{1,0:T(8,128)(2,1)} %get-tuple-element.25), channel_id=1, source_target_pairs={{0,16},{4,20},{8,24},{12,28},{16,0},{20,4},{24,8},{28,12},{1,17},{... | collective-permute-start | bytes 294920 | tf_op jit(solution)/shard_map/ppermute | solution.py:25
  64.1 23.5 %collective-permute-start.2 = (s32[208]{0:T(256)S(1)}, s32[208]{0:T(256)S(1)}, u32[]{:S(2)}, u32[]{:S(2)}) collective-permute-start(s32[208]{0:T(256)S(1)} %pad_add_fusion.2), channel_id=1, source_target_pairs={{0,16},{4,20},{8,24},{12,28},{16,0},{20,4},{24,8},{28,12},{1,17},{... | collective-permute-start | bytes 2504 | tf_op jit(solution)/shard_map/ppermute | solution.py:25
  87.6 35.8 %collective-permute-start.7 = (bf16[384,128]{1,0:T(8,128)(2,1)}, bf16[384,128]{1,0:T(8,128)(2,1)}, u32[]{:S(2)}, u32[]{:S(2)}) collective-permute-start(bf16[384,128]{1,0:T(8,128)(2,1)} %get-tuple-element.26), channel_id=1, source_target_pairs={{0,20},{4,16},{8,28},{12,24},{16,4},{20,0},{24,12},{28,8},{1,21},{... | collective-permute-start | bytes 294920 | tf_op jit(solution)/shard_map/ppermute | solution.py:25
  88.3 30.5 %copy-start.2 = (bf16[384,128]{1,0:T(8,128)(2,1)}, bf16[384,128]{1,0:T(8,128)(2,1)S(1)}, u32[]{:S(2)}) copy-start(bf16[384,128]{1,0:T(8,128)(2,1)S(1)} %collective-permute-done.3.refs_1_) | copy-start | bytes 294916
  88.3 36.6 %collective-permute-start.8 = (bf16[384,128]{1,0:T(8,128)(2,1)}, bf16[384,128]{1,0:T(8,128)(2,1)}, u32[]{:S(2)}, u32[]{:S(2)}) collective-permute-start(bf16[384,128]{1,0:T(8,128)(2,1)} %get-tuple-element.27), channel_id=1, source_target_pairs={{0,24},{4,28},{8,16},{12,20},{16,8},{20,12},{24,0},{28,4},{1,25},{... | collective-permute-start | bytes 294920 | tf_op jit(solution)/shard_map/ppermute | solution.py:25
  90.7 28.1 %copy-start.3 = (bf16[384,128]{1,0:T(8,128)(2,1)}, bf16[384,128]{1,0:T(8,128)(2,1)S(1)}, u32[]{:S(2)}) copy-start(bf16[384,128]{1,0:T(8,128)(2,1)S(1)} %collective-permute-done.4.refs_2_) | copy-start | bytes 294916
  90.7 35.6 %collective-permute-start.9 = (bf16[384,128]{1,0:T(8,128)(2,1)}, bf16[384,128]{1,0:T(8,128)(2,1)}, u32[]{:S(2)}, u32[]{:S(2)}) collective-permute-start(bf16[384,128]{1,0:T(8,128)(2,1)} %get-tuple-element.28), channel_id=1, source_target_pairs={{0,28},{4,24},{8,20},{12,16},{16,12},{20,8},{24,4},{28,0},{1,29},{... | collective-permute-start | bytes 294920 | tf_op jit(solution)/shard_map/ppermute | solution.py:25
  118.8 57.4 %all-to-all-start.1 = ((bf16[32,128,128]{2,1,0:T(8,128)(2,1)}), bf16[32,128,128]{2,1,0:T(8,128)(2,1)S(1)}, u32[]{:S(2)}, u32[]{:S(2)}) async-start(bf16[32,128,128]{2,1,0:T(8,128)(2,1)} %attend_all.1), calls=%async_computation.1 | async-start | bytes 2097152 | tf_op jit(solution)/shard_map/all_to_all | solution.py:359
  127.8 20.6 %collective-permute-start.11 = (bf16[8,256,128]{2,1,0:T(8,128)(2,1)}, bf16[8,256,128]{2,1,0:T(8,128)(2,1)S(1)}, u32[]{:S(2)}, u32[]{:S(2)}) collective-permute-start(bf16[8,256,128]{2,1,0:T(8,128)(2,1)} %fusion.refs_8_), channel_id=1, source_target_pairs={{0,2},{1,3},{2,0},{3,1},{4,6},{5,7},{6,4},{7,5},{8,10},{9,11},{10,... | collective-permute-start | bytes 1572872 | tf_op jit(solution)/shard_map/ppermute | solution.py:25
  129.6 18.8 %collective-permute-start.10 = (bf16[8,256,128]{2,1,0:T(8,128)(2,1)}, bf16[8,256,128]{2,1,0:T(8,128)(2,1)S(1)}, u32[]{:S(2)}, u32[]{:S(2)}) collective-permute-start(bf16[8,256,128]{2,1,0:T(8,128)(2,1)} %fusion.refs_8_), channel_id=1, source_target_pairs={{0,1},{1,0},{2,3},{3,2},{4,5},{5,4},{6,7},{7,6},{8,9},{9,8},{10,11... | collective-permute-start | bytes 1572872 | tf_op jit(solution)/shard_map/ppermute | solution.py:25
  148.4 1.9 %collective-permute-start.12 = (bf16[8,256,128]{2,1,0:T(8,128)(2,1)S(1)}, bf16[8,256,128]{2,1,0:T(8,128)(2,1)S(1)}, u32[]{:S(2)}, u32[]{:S(2)}) collective-permute-start(bf16[8,256,128]{2,1,0:T(8,128)(2,1)S(1)} %collective-permute-done.11.refs_10_), channel_id=1, source_target_pairs={{0,1},{1,0},{2,3},{3,2},{4,5},{5,4},{6,7},{7,6},{8,9},{9,8},{10,11... | collective-permute-start | bytes 1572872 | tf_op jit(solution)/shard_map/ppermute | solution.py:25
  159.1 7.1 %collective-permute-start.13 = (bf16[128,128]{1,0:T(8,128)(2,1)}, bf16[128,128]{1,0:T(8,128)(2,1)S(1)}, u32[]{:S(2)}, u32[]{:S(2)}) collective-permute-start(bf16[128,128]{1,0:T(8,128)(2,1)} %get-tuple-element.30), channel_id=1, source_target_pairs={{0,4},{4,0},{8,12},{12,8},{16,20},{20,16},{24,28},{28,24},{1,5},{5... | collective-permute-start | bytes 98312 | tf_op jit(solution)/shard_map/ppermute | solution.py:25
  160.3 9.2 %collective-permute-start.14 = (bf16[128,128]{1,0:T(8,128)(2,1)}, bf16[128,128]{1,0:T(8,128)(2,1)S(1)}, u32[]{:S(2)}, u32[]{:S(2)}) collective-permute-start(bf16[128,128]{1,0:T(8,128)(2,1)} %get-tuple-element.31), channel_id=1, source_target_pairs={{0,8},{4,12},{8,0},{12,4},{16,24},{20,28},{24,16},{28,20},{1,9},{5... | collective-permute-start | bytes 98312 | tf_op jit(solution)/shard_map/ppermute | solution.py:25
  162.3 7.9 %collective-permute-start.15 = (bf16[128,128]{1,0:T(8,128)(2,1)}, bf16[128,128]{1,0:T(8,128)(2,1)S(1)}, u32[]{:S(2)}, u32[]{:S(2)}) collective-permute-start(bf16[128,128]{1,0:T(8,128)(2,1)} %get-tuple-element.32), channel_id=1, source_target_pairs={{0,12},{4,8},{8,4},{12,0},{16,28},{20,24},{24,20},{28,16},{1,13},{... | collective-permute-start | bytes 98312 | tf_op jit(solution)/shard_map/ppermute | solution.py:25
  162.6 7.7 %collective-permute-start.16 = (bf16[128,128]{1,0:T(8,128)(2,1)}, bf16[128,128]{1,0:T(8,128)(2,1)S(1)}, u32[]{:S(2)}, u32[]{:S(2)}) collective-permute-start(bf16[128,128]{1,0:T(8,128)(2,1)} %get-tuple-element.33), channel_id=1, source_target_pairs={{0,16},{4,20},{8,24},{12,28},{16,0},{20,4},{24,8},{28,12},{1,17},{... | collective-permute-start | bytes 98312 | tf_op jit(solution)/shard_map/ppermute | solution.py:25
  165.0 6.2 %collective-permute-start.17 = (bf16[128,128]{1,0:T(8,128)(2,1)}, bf16[128,128]{1,0:T(8,128)(2,1)S(1)}, u32[]{:S(2)}, u32[]{:S(2)}) collective-permute-start(bf16[128,128]{1,0:T(8,128)(2,1)} %get-tuple-element.34), channel_id=1, source_target_pairs={{0,20},{4,16},{8,28},{12,24},{16,4},{20,0},{24,12},{28,8},{1,21},{... | collective-permute-start | bytes 98312 | tf_op jit(solution)/shard_map/ppermute | solution.py:25
  166.2 6.0 %collective-permute-start.18 = (bf16[128,128]{1,0:T(8,128)(2,1)}, bf16[128,128]{1,0:T(8,128)(2,1)S(1)}, u32[]{:S(2)}, u32[]{:S(2)}) collective-permute-start(bf16[128,128]{1,0:T(8,128)(2,1)} %get-tuple-element.35), channel_id=1, source_target_pairs={{0,24},{4,28},{8,16},{12,20},{16,8},{20,12},{24,0},{28,4},{1,25},{... | collective-permute-start | bytes 98312 | tf_op jit(solution)/shard_map/ppermute | solution.py:25
  169.4 6.8 %collective-permute-start.19 = (bf16[128,128]{1,0:T(8,128)(2,1)}, bf16[128,128]{1,0:T(8,128)(2,1)S(1)}, u32[]{:S(2)}, u32[]{:S(2)}) collective-permute-start(bf16[128,128]{1,0:T(8,128)(2,1)} %get-tuple-element.36), channel_id=1, source_target_pairs={{0,28},{4,24},{8,20},{12,16},{16,12},{20,8},{24,4},{28,0},{1,29},{... | collective-permute-start | bytes 98312 | tf_op jit(solution)/shard_map/ppermute | solution.py:25
  (16 other events, 113.5 us)

commit v2 on v1

v2 whole, which is shorter than its diff:
```python
import functools
import math

import jax
import jax.numpy as jnp
from jax import lax
from jax.experimental import pallas as pl
from jax.experimental.pallas import tpu as pltpu
from jax.sharding import PartitionSpec as P

HEAD_DIM = 128
BLOCK_LEN = 128
LIST_LEN = 12
MIN_COUNT = 4
ROW = LIST_LEN + 1
MIB = 1024 * 1024
CHUNK = 2
TOGETHER = 4
TABLE_ROWS = 16
IN_FLIGHT = 5
TIED = 7
SCORE_FACTOR = HEAD_DIM**-0.5 * math.log2(math.e)
ANY = pl.BlockSpec(memory_space=pl.ANY)
SMEM = pl.BlockSpec(memory_space=pltpu.SMEM)
DEVICES = ("seq", "uly")


def swap(x, axis, bit):
    return lax.ppermute(x, axis, [(i, i ^ bit) for i in range(lax.axis_size(axis))])


def gather_all(x, axis):
    parts = {0: x}
    bit = lax.axis_size(axis) // 2
    while bit:
        parts.update({rel | bit: swap(part, axis, bit) for rel, part in list(parts.items())})
        bit //= 2
    return [parts[rel] for rel in range(lax.axis_size(axis))]


def row_of(block, head_axis, gather_axis):
    inner = lax.axis_size("uly")
    outer, low = block // inner, block % inner
    head, other = (outer, low) if head_axis == "seq" else (low, outer)
    return (other ^ lax.axis_index(gather_axis)) * lax.axis_size(head_axis) + (
        head ^ lax.axis_index(head_axis)
    )


def pack_all_kernel(full, step, k_ref, v_ref, q_ref, out_ref):
    for d in range(step):
        for part, src in enumerate((k_ref, v_ref, q_ref)):
            for i in range(full):
                col = (d * full + i) * HEAD_DIM
                row = (part * full + i) * BLOCK_LEN
                out_ref[d, row : row + BLOCK_LEN] = src[:, col : col + HEAD_DIM]


def pack_all(queries, keys, values, full, devices):
    step = devices // 4
    block = pl.BlockSpec((BLOCK_LEN, step * full * HEAD_DIM), lambda j: (0, j))
    rows = 3 * full * BLOCK_LEN
    return pl.pallas_call(
        functools.partial(pack_all_kernel, full, step),
        grid=(devices // step,),
        out_shape=jax.ShapeDtypeStruct((devices, rows, HEAD_DIM), queries.dtype),
        in_specs=[block] * 3,
        out_specs=pl.BlockSpec((step, rows, HEAD_DIM), lambda j: (j, 0, 0)),
        cost_estimate=pl.CostEstimate(
            flops=0, transcendentals=0, bytes_accessed=devices * rows * HEAD_DIM * 4
        ),
        compiler_params=pltpu.CompilerParams(vmem_limit_bytes=56 * MIB),
        name="pack_all",
    )(keys, values, queries)


def pack_rest_kernel(head_axis, start, each, first, count, peers, lists, counts, k_ref, v_ref, q_ref, *refs):
    outs, bufs, sem = refs[:peers], refs[peers : peers + 3], refs[peers + 3]
    me, mine = lax.axis_index(head_axis), lax.axis_index("uly")
    width = peers * each * HEAD_DIM
    copies = [
        pltpu.make_async_copy(src.at[:, pl.ds(start * HEAD_DIM, width)], buf, sem)
        for src, buf in zip((k_ref, v_ref, q_ref), bufs)
    ]
    for copy in copies:
        copy.start()
    lane = lax.broadcasted_iota(jnp.int32, (TABLE_ROWS, HEAD_DIM), 1)
    table = jnp.where(lane == LIST_LEN, counts[mine], 0)
    for e in range(LIST_LEN):
        table = jnp.where(lane == e, lists[mine, e], table)
    table = table.astype(jnp.float32).astype(jnp.bfloat16)
    for copy in copies:
        copy.wait()
    for rel in range(peers):
        for part, buf in enumerate(bufs):
            for i in range(count):
                col = pl.multiple_of(((me ^ rel) * each + first + i) * HEAD_DIM, HEAD_DIM)
                row = (part * count + i) * BLOCK_LEN + (part == 2) * TABLE_ROWS
                outs[rel][row : row + BLOCK_LEN] = buf[:, pl.ds(col, HEAD_DIM)]
        row = 2 * count * BLOCK_LEN
        outs[rel][row : row + TABLE_ROWS] = table


def pack_rest(queries, keys, values, lists, counts, head_axis, start, each, first, count):
    peers = lax.axis_size(head_axis)
    rows = 3 * count * BLOCK_LEN + TABLE_ROWS
    return pl.pallas_call(
        functools.partial(pack_rest_kernel, head_axis, start, each, first, count, peers),
        out_shape=[jax.ShapeDtypeStruct((rows, HEAD_DIM), queries.dtype)] * peers,
        in_specs=[SMEM] * 2 + [ANY] * 3,
        out_specs=[pl.BlockSpec(memory_space=pltpu.VMEM)] * peers,
        scratch_shapes=[pltpu.VMEM((BLOCK_LEN, peers * each * HEAD_DIM), queries.dtype)] * 3
        + [pltpu.SemaphoreType.DMA],
        cost_estimate=pl.CostEstimate(
            flops=0, transcendentals=0, bytes_accessed=peers * rows * HEAD_DIM * 4
        ),
        compiler_params=pltpu.CompilerParams(vmem_limit_bytes=56 * MIB),
        name="pack_rest",
    )(lists, counts, keys, values, queries)


def attend_blocks(queries, useds, pairs, write):
    most = functools.reduce(jnp.maximum, useds)

    def run(entries):
        scores, values = [], []
        for t, q in enumerate(queries):
            k, v = pairs(t, entries)
            s = []
            for e in range(0, entries, 2):
                both = lax.dot_general(
                    q,
                    jnp.concatenate(k[e : e + 2], axis=0),
                    (((1,), (1,)), ((), ())),
                    preferred_element_type=jnp.float32,
                )
                s += [both[:, :BLOCK_LEN], both[:, BLOCK_LEN:]]
            for e in range(MIN_COUNT, entries):
                s[e] = s[e] + jnp.where(useds[t] > e, 0.0, -jnp.inf).astype(jnp.float32)
            scores.append(s)
            values.append(v)
        for t, (s, v) in enumerate(zip(scores, values)):
            top = jnp.max(functools.reduce(jnp.maximum, s), axis=1, keepdims=True)
            w = [jnp.exp2((s_e - top) * SCORE_FACTOR) for s_e in s]
            total = jnp.sum(functools.reduce(jnp.add, w), axis=1, keepdims=True)
            blended = jnp.dot(
                jnp.concatenate([w_e.astype(jnp.bfloat16) for w_e in w], axis=1),
                jnp.concatenate(v, axis=0),
                preferred_element_type=jnp.float32,
            )
            write(t, (blended * (1.0 / total)).astype(jnp.bfloat16))

    for entries in range(MIN_COUNT, LIST_LEN + 1, 2):
        pl.when((most == entries) | (most == entries - 1))(functools.partial(run, entries))


def attend_all_kernel(full, place, table, in_ref, out_ref, buf, o_buf, in_sem, out_sem):
    devices = in_ref.shape[0]
    copy = pltpu.make_async_copy(in_ref, buf, in_sem)
    copy.start()
    copy.wait()

    def step(j, carry):
        blocks = [j * TOGETHER + t for t in range(TOGETHER)]
        rows = [place(block) * ROW for block in blocks]
        useds = [table[row + LIST_LEN] for row in rows]
        for i in range(full):
            own = pl.ds(i * BLOCK_LEN, BLOCK_LEN)

            def pairs(t, entries):
                named = [table[rows[t] + e] for e in range(entries)]
                keys = [buf[b, own] for b in named]
                return keys, [buf[b, pl.ds((full + i) * BLOCK_LEN, BLOCK_LEN)] for b in named]

            def write(t, result):
                o_buf[blocks[t], own] = result

            queries = [buf[b, pl.ds((2 * full + i) * BLOCK_LEN, BLOCK_LEN)] for b in blocks]
            attend_blocks(queries, useds, pairs, write)
        done = pl.ds(j * TOGETHER, TOGETHER)
        pltpu.make_async_copy(o_buf.at[done], out_ref.at[done], out_sem).start()
        return carry

    lax.fori_loop(0, devices // TOGETHER, step, 0)
    pltpu.make_async_copy(o_buf, out_ref, out_sem).wait()


def attend_cost(blocks, heads, in_bytes):
    pairs = blocks * heads * LIST_LEN
    return pl.CostEstimate(
        flops=pairs * 4 * BLOCK_LEN * BLOCK_LEN * HEAD_DIM,
        transcendentals=pairs * BLOCK_LEN * BLOCK_LEN,
        bytes_accessed=in_bytes,
    )


def attend_all(table, arrived, full, place):
    devices = arrived.shape[0]
    shape = (devices, full * BLOCK_LEN, HEAD_DIM)
    return pl.pallas_call(
        functools.partial(attend_all_kernel, full, place),
        out_shape=jax.ShapeDtypeStruct(shape, jnp.bfloat16),
        in_specs=[SMEM, ANY],
        out_specs=ANY,
        scratch_shapes=[
            pltpu.VMEM(arrived.shape, jnp.bfloat16),
            pltpu.VMEM(shape, jnp.bfloat16),
            pltpu.SemaphoreType.DMA,
            pltpu.SemaphoreType.DMA,
        ],
        compiler_params=pltpu.CompilerParams(vmem_limit_bytes=16 * MIB),
        cost_estimate=attend_cost(devices, full, arrived.size * 2),
        name="attend_all",
    )(table, arrived)


def stack_kernel(peers, rows, *refs):
    pieces, out_ref, sem = refs[:peers], refs[peers], refs[peers + 1]
    copies = [
        pltpu.make_async_copy(piece.at[pl.ds(0, rows)], out_ref.at[rel], sem)
        for rel, piece in enumerate(pieces)
    ]
    for copy in copies:
        copy.start()
    for copy in copies:
        copy.wait()


def stack(pieces, rows):
    shape = (len(pieces), rows, HEAD_DIM)
    return pl.pallas_call(
        functools.partial(stack_kernel, len(pieces), rows),
        out_shape=jax.ShapeDtypeStruct(shape, jnp.bfloat16),
        in_specs=[ANY] * len(pieces),
        out_specs=pl.BlockSpec(memory_space=pltpu.VMEM),
        scratch_shapes=[pltpu.SemaphoreType.DMA],
        cost_estimate=pl.CostEstimate(flops=0, transcendentals=0, bytes_accessed=4 * math.prod(shape)),
        compiler_params=pltpu.CompilerParams(vmem_limit_bytes=12 * MIB),
        name="stack",
    )(*pieces)


def attend_rest_kernel(head_axis, gather_axis, count, peers, others, place, table, *refs):
    pieces, refs = refs[:peers], refs[peers:]
    gathered, refs = refs[:others], refs[others:]
    outs, refs = refs[:peers], refs[peers:]
    q_buf, kv_buf, o_buf, in_sem, out_sem = refs
    part_rows = count * BLOCK_LEN
    copies = [
        pltpu.make_async_copy(piece.at[pl.ds(2 * part_rows + TABLE_ROWS, part_rows)], q_buf.at[rel], in_sem)
        for rel, piece in enumerate(pieces)
    ]
    copies += [
        pltpu.make_async_copy(part.at[:, pl.ds(0, 2 * part_rows)], kv_buf.at[pl.ds(g * peers, peers)], in_sem)
        for g, part in enumerate(gathered)
    ]
    for copy in copies:
        copy.start()
    for copy in copies:
        copy.wait()
    my_head, my_gather = lax.axis_index(head_axis), lax.axis_index(gather_axis)
    inner = lax.axis_size("uly")

    def step(j, carry):
        mine = [j * TOGETHER + t for t in range(TOGETHER)]
        heads = [my_head ^ rel for rel in mine]
        blocks = [h * inner + my_gather if head_axis == "seq" else my_gather * inner + h for h in heads]
        rows = [place(block) * ROW for block in blocks]
        useds = [table[row + LIST_LEN] for row in rows]
        for i in range(count):
            own = pl.ds(i * BLOCK_LEN, BLOCK_LEN)

            def pairs(t, entries):
                slots = [place(table[rows[t] + e]) for e in range(entries)]
                keys = [kv_buf[slot, own] for slot in slots]
                return keys, [kv_buf[slot, pl.ds((count + i) * BLOCK_LEN, BLOCK_LEN)] for slot in slots]

            def write(t, result):
                o_buf[mine[t], own] = result

            attend_blocks([q_buf[r, own] for r in mine], useds, pairs, write)
        return carry

    lax.fori_loop(0, peers // TOGETHER, step, 0)
    copies = [
        pltpu.make_async_copy(o_buf.at[rel], outs[rel], out_sem) for rel in range(peers)
    ]
    for copy in copies:
        copy.start()
    for copy in copies:
        copy.wait()


def attend_rest(table, pieces, gathered, head_axis, gather_axis, count, place):
    peers, others = lax.axis_size(head_axis), lax.axis_size(gather_axis)
    part_rows = count * BLOCK_LEN
    kv_shape = (others * peers, 2 * part_rows, HEAD_DIM)
    return pl.pallas_call(
        functools.partial(attend_rest_kernel, head_axis, gather_axis, count, peers, others, place),
        out_shape=[jax.ShapeDtypeStruct((part_rows, HEAD_DIM), jnp.bfloat16)] * peers,
        in_specs=[SMEM] + [ANY] * (peers + others),
        out_specs=[ANY] * peers,
        scratch_shapes=[
            pltpu.VMEM((peers, part_rows, HEAD_DIM), jnp.bfloat16),
            pltpu.VMEM(kv_shape, jnp.bfloat16),
            pltpu.VMEM((peers, part_rows, HEAD_DIM), jnp.bfloat16),
            pltpu.SemaphoreType.DMA,
            pltpu.SemaphoreType.DMA,
        ],
        compiler_params=pltpu.CompilerParams(vmem_limit_bytes=2 * math.prod(kv_shape) + 12 * MIB),
        cost_estimate=attend_cost(peers, count, 2 * math.prod(kv_shape)),
        name="attend_rest",
    )(table, *pieces, *gathered)


def unpack_kernel(head_axis, start, each, full, chunks, peers, devices, *refs):
    has_main = 1 if full else 0
    n = has_main + len(chunks) * peers
    parts, out_ref, buf, in_sem, out_sem = refs[:n], refs[n], refs[n + 1], refs[n + 2], refs[n + 3]
    me = lax.axis_index(head_axis)
    copies = []
    for d in range(devices * has_main):
        for i in range(full):
            copies.append(
                pltpu.make_async_copy(
                    parts[0].at[d, pl.ds(i * BLOCK_LEN, BLOCK_LEN)],
                    buf.at[:, pl.ds((d * full + i) * HEAD_DIM, HEAD_DIM)],
                    in_sem,
                )
            )
    for j, (first, count) in enumerate(chunks):
        for rel in range(peers):
            for i in range(count):
                col = pl.multiple_of((start + (me ^ rel) * each + first + i) * HEAD_DIM, HEAD_DIM)
                copies.append(
                    pltpu.make_async_copy(
                        parts[has_main + j * peers + rel].at[pl.ds(i * BLOCK_LEN, BLOCK_LEN)],
                        buf.at[:, pl.ds(col, HEAD_DIM)],
                        in_sem,
                    )
                )
    for copy in copies:
        copy.start()
    for copy in copies:
        copy.wait()
    copy = pltpu.make_async_copy(buf, out_ref, out_sem)
    copy.start()
    copy.wait()


def unpack(parts, head_axis, start, each, full, chunks, devices, width):
    peers = lax.axis_size(head_axis)
    return pl.pallas_call(
        functools.partial(unpack_kernel, head_axis, start, each, full, chunks, peers, devices),
        out_shape=jax.ShapeDtypeStruct((BLOCK_LEN, width), jnp.bfloat16),
        in_specs=[ANY] * len(parts),
        out_specs=ANY,
        scratch_shapes=[
            pltpu.VMEM((BLOCK_LEN, width), jnp.bfloat16),
            pltpu.SemaphoreType.DMA,
            pltpu.SemaphoreType.DMA,
        ],
        cost_estimate=pl.CostEstimate(
            flops=0, transcendentals=0, bytes_accessed=2 * BLOCK_LEN * width * 2
        ),
        compiler_params=pltpu.CompilerParams(vmem_limit_bytes=8 * MIB),
        name="unpack",
    )(*parts)


def body(queries, keys, values, block_lists, block_counts):
    width = queries.shape[1]
    heads = width // HEAD_DIM
    devices = lax.axis_size(DEVICES)
    assert queries.shape[0] == BLOCK_LEN
    full = heads // devices
    start = full * devices
    head_axis, gather_axis = "seq", "uly"
    if (heads - start) % lax.axis_size(head_axis):
        head_axis, gather_axis = gather_axis, head_axis
    peers = lax.axis_size(head_axis)
    each = (heads - start) // peers
    chunks = tuple((first, min(CHUNK, each - first)) for first in range(0, each, CHUNK))
    half = peers // 2
    order = [rel for pair in zip(range(half, peers), [1, *range(2, half), 0]) for rel in pair if rel]
    place = functools.partial(row_of, head_axis=head_axis, gather_axis=gather_axis)
    assert devices <= 256

    arrivals, tied = [], []
    for first, count in chunks:
        sends = pack_rest(
            queries, keys, values, block_lists, block_counts, head_axis, start, each, first, count
        )
        queries, keys, values, sends = lax.optimization_barrier((queries, keys, values, sends))
        moved = {rel: swap(sends[rel], head_axis, rel) for rel in order}
        tied.extend(moved[rel] for rel in order[:TIED])
        arrivals.append([sends[0]] + [moved[rel] for rel in range(1, peers)])
    if full:
        sent = pack_all(queries, keys, values, full, devices)
        sent, _ = lax.optimization_barrier((sent, tied))
        arrived = lax.all_to_all(sent, DEVICES, split_axis=0, concat_axis=0, tiled=True)
    outputs, table = [], None
    for (first, count), pieces in zip(chunks, arrivals):
        kv_rows = 2 * count * BLOCK_LEN
        gathered = gather_all(stack(pieces, kv_rows + TABLE_ROWS), gather_axis)
        if table is None:
            table = jnp.concatenate([part[:, kv_rows, :ROW] for part in gathered])
            table = table.astype(jnp.int32).reshape(-1)
        outputs.append(attend_rest(table, pieces, gathered, head_axis, gather_axis, count, place))
    results, backs = [], []
    if full:
        arrived, _ = lax.optimization_barrier((arrived, outputs))
        blended = attend_all(table, arrived, full, place)
    for outs in outputs:
        late = list(range(half, peers)) + list(range(half - 1, 0, -1))
        moved = {rel: swap(outs[rel], head_axis, rel) for rel in late}
        if full:
            early = late[:IN_FLIGHT]
            blended, kept = lax.optimization_barrier((blended, [moved[rel] for rel in early]))
            moved.update(zip(early, kept))
        backs.extend([outs[0]] + [moved[rel] for rel in range(1, peers)])
    if full:
        results.append(lax.all_to_all(blended, DEVICES, split_axis=0, concat_axis=0, tiled=True))
    results.extend(backs)
    return unpack(results, head_axis, start, each, full, chunks, devices, width)


def solution(mesh):
    rows = P(DEVICES, None)
    placed = (rows, rows, rows, P("seq", None), P("seq"))
    return jax.shard_map(body, mesh=mesh, in_specs=placed, out_specs=rows, check_vma=False)
```

time: 181 us -> 153 us (0.85)
  Pallas kernels: 39.5 us -> 25.1 us
  starting transfers between devices: 48 us -> 33.7 us
  local copies, waits for them, and re-layouts: 12 us -> 22.8 us
  waiting for transfers between devices: 79 us -> 69.8 us
    ppermute x20 -> x17, waiting for transfers between devices: 79 us -> 59.3 us  [swap(): lax.ppermute(x, axis, [(i, i ^ bit) for i in range(lax.axis_size(axis))])]
    ppermute x20 -> x17, starting transfers between devices: 36.8 us -> 25.3 us  [swap(): lax.ppermute(x, axis, [(i, i ^ bit) for i in range(lax.axis_size(axis))])]
    unnamed x43 -> x64, local copies, waits for them, and re-layouts: 10.4 us -> 21.3 us
    pallas_call x1 -> x2, Pallas kernels: 22.7 us -> 11.8 us  [the longest x1 11.1 us: attend_all(): pl.pallas_call(functools.partial(attend_all_kernel, full, place), out_sha...]
    all_to_all x1, waiting for transfers between devices: 0.01 us -> 7.89 us  [body(): lax.all_to_all(blended, DEVICES, split_axis=0, concat_axis=0, tiled=True)]
    pallas_call x1, Pallas kernels: 7.97 us -> 4.66 us  [attend_rest(): pl.pallas_call(functools.partial(attend_rest_kernel, head_axis, gather_ax...]
    all_to_all x1, waiting for transfers between devices: 0.01 us -> 2.68 us  [body(): lax.all_to_all(sent, DEVICES, split_axis=0, concat_axis=0, tiled=True)]
    all_to_all x1, starting transfers between devices: 7.3 us -> 5.36 us  [body(): lax.all_to_all(sent, DEVICES, split_axis=0, concat_axis=0, tiled=True)]
  transfers between devices with their start and end apart: 22 -> 19, of which waited for: 8 -> 6; matrix products, arithmetic and copies ran while one was open for 5% -> 1% of each run, Pallas kernels for 18% -> 14%
where the time goes in v2:
time: 153 us; the launch traced here: 152 us
  waiting for transfers between devices  69.8 us (46%)
  starting transfers between devices  33.7 us (22%)
  Pallas kernels  25.1 us (16%)
  local copies, waits for them, and re-layouts  22.8 us (15%)
    ppermute x17, waiting for transfers between devices, swap(): lax.ppermute(x, axis, [(i, i ^ bit) for i in range(lax.axis_size(axis))])  59.3 us
    ppermute x17, starting transfers between devices, swap(): lax.ppermute(x, axis, [(i, i ^ bit) for i in range(lax.axis_size(axis))])  25.3 us
    unnamed x64, local copies, waits for them, and re-layouts  21.3 us
    pallas_call x1, Pallas kernels, attend_all(): pl.pallas_call(functools.partial(attend_all_kernel, full, place), out_sha...  11.1 us
    all_to_all x1, waiting for transfers between devices, body(): lax.all_to_all(blended, DEVICES, split_axis=0, concat_axis=0, tiled=True)  7.89 us
    all_to_all x1, starting transfers between devices, body(): lax.all_to_all(sent, DEVICES, split_axis=0, concat_axis=0, tiled=True)  5.36 us
    pallas_call x1, Pallas kernels, attend_rest(): pl.pallas_call(functools.partial(attend_rest_kernel, head_axis, gather_ax...  4.66 us
    pallas_call x1, Pallas kernels, pack_all(): pl.pallas_call(functools.partial(pack_all_kernel, full, step), grid=(devi...  4.33 us
  transfers between devices with their start and end apart: 19, of which 6 were waited for; matrix products, arithmetic and copies ran while one was open for 1% of the time, Pallas kernels for 14%

profile of v2, /device:TPU:0, one launch (start us, length us, event | category | flops | bytes accessed | tf_op | source)
XLA Modules:
  0.0 152.2 jit_solution(3779032088930165085)
XLA Ops:
  0.0 2.9 %pack_rest.1 = (bf16[400,128]{1,0:T(8,128)(2,1)}, bf16[400,128]{1,0:T(8,128)(2,1)}, bf16[400,128]{1,0:T(8,128)(2,1)}, bf16[400,128]{1,0:T(8,128)(2,1)}, bf16[400...) custom-call(s32[4,12]{1,0:T(4,128)} %lists.1, s32[4]{0:T(128)} %counts.1, ...), custom_call_target="tpu_custom_call" | custom-call | bytes 1638400 | tf_op jit(solution)/shard_map/pack_rest/pallas_call | solution.py:107
  2.9 3.0 %collective-permute-start = (bf16[400,128]{1,0:T(8,128)(2,1)}, bf16[400,128]{1,0:T(8,128)(2,1)S(1)}, u32[]{:S(2)}, u32[]{:S(2)}) collective-permute-start(bf16[400,128]{1,0:T(8,128)(2,1)} %get-tuple-element.49), channel_id=1, source_target_pairs={{0,4},{4,0},{8,12},{12,8},{16,20},{20,16},{24,28},{28,24},{1,5},{5... | collective-permute-start | bytes 307208 | tf_op jit(solution)/shard_map/ppermute | solution.py:29
  6.0 1.6 %collective-permute-start.1 = (bf16[400,128]{1,0:T(8,128)(2,1)}, bf16[400,128]{1,0:T(8,128)(2,1)S(1)}, u32[]{:S(2)}, u32[]{:S(2)}) collective-permute-start(bf16[400,128]{1,0:T(8,128)(2,1)} %get-tuple-element.50), channel_id=1, source_target_pairs={{0,8},{4,12},{8,0},{12,4},{16,24},{20,28},{24,16},{28,20},{1,9},{5... | collective-permute-start | bytes 307208 | tf_op jit(solution)/shard_map/ppermute | solution.py:29
  7.5 3.0 %collective-permute-start.3 = (bf16[400,128]{1,0:T(8,128)(2,1)}, bf16[400,128]{1,0:T(8,128)(2,1)S(1)}, u32[]{:S(2)}, u32[]{:S(2)}) collective-permute-start(bf16[400,128]{1,0:T(8,128)(2,1)} %get-tuple-element.52), channel_id=1, source_target_pairs={{0,16},{4,20},{8,24},{12,28},{16,0},{20,4},{24,8},{28,12},{1,17},{... | collective-permute-start | bytes 307208 | tf_op jit(solution)/shard_map/ppermute | solution.py:29
  11.8 3.6 %collective-permute-start.5 = (bf16[400,128]{1,0:T(8,128)(2,1)}, bf16[400,128]{1,0:T(8,128)(2,1)S(1)}, u32[]{:S(2)}, u32[]{:S(2)}) collective-permute-start(bf16[400,128]{1,0:T(8,128)(2,1)} %get-tuple-element.54), channel_id=1, source_target_pairs={{0,24},{4,28},{8,16},{12,20},{16,8},{20,12},{24,0},{28,4},{1,25},{... | collective-permute-start | bytes 307208 | tf_op jit(solution)/shard_map/ppermute | solution.py:29
  15.4 4.3 %pack_all.1 = bf16[32,384,128]{2,1,0:T(8,128)(2,1)} custom-call(bf16[128,5120]{1,0:T(8,128)(2,1)} %k_ref.2, bf16[128,5120]{1,0:T(8,128)(2,1)} %v_ref.2, bf16[128,5120]{1,0:T(8,128)(2,1)} %q_ref.2), custom_call_target="tpu_custom_call" | custom-call | bytes 6291456 | tf_op jit(solution)/shard_map/pack_all/pallas_call | solution.py:63
  20.4 6.0 %collective-permute-done.4.refs_5_ = bf16[400,128]{1,0:T(8,128)(2,1)S(1)} collective-permute-done((bf16[400,128]{1,0:T(8,128)(2,1)}, bf16[400,128]{1,0:T(8,128)(2,1)S(1)}, u32[]{:S(2)}, u32[]{:S(2)}) %collective-permute-start.4) | collective-permute-done | bytes 102432 | tf_op jit(solution)/shard_map/ppermute | solution.py:29
  28.4 5.4 %all-to-all-start = ((bf16[32,384,128]{2,1,0:T(8,128)(2,1)}), bf16[32,384,128]{2,1,0:T(8,128)(2,1)S(1)}, u32[]{:S(2)}, u32[]{:S(2)}) async-start(bf16[32,384,128]{2,1,0:T(8,128)(2,1)} %pack_all.1), calls=%async_computation | async-start | bytes 6291456 | tf_op jit(solution)/shard_map/all_to_all | solution.py:401
  38.1 1.8 %collective-permute-start.8 = (bf16[8,272,128]{2,1,0:T(8,128)(2,1)S(1)}, bf16[8,272,128]{2,1,0:T(8,128)(2,1)S(1)}, u32[]{:S(2)}, u32[]{:S(2)}) collective-permute-start(bf16[8,272,128]{2,1,0:T(8,128)(2,1)S(1)} %stack.1.refs_8_), channel_id=1, source_target_pairs={{0,2},{1,3},{2,0},{3,1},{4,6},{5,7},{6,4},{7,5},{8,10},{9,11},{10,... | collective-permute-start | bytes 1671176 | tf_op jit(solution)/shard_map/ppermute | solution.py:29
  39.9 38.2 %collective-permute-done.8.refs_10_ = bf16[8,272,128]{2,1,0:T(8,128)(2,1)S(1)} collective-permute-done((bf16[8,272,128]{2,1,0:T(8,128)(2,1)S(1)}, bf16[8,272,128]{2,1,0:T(8,128)(2,1)S(1)}, u32[]{:S(2)}, u32[]{:S(2)}) %collective-permute-start.8) | collective-permute-done | bytes 557088 | tf_op jit(solution)/shard_map/ppermute | solution.py:29
  82.0 1.4 reshape.4.table
  91.9 4.7 %attend_rest.1 = (bf16[128,128]{1,0:T(8,128)(2,1)S(1)}, bf16[128,128]{1,0:T(8,128)(2,1)S(1)}, bf16[128,128]{1,0:T(8,128)(2,1)S(1)}, bf16[128,128]{1,0:T(8,128)(2...) custom-call(s32[416]{0:T(512)S(1)} %copy-done.24, ...), custom_call_target="tpu_custom_call" | custom-call | flops 805306368 | bytes 2097152 | tf_op jit(solution)/shard_map/attend_rest/pallas_call | solution.py:298
  98.4 2.7 %collective-permute-start.11 = (bf16[128,128]{1,0:T(8,128)(2,1)}, bf16[128,128]{1,0:T(8,128)(2,1)S(1)}, u32[]{:S(2)}, u32[]{:S(2)}) collective-permute-start(bf16[128,128]{1,0:T(8,128)(2,1)} %get-tuple-element.65), channel_id=1, source_target_pairs={{0,20},{4,16},{8,28},{12,24},{16,4},{20,0},{24,12},{28,8},{1,21},{... | collective-permute-start | bytes 98312 | tf_op jit(solution)/shard_map/ppermute | solution.py:29
  101.1 1.6 %collective-permute-start.12 = (bf16[128,128]{1,0:T(8,128)(2,1)}, bf16[128,128]{1,0:T(8,128)(2,1)S(1)}, u32[]{:S(2)}, u32[]{:S(2)}) collective-permute-start(bf16[128,128]{1,0:T(8,128)(2,1)} %get-tuple-element.66), channel_id=1, source_target_pairs={{0,24},{4,28},{8,16},{12,20},{16,8},{20,12},{24,0},{28,4},{1,25},{... | collective-permute-start | bytes 98312 | tf_op jit(solution)/shard_map/ppermute | solution.py:29
  102.7 3.3 %collective-permute-start.13 = (bf16[128,128]{1,0:T(8,128)(2,1)}, bf16[128,128]{1,0:T(8,128)(2,1)S(1)}, u32[]{:S(2)}, u32[]{:S(2)}) collective-permute-start(bf16[128,128]{1,0:T(8,128)(2,1)} %get-tuple-element.67), channel_id=1, source_target_pairs={{0,28},{4,24},{8,20},{12,16},{16,12},{20,8},{24,4},{28,0},{1,29},{... | collective-permute-start | bytes 98312 | tf_op jit(solution)/shard_map/ppermute | solution.py:29
  106.0 2.7 %all-to-all-done.in_ref = bf16[32,384,128]{2,1,0:T(8,128)(2,1)S(1)} async-done(((bf16[32,384,128]{2,1,0:T(8,128)(2,1)}), bf16[32,384,128]{2,1,0:T(8,128)(2,1)S(1)}, u32[]{:S(2)}, u32[]{:S(2)}) %all-to-all-start) | async-done | bytes 3145760 | tf_op jit(solution)/shard_map/all_to_all | solution.py:401
  109.4 11.1 %attend_all.1 = bf16[32,128,128]{2,1,0:T(8,128)(2,1)S(1)} custom-call(s32[416]{0:T(512)S(1)} %copy-done.25, bf16[32,384,128]{2,1,0:T(8,128)(2,1)S(1)} %all-to-all-done.in_ref), custom_call_target="tpu_custom_call" | custom-call | flops 3221225472 | bytes 3145728 | tf_op jit(solution)/shard_map/attend_all/pallas_call | solution.py:200
  121.5 3.1 %all-to-all-start.1 = ((bf16[32,128,128]{2,1,0:T(8,128)(2,1)}), bf16[32,128,128]{2,1,0:T(8,128)(2,1)S(1)}, u32[]{:S(2)}, u32[]{:S(2)}) async-start(bf16[32,128,128]{2,1,0:T(8,128)(2,1)} %copy-done.2), calls=%async_computation.1 | async-start | bytes 2097152 | tf_op jit(solution)/shard_map/all_to_all | solution.py:423
  124.6 1.8 %collective-permute-start.15 = (bf16[128,128]{1,0:T(8,128)(2,1)S(1)}, bf16[128,128]{1,0:T(8,128)(2,1)S(1)}, u32[]{:S(2)}, u32[]{:S(2)}) collective-permute-start(bf16[128,128]{1,0:T(8,128)(2,1)S(1)} %copy-done.29), channel_id=1, source_target_pairs={{0,4},{4,0},{8,12},{12,8},{16,20},{20,16},{24,28},{28,24},{1,5},{5... | collective-permute-start | bytes 98312 | tf_op jit(solution)/shard_map/ppermute | solution.py:29
  126.4 1.5 collective-permute-start.16
  127.9 4.4 %collective-permute-done.15.refs_2_ = bf16[128,128]{1,0:T(8,128)(2,1)S(1)} collective-permute-done((bf16[128,128]{1,0:T(8,128)(2,1)S(1)}, bf16[128,128]{1,0:T(8,128)(2,1)S(1)}, u32[]{:S(2)}, u32[]{:S(2)}) %collective-permute-start.15) | collective-permute-done | bytes 32800 | tf_op jit(solution)/shard_map/ppermute | solution.py:29
  132.3 10.6 %collective-permute-done.16.refs_3_ = bf16[128,128]{1,0:T(8,128)(2,1)S(1)} collective-permute-done((bf16[128,128]{1,0:T(8,128)(2,1)S(1)}, bf16[128,128]{1,0:T(8,128)(2,1)S(1)}, u32[]{:S(2)}, u32[]{:S(2)}) %collective-permute-start.16) | collective-permute-done | bytes 32800 | tf_op jit(solution)/shard_map/ppermute | solution.py:29
  142.9 7.9 %all-to-all-done.1.refs_0_ = bf16[32,128,128]{2,1,0:T(8,128)(2,1)S(1)} async-done(((bf16[32,128,128]{2,1,0:T(8,128)(2,1)}), bf16[32,128,128]{2,1,0:T(8,128)(2,1)S(1)}, u32[]{:S(2)}, u32[]{:S(2)}) %all-to-all-start.1) | async-done | bytes 1048608 | tf_op jit(solution)/shard_map/all_to_all | solution.py:423
  150.8 1.4 unpack.1
  (90 shorter events, 24.0 us)
Async XLA Ops:
  2.9 8.9 %collective-permute-start = (bf16[400,128]{1,0:T(8,128)(2,1)}, bf16[400,128]{1,0:T(8,128)(2,1)S(1)}, u32[]{:S(2)}, u32[]{:S(2)}) collective-permute-start(bf16[400,128]{1,0:T(8,128)(2,1)} %get-tuple-element.49), channel_id=1, source_target_pairs={{0,4},{4,0},{8,12},{12,8},{16,20},{20,16},{24,28},{28,24},{1,5},{5... | collective-permute-start | bytes 307208 | tf_op jit(solution)/shard_map/ppermute | solution.py:29
  6.0 9.5 %collective-permute-start.1 = (bf16[400,128]{1,0:T(8,128)(2,1)}, bf16[400,128]{1,0:T(8,128)(2,1)S(1)}, u32[]{:S(2)}, u32[]{:S(2)}) collective-permute-start(bf16[400,128]{1,0:T(8,128)(2,1)} %get-tuple-element.50), channel_id=1, source_target_pairs={{0,8},{4,12},{8,0},{12,4},{16,24},{20,28},{24,16},{28,20},{1,9},{5... | collective-permute-start | bytes 307208 | tf_op jit(solution)/shard_map/ppermute | solution.py:29
  7.5 12.2 %collective-permute-start.2 = (bf16[400,128]{1,0:T(8,128)(2,1)}, bf16[400,128]{1,0:T(8,128)(2,1)S(1)}, u32[]{:S(2)}, u32[]{:S(2)}) collective-permute-start(bf16[400,128]{1,0:T(8,128)(2,1)} %get-tuple-element.51), channel_id=1, source_target_pairs={{0,12},{4,8},{8,4},{12,0},{16,28},{20,24},{24,20},{28,16},{1,13},{... | collective-permute-start | bytes 307208 | tf_op jit(solution)/shard_map/ppermute | solution.py:29
  7.5 12.2 %collective-permute-start.3 = (bf16[400,128]{1,0:T(8,128)(2,1)}, bf16[400,128]{1,0:T(8,128)(2,1)S(1)}, u32[]{:S(2)}, u32[]{:S(2)}) collective-permute-start(bf16[400,128]{1,0:T(8,128)(2,1)} %get-tuple-element.52), channel_id=1, source_target_pairs={{0,16},{4,20},{8,24},{12,28},{16,0},{20,4},{24,8},{28,12},{1,17},{... | collective-permute-start | bytes 307208 | tf_op jit(solution)/shard_map/ppermute | solution.py:29
  10.5 15.9 %collective-permute-start.4 = (bf16[400,128]{1,0:T(8,128)(2,1)}, bf16[400,128]{1,0:T(8,128)(2,1)S(1)}, u32[]{:S(2)}, u32[]{:S(2)}) collective-permute-start(bf16[400,128]{1,0:T(8,128)(2,1)} %get-tuple-element.53), channel_id=1, source_target_pairs={{0,20},{4,16},{8,28},{12,24},{16,4},{20,0},{24,12},{28,8},{1,21},{... | collective-permute-start | bytes 307208 | tf_op jit(solution)/shard_map/ppermute | solution.py:29
  11.8 15.3 %collective-permute-start.5 = (bf16[400,128]{1,0:T(8,128)(2,1)}, bf16[400,128]{1,0:T(8,128)(2,1)S(1)}, u32[]{:S(2)}, u32[]{:S(2)}) collective-permute-start(bf16[400,128]{1,0:T(8,128)(2,1)} %get-tuple-element.54), channel_id=1, source_target_pairs={{0,24},{4,28},{8,16},{12,20},{16,8},{20,12},{24,0},{28,4},{1,25},{... | collective-permute-start | bytes 307208 | tf_op jit(solution)/shard_map/ppermute | solution.py:29
  15.4 12.3 %collective-permute-start.6 = (bf16[400,128]{1,0:T(8,128)(2,1)}, bf16[400,128]{1,0:T(8,128)(2,1)S(1)}, u32[]{:S(2)}, u32[]{:S(2)}) collective-permute-start(bf16[400,128]{1,0:T(8,128)(2,1)} %get-tuple-element.55), channel_id=1, source_target_pairs={{0,28},{4,24},{8,20},{12,16},{16,12},{20,8},{24,4},{28,0},{1,29},{... | collective-permute-start | bytes 307208 | tf_op jit(solution)/shard_map/ppermute | solution.py:29
  19.8 14.0 %copy-start.9 = (bf16[400,128]{1,0:T(8,128)(2,1)S(1)}, bf16[400,128]{1,0:T(8,128)(2,1)}, u32[]{:S(2)}) copy-start(bf16[400,128]{1,0:T(8,128)(2,1)} %get-tuple-element.48.refs_0_) | copy-start | bytes 307204
  28.4 80.3 %all-to-all-start = ((bf16[32,384,128]{2,1,0:T(8,128)(2,1)}), bf16[32,384,128]{2,1,0:T(8,128)(2,1)S(1)}, u32[]{:S(2)}, u32[]{:S(2)}) async-start(bf16[32,384,128]{2,1,0:T(8,128)(2,1)} %pack_all.1), calls=%async_computation | async-start | bytes 6291456 | tf_op jit(solution)/shard_map/all_to_all | solution.py:401
  38.1 40.0 %collective-permute-start.8 = (bf16[8,272,128]{2,1,0:T(8,128)(2,1)S(1)}, bf16[8,272,128]{2,1,0:T(8,128)(2,1)S(1)}, u32[]{:S(2)}, u32[]{:S(2)}) collective-permute-start(bf16[8,272,128]{2,1,0:T(8,128)(2,1)S(1)} %stack.1.refs_8_), channel_id=1, source_target_pairs={{0,2},{1,3},{2,0},{3,1},{4,6},{5,7},{6,4},{7,5},{8,10},{9,11},{10,... | collective-permute-start | bytes 1671176 | tf_op jit(solution)/shard_map/ppermute | solution.py:29
  39.9 39.0 %collective-permute-start.7 = (bf16[8,272,128]{2,1,0:T(8,128)(2,1)S(1)}, bf16[8,272,128]{2,1,0:T(8,128)(2,1)S(1)}, u32[]{:S(2)}, u32[]{:S(2)}) collective-permute-start(bf16[8,272,128]{2,1,0:T(8,128)(2,1)S(1)} %stack.1.refs_8_), channel_id=1, source_target_pairs={{0,1},{1,0},{2,3},{3,2},{4,5},{5,4},{6,7},{7,6},{8,9},{9,8},{10,11... | collective-permute-start | bytes 1671176 | tf_op jit(solution)/shard_map/ppermute | solution.py:29
  78.1 2.5 %collective-permute-start.9 = (bf16[8,272,128]{2,1,0:T(8,128)(2,1)S(1)}, bf16[8,272,128]{2,1,0:T(8,128)(2,1)S(1)}, u32[]{:S(2)}, u32[]{:S(2)}) collective-permute-start(bf16[8,272,128]{2,1,0:T(8,128)(2,1)S(1)} %collective-permute-done.8.refs_10_), channel_id=1, source_target_pairs={{0,1},{1,0},{2,3},{3,2},{4,5},{5,4},{6,7},{7,6},{8,9},{9,8},{10,11... | collective-permute-start | bytes 1671176 | tf_op jit(solution)/shard_map/ppermute | solution.py:29
  83.4 1.1 copy-start.1
  98.4 23.1 %collective-permute-start.10 = (bf16[128,128]{1,0:T(8,128)(2,1)}, bf16[128,128]{1,0:T(8,128)(2,1)S(1)}, u32[]{:S(2)}, u32[]{:S(2)}) collective-permute-start(bf16[128,128]{1,0:T(8,128)(2,1)} %get-tuple-element.64), channel_id=1, source_target_pairs={{0,16},{4,20},{8,24},{12,28},{16,0},{20,4},{24,8},{28,12},{1,17},{... | collective-permute-start | bytes 98312 | tf_op jit(solution)/shard_map/ppermute | solution.py:29
  98.4 23.1 %collective-permute-start.11 = (bf16[128,128]{1,0:T(8,128)(2,1)}, bf16[128,128]{1,0:T(8,128)(2,1)S(1)}, u32[]{:S(2)}, u32[]{:S(2)}) collective-permute-start(bf16[128,128]{1,0:T(8,128)(2,1)} %get-tuple-element.65), channel_id=1, source_target_pairs={{0,20},{4,16},{8,28},{12,24},{16,4},{20,0},{24,12},{28,8},{1,21},{... | collective-permute-start | bytes 98312 | tf_op jit(solution)/shard_map/ppermute | solution.py:29
  101.1 20.4 %collective-permute-start.12 = (bf16[128,128]{1,0:T(8,128)(2,1)}, bf16[128,128]{1,0:T(8,128)(2,1)S(1)}, u32[]{:S(2)}, u32[]{:S(2)}) collective-permute-start(bf16[128,128]{1,0:T(8,128)(2,1)} %get-tuple-element.66), channel_id=1, source_target_pairs={{0,24},{4,28},{8,16},{12,20},{16,8},{20,12},{24,0},{28,4},{1,25},{... | collective-permute-start | bytes 98312 | tf_op jit(solution)/shard_map/ppermute | solution.py:29
  102.7 18.8 %collective-permute-start.13 = (bf16[128,128]{1,0:T(8,128)(2,1)}, bf16[128,128]{1,0:T(8,128)(2,1)S(1)}, u32[]{:S(2)}, u32[]{:S(2)}) collective-permute-start(bf16[128,128]{1,0:T(8,128)(2,1)} %get-tuple-element.67), channel_id=1, source_target_pairs={{0,28},{4,24},{8,20},{12,16},{16,12},{20,8},{24,4},{28,0},{1,29},{... | collective-permute-start | bytes 98312 | tf_op jit(solution)/shard_map/ppermute | solution.py:29
  106.0 15.5 %collective-permute-start.14 = (bf16[128,128]{1,0:T(8,128)(2,1)}, bf16[128,128]{1,0:T(8,128)(2,1)S(1)}, u32[]{:S(2)}, u32[]{:S(2)}) collective-permute-start(bf16[128,128]{1,0:T(8,128)(2,1)} %get-tuple-element.63), channel_id=1, source_target_pairs={{0,12},{4,8},{8,4},{12,0},{16,28},{20,24},{24,20},{28,16},{1,13},{... | collective-permute-start | bytes 98312 | tf_op jit(solution)/shard_map/ppermute | solution.py:29
  121.4 3.1 %copy-start.29 = (bf16[128,128]{1,0:T(8,128)(2,1)S(1)}, bf16[128,128]{1,0:T(8,128)(2,1)}, u32[]{:S(2)}) copy-start(bf16[128,128]{1,0:T(8,128)(2,1)} %copy-done.28) | copy-start | bytes 98308
  121.4 5.0 %copy-start.27 = (bf16[128,128]{1,0:T(8,128)(2,1)S(1)}, bf16[128,128]{1,0:T(8,128)(2,1)}, u32[]{:S(2)}) copy-start(bf16[128,128]{1,0:T(8,128)(2,1)} %copy-done.26) | copy-start | bytes 98308
  121.4 29.3 %copy-start.23 = (bf16[128,128]{1,0:T(8,128)(2,1)S(1)}, bf16[128,128]{1,0:T(8,128)(2,1)}, u32[]{:S(2)}) copy-start(bf16[128,128]{1,0:T(8,128)(2,1)} %copy-done.22) | copy-start | bytes 98308
  121.5 29.3 %all-to-all-start.1 = ((bf16[32,128,128]{2,1,0:T(8,128)(2,1)}), bf16[32,128,128]{2,1,0:T(8,128)(2,1)S(1)}, u32[]{:S(2)}, u32[]{:S(2)}) async-start(bf16[32,128,128]{2,1,0:T(8,128)(2,1)} %copy-done.2), calls=%async_computation.1 | async-start | bytes 2097152 | tf_op jit(solution)/shard_map/all_to_all | solution.py:423
  124.6 7.7 %collective-permute-start.15 = (bf16[128,128]{1,0:T(8,128)(2,1)S(1)}, bf16[128,128]{1,0:T(8,128)(2,1)S(1)}, u32[]{:S(2)}, u32[]{:S(2)}) collective-permute-start(bf16[128,128]{1,0:T(8,128)(2,1)S(1)} %copy-done.29), channel_id=1, source_target_pairs={{0,4},{4,0},{8,12},{12,8},{16,20},{20,16},{24,28},{28,24},{1,5},{5... | collective-permute-start | bytes 98312 | tf_op jit(solution)/shard_map/ppermute | solution.py:29
  126.4 16.5 %collective-permute-start.16 = (bf16[128,128]{1,0:T(8,128)(2,1)S(1)}, bf16[128,128]{1,0:T(8,128)(2,1)S(1)}, u32[]{:S(2)}, u32[]{:S(2)}) collective-permute-start(bf16[128,128]{1,0:T(8,128)(2,1)S(1)} %copy-done.27), channel_id=1, source_target_pairs={{0,8},{4,12},{8,0},{12,4},{16,24},{20,28},{24,16},{28,20},{1,9},{5... | collective-permute-start | bytes 98312 | tf_op jit(solution)/shard_map/ppermute | solution.py:29
  (25 other events, 20.3 us)

commit v3 on v2

--- a/solution.py
+++ b/solution.py
@@ -22,6 +22,7 @@
 SCORE_FACTOR = HEAD_DIM**-0.5 * math.log2(math.e)
 ANY = pl.BlockSpec(memory_space=pl.ANY)
 SMEM = pl.BlockSpec(memory_space=pltpu.SMEM)
+HBM = pl.BlockSpec(memory_space=pltpu.HBM)
 DEVICES = ("seq", "uly")
 
 
@@ -75,13 +76,19 @@
 
 
 def pack_rest_kernel(head_axis, start, each, first, count, peers, lists, counts, k_ref, v_ref, q_ref, *refs):
-    outs, bufs, sem = refs[:peers], refs[peers : peers + 3], refs[peers + 3]
+    outs, sem = refs[:peers], refs[peers]
     me, mine = lax.axis_index(head_axis), lax.axis_index("uly")
-    width = peers * each * HEAD_DIM
-    copies = [
-        pltpu.make_async_copy(src.at[:, pl.ds(start * HEAD_DIM, width)], buf, sem)
-        for src, buf in zip((k_ref, v_ref, q_ref), bufs)
-    ]
+    copies = []
+    for rel in range(peers):
+        for part, src in enumerate((k_ref, v_ref, q_ref)):
+            for i in range(count):
+                col = pl.multiple_of((start + (me ^ rel) * each + first + i) * HEAD_DIM, HEAD_DIM)
+                row = (part * count + i) * BLOCK_LEN + (part == 2) * TABLE_ROWS
+                copies.append(
+                    pltpu.make_async_copy(
+                        src.at[:, pl.ds(col, HEAD_DIM)], outs[rel].at[pl.ds(row, BLOCK_LEN)], sem
+                    )
+                )
     for copy in copies:
         copy.start()
     lane = lax.broadcasted_iota(jnp.int32, (TABLE_ROWS, HEAD_DIM), 1)
@@ -89,16 +96,11 @@
     for e in range(LIST_LEN):
         table = jnp.where(lane == e, lists[mine, e], table)
     table = table.astype(jnp.float32).astype(jnp.bfloat16)
-    for copy in copies:
-        copy.wait()
     for rel in range(peers):
-        for part, buf in enumerate(bufs):
-            for i in range(count):
-                col = pl.multiple_of(((me ^ rel) * each + first + i) * HEAD_DIM, HEAD_DIM)
-                row = (part * count + i) * BLOCK_LEN + (part == 2) * TABLE_ROWS
-                outs[rel][row : row + BLOCK_LEN] = buf[:, pl.ds(col, HEAD_DIM)]
         row = 2 * count * BLOCK_LEN
         outs[rel][row : row + TABLE_ROWS] = table
+    for copy in copies:
+        copy.wait()
 
 
 def pack_rest(queries, keys, values, lists, counts, head_axis, start, each, first, count):
@@ -109,8 +111,7 @@
         out_shape=[jax.ShapeDtypeStruct((rows, HEAD_DIM), queries.dtype)] * peers,
         in_specs=[SMEM] * 2 + [ANY] * 3,
         out_specs=[pl.BlockSpec(memory_space=pltpu.VMEM)] * peers,
-        scratch_shapes=[pltpu.VMEM((BLOCK_LEN, peers * each * HEAD_DIM), queries.dtype)] * 3
-        + [pltpu.SemaphoreType.DMA],
+        scratch_shapes=[pltpu.SemaphoreType.DMA],
         cost_estimate=pl.CostEstimate(
             flops=0, transcendentals=0, bytes_accessed=peers * rows * HEAD_DIM * 4
         ),
@@ -154,14 +155,14 @@
         pl.when((most == entries) | (most == entries - 1))(functools.partial(run, entries))
 
 
-def attend_all_kernel(full, place, table, in_ref, out_ref, buf, o_buf, in_sem, out_sem):
-    devices = in_ref.shape[0]
-    copy = pltpu.make_async_copy(in_ref, buf, in_sem)
+def attend_all_kernel(full, place, table_ref, buf, out_ref, table, o_buf, in_sem, out_sem):
+    devices = buf.shape[0]
+    copy = pltpu.make_async_copy(table_ref, table, in_sem)
     copy.start()
     copy.wait()
 
     def step(j, carry):
-        blocks = [j * TOGETHER + t for t in range(TOGETHER)]
+        blocks = [table[devices * ROW + j * TOGETHER + t] for t in range(TOGETHER)]
         rows = [place(block) * ROW for block in blocks]
         useds = [table[row + LIST_LEN] for row in rows]
         for i in range(full):
@@ -177,8 +178,8 @@
 
             queries = [buf[b, pl.ds((2 * full + i) * BLOCK_LEN, BLOCK_LEN)] for b in blocks]
             attend_blocks(queries, useds, pairs, write)
-        done = pl.ds(j * TOGETHER, TOGETHER)
-        pltpu.make_async_copy(o_buf.at[done], out_ref.at[done], out_sem).start()
+        for block in blocks:
+            pltpu.make_async_copy(o_buf.at[block], out_ref.at[block], out_sem).start()
         return carry
 
     lax.fori_loop(0, devices // TOGETHER, step, 0)
@@ -199,11 +200,11 @@
     shape = (devices, full * BLOCK_LEN, HEAD_DIM)
     return pl.pallas_call(
         functools.partial(attend_all_kernel, full, place),
-        out_shape=jax.ShapeDtypeStruct(shape, jnp.bfloat16),
-        in_specs=[SMEM, ANY],
-        out_specs=ANY,
+        out_shape=pltpu.HBM(shape, jnp.bfloat16),
+        in_specs=[HBM, pl.BlockSpec(memory_space=pltpu.VMEM)],
+        out_specs=HBM,
         scratch_shapes=[
-            pltpu.VMEM(arrived.shape, jnp.bfloat16),
+            pltpu.SMEM(table.shape, jnp.int32),
             pltpu.VMEM(shape, jnp.bfloat16),
             pltpu.SemaphoreType.DMA,
             pltpu.SemaphoreType.DMA,
@@ -214,12 +215,28 @@
     )(table, arrived)
 
 
+def by_count(counts, blocks):
+    index = jnp.arange(counts.size, dtype=jnp.int32)
+    key = counts * counts.size + index
+    rank = jnp.sum((key[None, :] < key[:, None]).astype(jnp.int32), axis=1)
+    return jnp.sum(jnp.where(rank[None, :] == index[:, None], blocks[None, :], 0), axis=1)
+
+
+def block_ids(head_axis, gather_axis):
+    index = jnp.arange(lax.axis_size(DEVICES), dtype=jnp.int32)
+    peers = lax.axis_size(head_axis)
+    head = (index % peers) ^ lax.axis_index(head_axis)
+    other = (index // peers) ^ lax.axis_index(gather_axis)
+    return head * lax.axis_size("uly") + other if head_axis == "seq" else other * lax.axis_size("uly") + head
+
+
 def stack_kernel(peers, rows, *refs):
-    pieces, out_ref, sem = refs[:peers], refs[peers], refs[peers + 1]
-    copies = [
-        pltpu.make_async_copy(piece.at[pl.ds(0, rows)], out_ref.at[rel], sem)
-        for rel, piece in enumerate(pieces)
-    ]
+    pieces, (kv_ref, q_ref, sem) = refs[:peers], refs[peers:]
+    copies = []
+    for rel, piece in enumerate(pieces):
+        copies.append(pltpu.make_async_copy(piece.at[pl.ds(0, rows)], kv_ref.at[rel], sem))
+        rest = pl.ds(rows, piece.shape[0] - rows)
+        copies.append(pltpu.make_async_copy(piece.at[rest], q_ref.at[rel], sem))
     for copy in copies:
         copy.start()
     for copy in copies:
@@ -227,29 +244,28 @@
 
 
 def stack(pieces, rows):
-    shape = (len(pieces), rows, HEAD_DIM)
-    return pl.pallas_call(
-        functools.partial(stack_kernel, len(pieces), rows),
-        out_shape=jax.ShapeDtypeStruct(shape, jnp.bfloat16),
-        in_specs=[ANY] * len(pieces),
-        out_specs=pl.BlockSpec(memory_space=pltpu.VMEM),
+    peers, rest = len(pieces), pieces[0].shape[0] - rows
+    vmem = pl.BlockSpec(memory_space=pltpu.VMEM)
+    return pl.pallas_call(
+        functools.partial(stack_kernel, peers, rows),
+        out_shape=[jax.ShapeDtypeStruct((peers, n, HEAD_DIM), jnp.bfloat16) for n in (rows, rest)],
+        in_specs=[ANY] * peers,
+        out_specs=[vmem] * 2,
         scratch_shapes=[pltpu.SemaphoreType.DMA],
-        cost_estimate=pl.CostEstimate(flops=0, transcendentals=0, bytes_accessed=4 * math.prod(shape)),
+        cost_estimate=pl.CostEstimate(
+            flops=0, transcendentals=0, bytes_accessed=4 * peers * (rows + rest) * HEAD_DIM
+        ),
         compiler_params=pltpu.CompilerParams(vmem_limit_bytes=12 * MIB),
         name="stack",
-    )(*pieces)
+    )(*[pltpu.with_memory_space_constraint(piece, pltpu.HBM) for piece in pieces])
 
 
 def attend_rest_kernel(head_axis, gather_axis, count, peers, others, place, table, *refs):
-    pieces, refs = refs[:peers], refs[peers:]
-    gathered, refs = refs[:others], refs[others:]
+    q_ref, gathered, refs = refs[0], refs[1 : others + 1], refs[others + 1 :]
     outs, refs = refs[:peers], refs[peers:]
     q_buf, kv_buf, o_buf, in_sem, out_sem = refs
     part_rows = count * BLOCK_LEN
-    copies = [
-        pltpu.make_async_copy(piece.at[pl.ds(2 * part_rows + TABLE_ROWS, part_rows)], q_buf.at[rel], in_sem)
-        for rel, piece in enumerate(pieces)
-    ]
+    copies = [pltpu.make_async_copy(q_ref, q_buf, in_sem)]
     copies += [
         pltpu.make_async_copy(part.at[:, pl.ds(0, 2 * part_rows)], kv_buf.at[pl.ds(g * peers, peers)], in_sem)
         for g, part in enumerate(gathered)
@@ -291,14 +307,14 @@
         copy.wait()
 
 
-def attend_rest(table, pieces, gathered, head_axis, gather_axis, count, place):
+def attend_rest(table, queries, gathered, head_axis, gather_axis, count, place):
     peers, others = lax.axis_size(head_axis), lax.axis_size(gather_axis)
     part_rows = count * BLOCK_LEN
     kv_shape = (others * peers, 2 * part_rows, HEAD_DIM)
     return pl.pallas_call(
         functools.partial(attend_rest_kernel, head_axis, gather_axis, count, peers, others, place),
         out_shape=[jax.ShapeDtypeStruct((part_rows, HEAD_DIM), jnp.bfloat16)] * peers,
-        in_specs=[SMEM] + [ANY] * (peers + others),
+        in_specs=[SMEM] + [ANY] * (1 + others),
         out_specs=[ANY] * peers,
         scratch_shapes=[
             pltpu.VMEM((peers, part_rows, HEAD_DIM), jnp.bfloat16),
@@ -307,10 +323,10 @@
             pltpu.SemaphoreType.DMA,
             pltpu.SemaphoreType.DMA,
         ],
-        compiler_params=pltpu.CompilerParams(vmem_limit_bytes=2 * math.prod(kv_shape) + 12 * MIB),
+        compiler_params=pltpu.CompilerParams(vmem_limit_bytes=2 * math.prod(kv_shape) + 8 * MIB),
         cost_estimate=attend_cost(peers, count, 2 * math.prod(kv_shape)),
         name="attend_rest",
-    )(table, *pieces, *gathered)
+    )(table, queries, *gathered)
 
 
 def unpack_kernel(head_axis, start, each, full, chunks, peers, devices, *refs):
@@ -402,15 +418,18 @@
     outputs, table = [], None
     for (first, count), pieces in zip(chunks, arrivals):
         kv_rows = 2 * count * BLOCK_LEN
-        gathered = gather_all(stack(pieces, kv_rows + TABLE_ROWS), gather_axis)
+        kv, q = stack(pieces, kv_rows + TABLE_ROWS)
+        gathered = gather_all(kv, gather_axis)
         if table is None:
             table = jnp.concatenate([part[:, kv_rows, :ROW] for part in gathered])
-            table = table.astype(jnp.int32).reshape(-1)
-        outputs.append(attend_rest(table, pieces, gathered, head_axis, gather_axis, count, place))
+            table = table.astype(jnp.int32)
+            counts, table = table[:, LIST_LEN], table.reshape(-1)
+        outputs.append(attend_rest(table, q, gathered, head_axis, gather_axis, count, place))
     results, backs = [], []
     if full:
-        arrived, _ = lax.optimization_barrier((arrived, outputs))
-        blended = attend_all(table, arrived, full, place)
+        ordered = jnp.concatenate([table, by_count(counts, block_ids(head_axis, gather_axis))])
+        arrived, ordered, _ = lax.optimization_barrier((arrived, ordered, outputs))
+        blended = attend_all(ordered, arrived, full, place)
     for outs in outputs:
         late = list(range(half, peers)) + list(range(half - 1, 0, -1))
         moved = {rel: swap(outs[rel], head_axis, rel) for rel in late}

time: 153 us -> 147 us (0.961)
  local copies, waits for them, and re-layouts: 22.8 us -> 5.41 us
  waiting for transfers between devices: 69.8 us -> 77.1 us
  starting transfers between devices: 33.7 us -> 37.7 us
    unnamed x64 -> x22, local copies, waits for them, and re-layouts: 21.3 us -> 2.41 us
    all_to_all x1, waiting for transfers between devices: 2.68 us -> 12.7 us  [body(): lax.all_to_all(sent, DEVICES, split_axis=0, concat_axis=0, tiled=True)]
    ppermute x17, starting transfers between devices: 25.3 us -> 29.8 us  [swap(): lax.ppermute(x, axis, [(i, i ^ bit) for i in range(lax.axis_size(axis))])]
    slice x4, local copies, waits for them, and re-layouts: 0.02 us -> 2.89 us  [body(): table = jnp.concatenate([part[:, kv_rows, :ROW] for part in gathered])]
    ppermute x17, waiting for transfers between devices: 59.3 us -> 56.6 us  [swap(): lax.ppermute(x, axis, [(i, i ^ bit) for i in range(lax.axis_size(axis))])]
    pallas_call x1, Pallas kernels: 11.1 us -> 9.17 us  [attend_all(): pl.pallas_call(functools.partial(attend_all_kernel, full, place), out_sha...]
  transfers between devices with their start and end apart: 19 -> 19, of which waited for: 6 -> 7; matrix products, arithmetic and copies ran while one was open for 1% -> 2% of each run, Pallas kernels for 14% -> 14%
where the time goes in v3:
time: 147 us; the launch traced here: 146 us
  waiting for transfers between devices  77.1 us (52%)
  starting transfers between devices  37.7 us (26%)
  Pallas kernels  25 us (17%)
  local copies, waits for them, and re-layouts  5.41 us (4%)
    ppermute x17, waiting for transfers between devices, swap(): lax.ppermute(x, axis, [(i, i ^ bit) for i in range(lax.axis_size(axis))])  56.6 us
    ppermute x17, starting transfers between devices, swap(): lax.ppermute(x, axis, [(i, i ^ bit) for i in range(lax.axis_size(axis))])  29.8 us
    all_to_all x1, waiting for transfers between devices, body(): lax.all_to_all(sent, DEVICES, split_axis=0, concat_axis=0, tiled=True)  12.7 us
    pallas_call x1, Pallas kernels, attend_all(): pl.pallas_call(functools.partial(attend_all_kernel, full, place), out_sha...  9.17 us
    all_to_all x1, waiting for transfers between devices, body(): lax.all_to_all(blended, DEVICES, split_axis=0, concat_axis=0, tiled=True)  7.89 us
    pallas_call x1, Pallas kernels, attend_rest(): pl.pallas_call(functools.partial(attend_rest_kernel, head_axis, gather_ax...  5.37 us
    all_to_all x1, starting transfers between devices, body(): lax.all_to_all(sent, DEVICES, split_axis=0, concat_axis=0, tiled=True)  4.44 us
    pallas_call x1, Pallas kernels, pack_all(): pl.pallas_call(functools.partial(pack_all_kernel, full, step), grid=(devi...  4.33 us
  transfers between devices with their start and end apart: 19, of which 7 were waited for; matrix products, arithmetic and copies ran while one was open for 2% of the time, Pallas kernels for 14%

profile of v3, /device:TPU:0, one launch (start us, length us, event | category | flops | bytes accessed | tf_op | source)
XLA Modules:
  0.0 146.0 jit_solution(9149669553590222024)
XLA Ops:
  0.0 2.7 %pack_rest.1 = (bf16[400,128]{1,0:T(8,128)(2,1)}, bf16[400,128]{1,0:T(8,128)(2,1)}, bf16[400,128]{1,0:T(8,128)(2,1)}, bf16[400,128]{1,0:T(8,128)(2,1)}, bf16[400...) custom-call(s32[4,12]{1,0:T(4,128)} %lists.1, s32[4]{0:T(128)} %counts.1, ...), custom_call_target="tpu_custom_call" | custom-call | bytes 1638400 | tf_op jit(solution)/shard_map/pack_rest/pallas_call | solution.py:109
  2.7 4.1 %collective-permute-start = (bf16[400,128]{1,0:T(8,128)(2,1)}, bf16[400,128]{1,0:T(8,128)(2,1)S(1)}, u32[]{:S(2)}, u32[]{:S(2)}) collective-permute-start(bf16[400,128]{1,0:T(8,128)(2,1)} %get-tuple-element.54), channel_id=1, source_target_pairs={{0,16},{4,20},{8,24},{12,28},{16,0},{20,4},{24,8},{28,12},{1,17},{... | collective-permute-start | bytes 307208 | tf_op jit(solution)/shard_map/ppermute | solution.py:30
  6.8 1.5 %collective-permute-start.1 = (bf16[400,128]{1,0:T(8,128)(2,1)}, bf16[400,128]{1,0:T(8,128)(2,1)S(1)}, u32[]{:S(2)}, u32[]{:S(2)}) collective-permute-start(bf16[400,128]{1,0:T(8,128)(2,1)} %get-tuple-element.55), channel_id=1, source_target_pairs={{0,4},{4,0},{8,12},{12,8},{16,20},{20,16},{24,28},{28,24},{1,5},{5... | collective-permute-start | bytes 307208 | tf_op jit(solution)/shard_map/ppermute | solution.py:30
  8.3 1.8 %collective-permute-start.3 = (bf16[400,128]{1,0:T(8,128)(2,1)}, bf16[400,128]{1,0:T(8,128)(2,1)S(1)}, u32[]{:S(2)}, u32[]{:S(2)}) collective-permute-start(bf16[400,128]{1,0:T(8,128)(2,1)} %get-tuple-element.57), channel_id=1, source_target_pairs={{0,8},{4,12},{8,0},{12,4},{16,24},{20,28},{24,16},{28,20},{1,9},{5... | collective-permute-start | bytes 307208 | tf_op jit(solution)/shard_map/ppermute | solution.py:30
  10.2 2.5 %collective-permute-start.4 = (bf16[400,128]{1,0:T(8,128)(2,1)}, bf16[400,128]{1,0:T(8,128)(2,1)S(1)}, u32[]{:S(2)}, u32[]{:S(2)}) collective-permute-start(bf16[400,128]{1,0:T(8,128)(2,1)} %get-tuple-element.58), channel_id=1, source_target_pairs={{0,24},{4,28},{8,16},{12,20},{16,8},{20,12},{24,0},{28,4},{1,25},{... | collective-permute-start | bytes 307208 | tf_op jit(solution)/shard_map/ppermute | solution.py:30
  12.7 1.5 %collective-permute-done.refs_4_ = bf16[400,128]{1,0:T(8,128)(2,1)S(1)} collective-permute-done((bf16[400,128]{1,0:T(8,128)(2,1)}, bf16[400,128]{1,0:T(8,128)(2,1)S(1)}, u32[]{:S(2)}, u32[]{:S(2)}) %collective-permute-start) | collective-permute-done | bytes 102432 | tf_op jit(solution)/shard_map/ppermute | solution.py:30
  14.2 2.8 %collective-permute-start.5 = (bf16[400,128]{1,0:T(8,128)(2,1)}, bf16[400,128]{1,0:T(8,128)(2,1)S(1)}, u32[]{:S(2)}, u32[]{:S(2)}) collective-permute-start(bf16[400,128]{1,0:T(8,128)(2,1)} %get-tuple-element.59), channel_id=1, source_target_pairs={{0,12},{4,8},{8,4},{12,0},{16,28},{20,24},{24,20},{28,16},{1,13},{... | collective-permute-start | bytes 307208 | tf_op jit(solution)/shard_map/ppermute | solution.py:30
  16.9 4.3 %collective-permute-start.6 = (bf16[400,128]{1,0:T(8,128)(2,1)}, bf16[400,128]{1,0:T(8,128)(2,1)S(1)}, u32[]{:S(2)}, u32[]{:S(2)}) collective-permute-start(bf16[400,128]{1,0:T(8,128)(2,1)} %get-tuple-element.60), channel_id=1, source_target_pairs={{0,28},{4,24},{8,20},{12,16},{16,12},{20,8},{24,4},{28,0},{1,29},{... | collective-permute-start | bytes 307208 | tf_op jit(solution)/shard_map/ppermute | solution.py:30
  21.3 4.3 %pack_all.1 = bf16[32,384,128]{2,1,0:T(8,128)(2,1)} custom-call(bf16[128,5120]{1,0:T(8,128)(2,1)} %k_ref.2, bf16[128,5120]{1,0:T(8,128)(2,1)} %v_ref.2, bf16[128,5120]{1,0:T(8,128)(2,1)} %q_ref.2), custom_call_target="tpu_custom_call" | custom-call | bytes 6291456 | tf_op jit(solution)/shard_map/pack_all/pallas_call | solution.py:64
  26.4 4.4 %all-to-all-start = ((bf16[32,384,128]{2,1,0:T(8,128)(2,1)}), bf16[32,384,128]{2,1,0:T(8,128)(2,1)S(1)}, u32[]{:S(2)}, u32[]{:S(2)}) async-start(bf16[32,384,128]{2,1,0:T(8,128)(2,1)} %pack_all.1), calls=%async_computation | async-start | bytes 6291456 | tf_op jit(solution)/shard_map/all_to_all | solution.py:417
  30.9 2.0 %stack.1 = (bf16[8,272,128]{2,1,0:T(8,128)(2,1)}, bf16[8,128,128]{2,1,0:T(8,128)(2,1)S(1)}) custom-call(bf16[400,128]{1,0:T(8,128)(2,1)} %get-tuple-element.62.refs_0_, bf16[400,128]{1,0:T(8,128)(2,1)} %copy-done.3, bf16[400,128]{1,0:T(8,128)(2,1)} %copy-done.5, bf16[400,128]{1,0:T(8,128)(2,1)} %copy-done.7, bf16[400,128]{1,0:T(8,128)(2,1)} %copy-done.2, ...), custom_call_target="tpu_custom_call" | custom-call | bytes 1638400 | tf_op jit(solution)/shard_map/stack/pallas_call | solution.py:249
  33.6 1.8 %collective-permute-start.8 = (bf16[8,272,128]{2,1,0:T(8,128)(2,1)}, bf16[8,272,128]{2,1,0:T(8,128)(2,1)}, u32[]{:S(2)}, u32[]{:S(2)}) collective-permute-start(bf16[8,272,128]{2,1,0:T(8,128)(2,1)} %get-tuple-element.63.refs_1_), channel_id=1, source_target_pairs={{0,2},{1,3},{2,0},{3,1},{4,6},{5,7},{6,4},{7,5},{8,10},{9,11},{10,... | collective-permute-start | bytes 1671176 | tf_op jit(solution)/shard_map/ppermute | solution.py:30
  35.4 39.9 %collective-permute-done.8.refs_3_ = bf16[8,272,128]{2,1,0:T(8,128)(2,1)} collective-permute-done((bf16[8,272,128]{2,1,0:T(8,128)(2,1)}, bf16[8,272,128]{2,1,0:T(8,128)(2,1)}, u32[]{:S(2)}, u32[]{:S(2)}) %collective-permute-start.8) | collective-permute-done | bytes 557088 | tf_op jit(solution)/shard_map/ppermute | solution.py:30
  79.4 5.4 %attend_rest.1 = (bf16[128,128]{1,0:T(8,128)(2,1)S(1)}, bf16[128,128]{1,0:T(8,128)(2,1)S(1)}, bf16[128,128]{1,0:T(8,128)(2,1)S(1)}, bf16[128,128]{1,0:T(8,128)(2...) custom-call(s32[416]{0:T(512)S(1)} %reshape.41.table, ...), custom_call_target="tpu_custom_call" | custom-call | flops 805306368 | bytes 2097152 | tf_op jit(solution)/shard_map/attend_rest/pallas_call | solution.py:314
  84.8 2.7 %collective-permute-start.11 = (bf16[128,128]{1,0:T(8,128)(2,1)S(1)}, bf16[128,128]{1,0:T(8,128)(2,1)S(1)}, u32[]{:S(2)}, u32[]{:S(2)}) collective-permute-start(bf16[128,128]{1,0:T(8,128)(2,1)S(1)} %get-tuple-element.70), channel_id=1, source_target_pairs={{0,20},{4,16},{8,28},{12,24},{16,4},{20,0},{24,12},{28,8},{1,21},{... | collective-permute-start | bytes 98312 | tf_op jit(solution)/shard_map/ppermute | solution.py:30
  87.5 1.6 %collective-permute-start.12 = (bf16[128,128]{1,0:T(8,128)(2,1)S(1)}, bf16[128,128]{1,0:T(8,128)(2,1)S(1)}, u32[]{:S(2)}, u32[]{:S(2)}) collective-permute-start(bf16[128,128]{1,0:T(8,128)(2,1)S(1)} %get-tuple-element.71), channel_id=1, source_target_pairs={{0,24},{4,28},{8,16},{12,20},{16,8},{20,12},{24,0},{28,4},{1,25},{... | collective-permute-start | bytes 98312 | tf_op jit(solution)/shard_map/ppermute | solution.py:30
  89.1 3.3 %collective-permute-start.13 = (bf16[128,128]{1,0:T(8,128)(2,1)S(1)}, bf16[128,128]{1,0:T(8,128)(2,1)S(1)}, u32[]{:S(2)}, u32[]{:S(2)}) collective-permute-start(bf16[128,128]{1,0:T(8,128)(2,1)S(1)} %get-tuple-element.72), channel_id=1, source_target_pairs={{0,28},{4,24},{8,20},{12,16},{16,12},{20,8},{24,4},{28,0},{1,29},{... | collective-permute-start | bytes 98312 | tf_op jit(solution)/shard_map/ppermute | solution.py:30
  93.0 12.7 %all-to-all-done.buf = bf16[32,384,128]{2,1,0:T(8,128)(2,1)S(1)} async-done(((bf16[32,384,128]{2,1,0:T(8,128)(2,1)}), bf16[32,384,128]{2,1,0:T(8,128)(2,1)S(1)}, u32[]{:S(2)}, u32[]{:S(2)}) %all-to-all-start) | async-done | bytes 3145760 | tf_op jit(solution)/shard_map/all_to_all | solution.py:417
  105.7 9.2 %attend_all.1 = bf16[32,128,128]{2,1,0:T(8,128)(2,1)} custom-call(s32[448]{0:T(512)S(1)} %pad_add_fusion.table_ref, bf16[32,384,128]{2,1,0:T(8,128)(2,1)S(1)} %all-to-all-done.buf), custom_call_target="tpu_custom_call" | custom-call | flops 3221225472 | bytes 3145728 | tf_op jit(solution)/shard_map/attend_all/pallas_call | solution.py:201
  114.9 3.4 %all-to-all-start.1 = ((bf16[32,128,128]{2,1,0:T(8,128)(2,1)}), bf16[32,128,128]{2,1,0:T(8,128)(2,1)S(1)}, u32[]{:S(2)}, u32[]{:S(2)}) async-start(bf16[32,128,128]{2,1,0:T(8,128)(2,1)} %attend_all.1), calls=%async_computation.1 | async-start | bytes 2097152 | tf_op jit(solution)/shard_map/all_to_all | solution.py:442
  118.4 1.8 %collective-permute-start.15 = (bf16[128,128]{1,0:T(8,128)(2,1)S(1)}, bf16[128,128]{1,0:T(8,128)(2,1)S(1)}, u32[]{:S(2)}, u32[]{:S(2)}) collective-permute-start(bf16[128,128]{1,0:T(8,128)(2,1)S(1)} %get-tuple-element.66), channel_id=1, source_target_pairs={{0,4},{4,0},{8,12},{12,8},{16,20},{20,16},{24,28},{28,24},{1,5},{5... | collective-permute-start | bytes 98312 | tf_op jit(solution)/shard_map/ppermute | solution.py:30
  121.7 4.4 %collective-permute-done.15.refs_2_ = bf16[128,128]{1,0:T(8,128)(2,1)S(1)} collective-permute-done((bf16[128,128]{1,0:T(8,128)(2,1)S(1)}, bf16[128,128]{1,0:T(8,128)(2,1)S(1)}, u32[]{:S(2)}, u32[]{:S(2)}) %collective-permute-start.15) | collective-permute-done | bytes 32800 | tf_op jit(solution)/shard_map/ppermute | solution.py:30
  126.1 10.6 %collective-permute-done.16.refs_3_ = bf16[128,128]{1,0:T(8,128)(2,1)S(1)} collective-permute-done((bf16[128,128]{1,0:T(8,128)(2,1)S(1)}, bf16[128,128]{1,0:T(8,128)(2,1)S(1)}, u32[]{:S(2)}, u32[]{:S(2)}) %collective-permute-start.16) | collective-permute-done | bytes 32800 | tf_op jit(solution)/shard_map/ppermute | solution.py:30
  136.7 7.9 %all-to-all-done.1.refs_0_ = bf16[32,128,128]{2,1,0:T(8,128)(2,1)S(1)} async-done(((bf16[32,128,128]{2,1,0:T(8,128)(2,1)}), bf16[32,128,128]{2,1,0:T(8,128)(2,1)S(1)}, u32[]{:S(2)}, u32[]{:S(2)}) %all-to-all-start.1) | async-done | bytes 1048608 | tf_op jit(solution)/shard_map/all_to_all | solution.py:442
  (54 shorter events, 9.1 us)
Async XLA Ops:
  2.7 11.5 %collective-permute-start = (bf16[400,128]{1,0:T(8,128)(2,1)}, bf16[400,128]{1,0:T(8,128)(2,1)S(1)}, u32[]{:S(2)}, u32[]{:S(2)}) collective-permute-start(bf16[400,128]{1,0:T(8,128)(2,1)} %get-tuple-element.54), channel_id=1, source_target_pairs={{0,16},{4,20},{8,24},{12,28},{16,0},{20,4},{24,8},{28,12},{1,17},{... | collective-permute-start | bytes 307208 | tf_op jit(solution)/shard_map/ppermute | solution.py:30
  6.8 10.1 %collective-permute-start.1 = (bf16[400,128]{1,0:T(8,128)(2,1)}, bf16[400,128]{1,0:T(8,128)(2,1)S(1)}, u32[]{:S(2)}, u32[]{:S(2)}) collective-permute-start(bf16[400,128]{1,0:T(8,128)(2,1)} %get-tuple-element.55), channel_id=1, source_target_pairs={{0,4},{4,0},{8,12},{12,8},{16,20},{20,16},{24,28},{28,24},{1,5},{5... | collective-permute-start | bytes 307208 | tf_op jit(solution)/shard_map/ppermute | solution.py:30
  8.3 17.3 %collective-permute-start.2 = (bf16[400,128]{1,0:T(8,128)(2,1)}, bf16[400,128]{1,0:T(8,128)(2,1)S(1)}, u32[]{:S(2)}, u32[]{:S(2)}) collective-permute-start(bf16[400,128]{1,0:T(8,128)(2,1)} %get-tuple-element.56), channel_id=1, source_target_pairs={{0,20},{4,16},{8,28},{12,24},{16,4},{20,0},{24,12},{28,8},{1,21},{... | collective-permute-start | bytes 307208 | tf_op jit(solution)/shard_map/ppermute | solution.py:30
  8.3 17.3 %collective-permute-start.3 = (bf16[400,128]{1,0:T(8,128)(2,1)}, bf16[400,128]{1,0:T(8,128)(2,1)S(1)}, u32[]{:S(2)}, u32[]{:S(2)}) collective-permute-start(bf16[400,128]{1,0:T(8,128)(2,1)} %get-tuple-element.57), channel_id=1, source_target_pairs={{0,8},{4,12},{8,0},{12,4},{16,24},{20,28},{24,16},{28,20},{1,9},{5... | collective-permute-start | bytes 307208 | tf_op jit(solution)/shard_map/ppermute | solution.py:30
  10.2 15.5 %collective-permute-start.4 = (bf16[400,128]{1,0:T(8,128)(2,1)}, bf16[400,128]{1,0:T(8,128)(2,1)S(1)}, u32[]{:S(2)}, u32[]{:S(2)}) collective-permute-start(bf16[400,128]{1,0:T(8,128)(2,1)} %get-tuple-element.58), channel_id=1, source_target_pairs={{0,24},{4,28},{8,16},{12,20},{16,8},{20,12},{24,0},{28,4},{1,25},{... | collective-permute-start | bytes 307208 | tf_op jit(solution)/shard_map/ppermute | solution.py:30
  14.2 11.4 %copy-start.2 = (bf16[400,128]{1,0:T(8,128)(2,1)}, bf16[400,128]{1,0:T(8,128)(2,1)S(1)}, u32[]{:S(2)}) copy-start(bf16[400,128]{1,0:T(8,128)(2,1)S(1)} %collective-permute-done.refs_4_) | copy-start | bytes 307204
  14.2 11.5 %collective-permute-start.5 = (bf16[400,128]{1,0:T(8,128)(2,1)}, bf16[400,128]{1,0:T(8,128)(2,1)S(1)}, u32[]{:S(2)}, u32[]{:S(2)}) collective-permute-start(bf16[400,128]{1,0:T(8,128)(2,1)} %get-tuple-element.59), channel_id=1, source_target_pairs={{0,12},{4,8},{8,4},{12,0},{16,28},{20,24},{24,20},{28,16},{1,13},{... | collective-permute-start | bytes 307208 | tf_op jit(solution)/shard_map/ppermute | solution.py:30
  16.9 8.7 %copy-start.3 = (bf16[400,128]{1,0:T(8,128)(2,1)}, bf16[400,128]{1,0:T(8,128)(2,1)S(1)}, u32[]{:S(2)}) copy-start(bf16[400,128]{1,0:T(8,128)(2,1)S(1)} %collective-permute-done.1.refs_1_) | copy-start | bytes 307204
  16.9 8.7 %collective-permute-start.6 = (bf16[400,128]{1,0:T(8,128)(2,1)}, bf16[400,128]{1,0:T(8,128)(2,1)S(1)}, u32[]{:S(2)}, u32[]{:S(2)}) collective-permute-start(bf16[400,128]{1,0:T(8,128)(2,1)} %get-tuple-element.60), channel_id=1, source_target_pairs={{0,28},{4,24},{8,20},{12,16},{16,12},{20,8},{24,4},{28,0},{1,29},{... | collective-permute-start | bytes 307208 | tf_op jit(solution)/shard_map/ppermute | solution.py:30
  25.6 0.8 copy-start.4
  25.6 0.8 copy-start.5
  26.4 79.3 %all-to-all-start = ((bf16[32,384,128]{2,1,0:T(8,128)(2,1)}), bf16[32,384,128]{2,1,0:T(8,128)(2,1)S(1)}, u32[]{:S(2)}, u32[]{:S(2)}) async-start(bf16[32,384,128]{2,1,0:T(8,128)(2,1)} %pack_all.1), calls=%async_computation | async-start | bytes 6291456 | tf_op jit(solution)/shard_map/all_to_all | solution.py:417
  33.6 41.7 %collective-permute-start.8 = (bf16[8,272,128]{2,1,0:T(8,128)(2,1)}, bf16[8,272,128]{2,1,0:T(8,128)(2,1)}, u32[]{:S(2)}, u32[]{:S(2)}) collective-permute-start(bf16[8,272,128]{2,1,0:T(8,128)(2,1)} %get-tuple-element.63.refs_1_), channel_id=1, source_target_pairs={{0,2},{1,3},{2,0},{3,1},{4,6},{5,7},{6,4},{7,5},{8,10},{9,11},{10,... | collective-permute-start | bytes 1671176 | tf_op jit(solution)/shard_map/ppermute | solution.py:30
  35.4 40.6 %collective-permute-start.7 = (bf16[8,272,128]{2,1,0:T(8,128)(2,1)}, bf16[8,272,128]{2,1,0:T(8,128)(2,1)}, u32[]{:S(2)}, u32[]{:S(2)}) collective-permute-start(bf16[8,272,128]{2,1,0:T(8,128)(2,1)} %get-tuple-element.63.refs_1_), channel_id=1, source_target_pairs={{0,1},{1,0},{2,3},{3,2},{4,5},{5,4},{6,7},{7,6},{8,9},{9,8},{10,11... | collective-permute-start | bytes 1671176 | tf_op jit(solution)/shard_map/ppermute | solution.py:30
  75.3 2.3 %collective-permute-start.9 = (bf16[8,272,128]{2,1,0:T(8,128)(2,1)}, bf16[8,272,128]{2,1,0:T(8,128)(2,1)}, u32[]{:S(2)}, u32[]{:S(2)}) collective-permute-start(bf16[8,272,128]{2,1,0:T(8,128)(2,1)} %collective-permute-done.8.refs_3_), channel_id=1, source_target_pairs={{0,1},{1,0},{2,3},{3,2},{4,5},{5,4},{6,7},{7,6},{8,9},{9,8},{10,11... | collective-permute-start | bytes 1671176 | tf_op jit(solution)/shard_map/ppermute | solution.py:30
  78.4 1.0 copy-start.1
  84.7 30.2 %collective-permute-start.10 = (bf16[128,128]{1,0:T(8,128)(2,1)}, bf16[128,128]{1,0:T(8,128)(2,1)S(1)}, u32[]{:S(2)}, u32[]{:S(2)}) collective-permute-start(bf16[128,128]{1,0:T(8,128)(2,1)} %get-tuple-element.69), channel_id=1, source_target_pairs={{0,16},{4,20},{8,24},{12,28},{16,0},{20,4},{24,8},{28,12},{1,17},{... | collective-permute-start | bytes 98312 | tf_op jit(solution)/shard_map/ppermute | solution.py:30
  84.8 30.1 %collective-permute-start.11 = (bf16[128,128]{1,0:T(8,128)(2,1)S(1)}, bf16[128,128]{1,0:T(8,128)(2,1)S(1)}, u32[]{:S(2)}, u32[]{:S(2)}) collective-permute-start(bf16[128,128]{1,0:T(8,128)(2,1)S(1)} %get-tuple-element.70), channel_id=1, source_target_pairs={{0,20},{4,16},{8,28},{12,24},{16,4},{20,0},{24,12},{28,8},{1,21},{... | collective-permute-start | bytes 98312 | tf_op jit(solution)/shard_map/ppermute | solution.py:30
  87.5 27.4 %collective-permute-start.12 = (bf16[128,128]{1,0:T(8,128)(2,1)S(1)}, bf16[128,128]{1,0:T(8,128)(2,1)S(1)}, u32[]{:S(2)}, u32[]{:S(2)}) collective-permute-start(bf16[128,128]{1,0:T(8,128)(2,1)S(1)} %get-tuple-element.71), channel_id=1, source_target_pairs={{0,24},{4,28},{8,16},{12,20},{16,8},{20,12},{24,0},{28,4},{1,25},{... | collective-permute-start | bytes 98312 | tf_op jit(solution)/shard_map/ppermute | solution.py:30
  89.1 25.8 %collective-permute-start.13 = (bf16[128,128]{1,0:T(8,128)(2,1)S(1)}, bf16[128,128]{1,0:T(8,128)(2,1)S(1)}, u32[]{:S(2)}, u32[]{:S(2)}) collective-permute-start(bf16[128,128]{1,0:T(8,128)(2,1)S(1)} %get-tuple-element.72), channel_id=1, source_target_pairs={{0,28},{4,24},{8,20},{12,16},{16,12},{20,8},{24,4},{28,0},{1,29},{... | collective-permute-start | bytes 98312 | tf_op jit(solution)/shard_map/ppermute | solution.py:30
  92.5 22.5 %collective-permute-start.14 = (bf16[128,128]{1,0:T(8,128)(2,1)S(1)}, bf16[128,128]{1,0:T(8,128)(2,1)S(1)}, u32[]{:S(2)}, u32[]{:S(2)}) collective-permute-start(bf16[128,128]{1,0:T(8,128)(2,1)S(1)} %get-tuple-element.68), channel_id=1, source_target_pairs={{0,12},{4,8},{8,4},{12,0},{16,28},{20,24},{24,20},{28,16},{1,13},{... | collective-permute-start | bytes 98312 | tf_op jit(solution)/shard_map/ppermute | solution.py:30
  114.9 29.6 %all-to-all-start.1 = ((bf16[32,128,128]{2,1,0:T(8,128)(2,1)}), bf16[32,128,128]{2,1,0:T(8,128)(2,1)S(1)}, u32[]{:S(2)}, u32[]{:S(2)}) async-start(bf16[32,128,128]{2,1,0:T(8,128)(2,1)} %attend_all.1), calls=%async_computation.1 | async-start | bytes 2097152 | tf_op jit(solution)/shard_map/all_to_all | solution.py:442
  118.4 7.7 %collective-permute-start.15 = (bf16[128,128]{1,0:T(8,128)(2,1)S(1)}, bf16[128,128]{1,0:T(8,128)(2,1)S(1)}, u32[]{:S(2)}, u32[]{:S(2)}) collective-permute-start(bf16[128,128]{1,0:T(8,128)(2,1)S(1)} %get-tuple-element.66), channel_id=1, source_target_pairs={{0,4},{4,0},{8,12},{12,8},{16,20},{20,16},{24,28},{28,24},{1,5},{5... | collective-permute-start | bytes 98312 | tf_op jit(solution)/shard_map/ppermute | solution.py:30
  120.2 16.5 %collective-permute-start.16 = (bf16[128,128]{1,0:T(8,128)(2,1)S(1)}, bf16[128,128]{1,0:T(8,128)(2,1)S(1)}, u32[]{:S(2)}, u32[]{:S(2)}) collective-permute-start(bf16[128,128]{1,0:T(8,128)(2,1)S(1)} %get-tuple-element.67), channel_id=1, source_target_pairs={{0,8},{4,12},{8,0},{12,4},{16,24},{20,28},{24,16},{28,20},{1,9},{5... | collective-permute-start | bytes 98312 | tf_op jit(solution)/shard_map/ppermute | solution.py:30
  (4 other events, 2.8 us)

commit v4 on v3

--- a/solution.py
+++ b/solution.py
@@ -15,7 +15,8 @@
 ROW = LIST_LEN + 1
 MIB = 1024 * 1024
 CHUNK = 2
-TOGETHER = 4
+TOGETHER = 8
+REST_TOGETHER = 4
 TABLE_ROWS = 16
 IN_FLIGHT = 5
 TIED = 7
@@ -31,11 +32,10 @@
 
 
 def gather_all(x, axis):
-    parts = {0: x}
-    bit = lax.axis_size(axis) // 2
-    while bit:
+    parts, bit = {0: x}, 1
+    while bit < lax.axis_size(axis):
         parts.update({rel | bit: swap(part, axis, bit) for rel, part in list(parts.items())})
-        bit //= 2
+        bit *= 2
     return [parts[rel] for rel in range(lax.axis_size(axis))]
 
 
@@ -108,14 +108,14 @@
     rows = 3 * count * BLOCK_LEN + TABLE_ROWS
     return pl.pallas_call(
         functools.partial(pack_rest_kernel, head_axis, start, each, first, count, peers),
-        out_shape=[jax.ShapeDtypeStruct((rows, HEAD_DIM), queries.dtype)] * peers,
+        out_shape=[pltpu.VMEM((rows, HEAD_DIM), queries.dtype)] * peers,
         in_specs=[SMEM] * 2 + [ANY] * 3,
         out_specs=[pl.BlockSpec(memory_space=pltpu.VMEM)] * peers,
         scratch_shapes=[pltpu.SemaphoreType.DMA],
         cost_estimate=pl.CostEstimate(
             flops=0, transcendentals=0, bytes_accessed=peers * rows * HEAD_DIM * 4
         ),
-        compiler_params=pltpu.CompilerParams(vmem_limit_bytes=56 * MIB),
+        compiler_params=pltpu.CompilerParams(vmem_limit_bytes=60 * MIB),
         name="pack_rest",
     )(lists, counts, keys, values, queries)
 
@@ -257,7 +257,7 @@
         ),
         compiler_params=pltpu.CompilerParams(vmem_limit_bytes=12 * MIB),
         name="stack",
-    )(*[pltpu.with_memory_space_constraint(piece, pltpu.HBM) for piece in pieces])
+    )(pieces[0], *[pltpu.with_memory_space_constraint(piece, pltpu.HBM) for piece in pieces[1:]])
 
 
 def attend_rest_kernel(head_axis, gather_axis, count, peers, others, place, table, *refs):
@@ -274,14 +274,9 @@
         copy.start()
     for copy in copies:
         copy.wait()
-    my_head, my_gather = lax.axis_index(head_axis), lax.axis_index(gather_axis)
-    inner = lax.axis_size("uly")
-
     def step(j, carry):
-        mine = [j * TOGETHER + t for t in range(TOGETHER)]
-        heads = [my_head ^ rel for rel in mine]
-        blocks = [h * inner + my_gather if head_axis == "seq" else my_gather * inner + h for h in heads]
-        rows = [place(block) * ROW for block in blocks]
+        mine = [j * REST_TOGETHER + t for t in range(REST_TOGETHER)]
+        rows = [rel * ROW for rel in mine]
         useds = [table[row + LIST_LEN] for row in rows]
         for i in range(count):
             own = pl.ds(i * BLOCK_LEN, BLOCK_LEN)
@@ -297,7 +292,7 @@
             attend_blocks([q_buf[r, own] for r in mine], useds, pairs, write)
         return carry
 
-    lax.fori_loop(0, peers // TOGETHER, step, 0)
+    lax.fori_loop(0, peers // REST_TOGETHER, step, 0)
     copies = [
         pltpu.make_async_copy(o_buf.at[rel], outs[rel], out_sem) for rel in range(peers)
     ]
@@ -326,13 +321,13 @@
         compiler_params=pltpu.CompilerParams(vmem_limit_bytes=2 * math.prod(kv_shape) + 8 * MIB),
         cost_estimate=attend_cost(peers, count, 2 * math.prod(kv_shape)),
         name="attend_rest",
-    )(table, queries, *gathered)
+    )(table, pltpu.with_memory_space_constraint(queries, pltpu.HBM), *gathered)
 
 
 def unpack_kernel(head_axis, start, each, full, chunks, peers, devices, *refs):
     has_main = 1 if full else 0
     n = has_main + len(chunks) * peers
-    parts, out_ref, buf, in_sem, out_sem = refs[:n], refs[n], refs[n + 1], refs[n + 2], refs[n + 3]
+    parts, out_ref, sem = refs[:n], refs[n], refs[n + 1]
     me = lax.axis_index(head_axis)
     copies = []
     for d in range(devices * has_main):
@@ -340,8 +335,8 @@
             copies.append(
                 pltpu.make_async_copy(
                     parts[0].at[d, pl.ds(i * BLOCK_LEN, BLOCK_LEN)],
-                    buf.at[:, pl.ds((d * full + i) * HEAD_DIM, HEAD_DIM)],
-                    in_sem,
+                    out_ref.at[:, pl.ds((d * full + i) * HEAD_DIM, HEAD_DIM)],
+                    sem,
                 )
             )
     for j, (first, count) in enumerate(chunks):
@@ -351,17 +346,14 @@
                 copies.append(
                     pltpu.make_async_copy(
                         parts[has_main + j * peers + rel].at[pl.ds(i * BLOCK_LEN, BLOCK_LEN)],
-                        buf.at[:, pl.ds(col, HEAD_DIM)],
-                        in_sem,
+                        out_ref.at[:, pl.ds(col, HEAD_DIM)],
+                        sem,
                     )
                 )
     for copy in copies:
         copy.start()
     for copy in copies:
         copy.wait()
-    copy = pltpu.make_async_copy(buf, out_ref, out_sem)
-    copy.start()
-    copy.wait()
 
 
 def unpack(parts, head_axis, start, each, full, chunks, devices, width):
@@ -371,11 +363,7 @@
         out_shape=jax.ShapeDtypeStruct((BLOCK_LEN, width), jnp.bfloat16),
         in_specs=[ANY] * len(parts),
         out_specs=ANY,
-        scratch_shapes=[
-            pltpu.VMEM((BLOCK_LEN, width), jnp.bfloat16),
-            pltpu.SemaphoreType.DMA,
-            pltpu.SemaphoreType.DMA,
-        ],
+        scratch_shapes=[pltpu.SemaphoreType.DMA],
         cost_estimate=pl.CostEstimate(
             flops=0, transcendentals=0, bytes_accessed=2 * BLOCK_LEN * width * 2
         ),
@@ -419,15 +407,15 @@
     for (first, count), pieces in zip(chunks, arrivals):
         kv_rows = 2 * count * BLOCK_LEN
         kv, q = stack(pieces, kv_rows + TABLE_ROWS)
+        lists = kv[:, kv_rows, :ROW].astype(jnp.int32).reshape(-1)
         gathered = gather_all(kv, gather_axis)
         if table is None:
-            table = jnp.concatenate([part[:, kv_rows, :ROW] for part in gathered])
-            table = table.astype(jnp.int32)
-            counts, table = table[:, LIST_LEN], table.reshape(-1)
-        outputs.append(attend_rest(table, q, gathered, head_axis, gather_axis, count, place))
+            table = jnp.concatenate([part[:, kv_rows, :ROW] for part in gathered]).astype(jnp.int32)
+        outputs.append(attend_rest(lists, q, gathered, head_axis, gather_axis, count, place))
     results, backs = [], []
     if full:
-        ordered = jnp.concatenate([table, by_count(counts, block_ids(head_axis, gather_axis))])
+        ordered = by_count(table[:, LIST_LEN], block_ids(head_axis, gather_axis))
+        ordered = jnp.concatenate([table.reshape(-1), ordered])
         arrived, ordered, _ = lax.optimization_barrier((arrived, ordered, outputs))
         blended = attend_all(ordered, arrived, full, place)
     for outs in outputs:

time: 147 us -> 146 us (level)
  starting transfers between devices: 37.7 us -> 43.4 us
  waiting for transfers between devices: 77.1 us -> 71.6 us
    all_to_all x1, waiting for transfers between devices: 12.7 us -> 0.58 us  [body(): lax.all_to_all(sent, DEVICES, split_axis=0, concat_axis=0, tiled=True)]
    ppermute x17, waiting for transfers between devices: 56.6 us -> 63.2 us  [swap(): lax.ppermute(x, axis, [(i, i ^ bit) for i in range(lax.axis_size(axis))])]
    ppermute x17, starting transfers between devices: 29.8 us -> 34.2 us  [swap(): lax.ppermute(x, axis, [(i, i ^ bit) for i in range(lax.axis_size(axis))])]
  transfers between devices with their start and end apart: 19 -> 19, of which waited for: 7 -> 8; matrix products, arithmetic and copies ran while one was open for 2% -> 3% of each run, Pallas kernels for 14% -> 15%
where the time goes in v4:
time: 146 us; the launch traced here: 145 us
  waiting for transfers between devices  71.6 us (49%)
  starting transfers between devices  43.4 us (30%)
  Pallas kernels  24 us (16%)
  local copies, waits for them, and re-layouts  4.51 us (3%)
    ppermute x17, waiting for transfers between devices, swap(): lax.ppermute(x, axis, [(i, i ^ bit) for i in range(lax.axis_size(axis))])  63.2 us
    ppermute x17, starting transfers between devices, swap(): lax.ppermute(x, axis, [(i, i ^ bit) for i in range(lax.axis_size(axis))])  34.2 us
    pallas_call x1, Pallas kernels, attend_all(): pl.pallas_call(functools.partial(attend_all_kernel, full, place), out_sha...  9.05 us
    all_to_all x1, waiting for transfers between devices, body(): lax.all_to_all(blended, DEVICES, split_axis=0, concat_axis=0, tiled=True)  7.89 us
    pallas_call x1, Pallas kernels, attend_rest(): pl.pallas_call(functools.partial(attend_rest_kernel, head_axis, gather_ax...  5.63 us
    all_to_all x1, starting transfers between devices, body(): lax.all_to_all(blended, DEVICES, split_axis=0, concat_axis=0, tiled=True)  4.64 us
    all_to_all x1, starting transfers between devices, body(): lax.all_to_all(sent, DEVICES, split_axis=0, concat_axis=0, tiled=True)  4.56 us
    pallas_call x1, Pallas kernels, pack_all(): pl.pallas_call(functools.partial(pack_all_kernel, full, step), grid=(devi...  4.32 us
  transfers between devices with their start and end apart: 19, of which 8 were waited for; matrix products, arithmetic and copies ran while one was open for 3% of the time, Pallas kernels for 15%

profile of v4, /device:TPU:0, one launch (start us, length us, event | category | flops | bytes accessed | tf_op | source)
XLA Modules:
  0.0 145.2 jit_solution(11638197403226308644)
XLA Ops:
  0.0 1.8 %pack_rest.1 = (bf16[400,128]{1,0:T(8,128)(2,1)S(1)}, bf16[400,128]{1,0:T(8,128)(2,1)S(1)}, bf16[400,128]{1,0:T(8,128)(2,1)S(1)}, bf16[400,128]{1,0:T(8,128)(2,1...) custom-call(s32[4,12]{1,0:T(4,128)} %lists.1, ...), custom_call_target="tpu_custom_call" | custom-call | bytes 1638400 | tf_op jit(solution)/shard_map/pack_rest/pallas_call | solution.py:109
  1.8 4.1 %collective-permute-start = (bf16[400,128]{1,0:T(8,128)(2,1)S(1)}, bf16[400,128]{1,0:T(8,128)(2,1)S(1)}, u32[]{:S(2)}, u32[]{:S(2)}) collective-permute-start(bf16[400,128]{1,0:T(8,128)(2,1)S(1)} %get-tuple-element.54), channel_id=1, source_target_pairs={{0,16},{4,20},{8,24},{12,28},{16,0},{20,4},{24,8},{28,12},{1,17},{... | collective-permute-start | bytes 307208 | tf_op jit(solution)/shard_map/ppermute | solution.py:31
  5.9 1.5 %collective-permute-start.1 = (bf16[400,128]{1,0:T(8,128)(2,1)S(1)}, bf16[400,128]{1,0:T(8,128)(2,1)S(1)}, u32[]{:S(2)}, u32[]{:S(2)}) collective-permute-start(bf16[400,128]{1,0:T(8,128)(2,1)S(1)} %get-tuple-element.55), channel_id=1, source_target_pairs={{0,4},{4,0},{8,12},{12,8},{16,20},{20,16},{24,28},{28,24},{1,5},{5... | collective-permute-start | bytes 307208 | tf_op jit(solution)/shard_map/ppermute | solution.py:31
  7.5 1.8 %collective-permute-start.3 = (bf16[400,128]{1,0:T(8,128)(2,1)S(1)}, bf16[400,128]{1,0:T(8,128)(2,1)S(1)}, u32[]{:S(2)}, u32[]{:S(2)}) collective-permute-start(bf16[400,128]{1,0:T(8,128)(2,1)S(1)} %get-tuple-element.57), channel_id=1, source_target_pairs={{0,8},{4,12},{8,0},{12,4},{16,24},{20,28},{24,16},{28,20},{1,9},{5... | collective-permute-start | bytes 307208 | tf_op jit(solution)/shard_map/ppermute | solution.py:31
  9.3 2.5 %collective-permute-start.4 = (bf16[400,128]{1,0:T(8,128)(2,1)S(1)}, bf16[400,128]{1,0:T(8,128)(2,1)S(1)}, u32[]{:S(2)}, u32[]{:S(2)}) collective-permute-start(bf16[400,128]{1,0:T(8,128)(2,1)S(1)} %get-tuple-element.58), channel_id=1, source_target_pairs={{0,24},{4,28},{8,16},{12,20},{16,8},{20,12},{24,0},{28,4},{1,25},{... | collective-permute-start | bytes 307208 | tf_op jit(solution)/shard_map/ppermute | solution.py:31
  13.1 2.7 %collective-permute-start.5 = (bf16[400,128]{1,0:T(8,128)(2,1)S(1)}, bf16[400,128]{1,0:T(8,128)(2,1)S(1)}, u32[]{:S(2)}, u32[]{:S(2)}) collective-permute-start(bf16[400,128]{1,0:T(8,128)(2,1)S(1)} %get-tuple-element.59), channel_id=1, source_target_pairs={{0,12},{4,8},{8,4},{12,0},{16,28},{20,24},{24,20},{28,16},{1,13},{... | collective-permute-start | bytes 307208 | tf_op jit(solution)/shard_map/ppermute | solution.py:31
  15.8 4.3 %collective-permute-start.6 = (bf16[400,128]{1,0:T(8,128)(2,1)S(1)}, bf16[400,128]{1,0:T(8,128)(2,1)S(1)}, u32[]{:S(2)}, u32[]{:S(2)}) collective-permute-start(bf16[400,128]{1,0:T(8,128)(2,1)S(1)} %get-tuple-element.60), channel_id=1, source_target_pairs={{0,28},{4,24},{8,20},{12,16},{16,12},{20,8},{24,4},{28,0},{1,29},{... | collective-permute-start | bytes 307208 | tf_op jit(solution)/shard_map/ppermute | solution.py:31
  20.1 4.3 %pack_all.1 = bf16[32,384,128]{2,1,0:T(8,128)(2,1)} custom-call(bf16[128,5120]{1,0:T(8,128)(2,1)} %k_ref.2, bf16[128,5120]{1,0:T(8,128)(2,1)} %v_ref.2, bf16[128,5120]{1,0:T(8,128)(2,1)} %q_ref.2), custom_call_target="tpu_custom_call" | custom-call | bytes 6291456 | tf_op jit(solution)/shard_map/pack_all/pallas_call | solution.py:64
  25.2 4.6 %all-to-all-start = ((bf16[32,384,128]{2,1,0:T(8,128)(2,1)}), bf16[32,384,128]{2,1,0:T(8,128)(2,1)S(1)}, u32[]{:S(2)}, u32[]{:S(2)}) async-start(bf16[32,384,128]{2,1,0:T(8,128)(2,1)} %pack_all.1), calls=%async_computation | async-start | bytes 6291456 | tf_op jit(solution)/shard_map/all_to_all | solution.py:405
  29.8 2.1 %stack.1 = (bf16[8,272,128]{2,1,0:T(8,128)(2,1)}, bf16[8,128,128]{2,1,0:T(8,128)(2,1)S(1)}) custom-call(bf16[400,128]{1,0:T(8,128)(2,1)S(1)} %get-tuple-element.62.refs_0_, bf16[400,128]{1,0:T(8,128)(2,1)} %copy-done.2, bf16[400,128]{1,0:T(8,128)(2,1)} %copy-done.4, bf16[400,128]{1,0:T(8,128)(2,1)} %copy-done.6, bf16[400,128]{1,0:T(8,128)(2,1)} %copy-done.1, ...), custom_call_target="tpu_custom_call" | custom-call | bytes 1638400 | tf_op jit(solution)/shard_map/stack/pallas_call | solution.py:249
  32.8 1.7 %collective-permute-start.8 = (bf16[8,272,128]{2,1,0:T(8,128)(2,1)}, bf16[8,272,128]{2,1,0:T(8,128)(2,1)}, u32[]{:S(2)}, u32[]{:S(2)}) collective-permute-start(bf16[8,272,128]{2,1,0:T(8,128)(2,1)} %get-tuple-element.63.refs_1_), channel_id=1, source_target_pairs={{0,2},{1,3},{2,0},{3,1},{4,6},{5,7},{6,4},{7,5},{8,10},{9,11},{10,... | collective-permute-start | bytes 1671176 | tf_op jit(solution)/shard_map/ppermute | solution.py:31
  34.9 1.8 %collective-permute-start.9 = (bf16[8,272,128]{2,1,0:T(8,128)(2,1)}, bf16[8,272,128]{2,1,0:T(8,128)(2,1)}, u32[]{:S(2)}, u32[]{:S(2)}) collective-permute-start(bf16[8,272,128]{2,1,0:T(8,128)(2,1)} %collective-permute-done.7.refs_2_), channel_id=1, source_target_pairs={{0,2},{1,3},{2,0},{3,1},{4,6},{5,7},{6,4},{7,5},{8,10},{9,11},{10,... | collective-permute-start | bytes 1671176 | tf_op jit(solution)/shard_map/ppermute | solution.py:31
  38.9 35.7 %collective-permute-done.8.refs_3_ = bf16[8,272,128]{2,1,0:T(8,128)(2,1)} collective-permute-done((bf16[8,272,128]{2,1,0:T(8,128)(2,1)}, bf16[8,272,128]{2,1,0:T(8,128)(2,1)}, u32[]{:S(2)}, u32[]{:S(2)}) %collective-permute-start.8) | collective-permute-done | bytes 557088 | tf_op jit(solution)/shard_map/ppermute | solution.py:31
  75.4 10.7 %collective-permute-done.9.refs_4_ = bf16[8,272,128]{2,1,0:T(8,128)(2,1)} collective-permute-done((bf16[8,272,128]{2,1,0:T(8,128)(2,1)}, bf16[8,272,128]{2,1,0:T(8,128)(2,1)}, u32[]{:S(2)}, u32[]{:S(2)}) %collective-permute-start.9) | collective-permute-done | bytes 557088 | tf_op jit(solution)/shard_map/ppermute | solution.py:31
  86.9 5.6 %attend_rest.1 = (bf16[128,128]{1,0:T(8,128)(2,1)S(1)}, bf16[128,128]{1,0:T(8,128)(2,1)S(1)}, bf16[128,128]{1,0:T(8,128)(2,1)S(1)}, bf16[128,128]{1,0:T(8,128)(2...) custom-call(s32[104]{0:T(128)S(1)} %reshape.46.table, ...), custom_call_target="tpu_custom_call" | custom-call | flops 805306368 | bytes 2097152 | tf_op jit(solution)/shard_map/attend_rest/pallas_call | solution.py:309
  92.6 4.0 %collective-permute-start.10 = (bf16[128,128]{1,0:T(8,128)(2,1)}, bf16[128,128]{1,0:T(8,128)(2,1)S(1)}, u32[]{:S(2)}, u32[]{:S(2)}) collective-permute-start(bf16[128,128]{1,0:T(8,128)(2,1)} %get-tuple-element.69), channel_id=1, source_target_pairs={{0,16},{4,20},{8,24},{12,28},{16,0},{20,4},{24,8},{28,12},{1,17},{... | collective-permute-start | bytes 98312 | tf_op jit(solution)/shard_map/ppermute | solution.py:31
  96.5 2.0 %collective-permute-start.11 = (bf16[128,128]{1,0:T(8,128)(2,1)S(1)}, bf16[128,128]{1,0:T(8,128)(2,1)S(1)}, u32[]{:S(2)}, u32[]{:S(2)}) collective-permute-start(bf16[128,128]{1,0:T(8,128)(2,1)S(1)} %get-tuple-element.70), channel_id=1, source_target_pairs={{0,20},{4,16},{8,28},{12,24},{16,4},{20,0},{24,12},{28,8},{1,21},{... | collective-permute-start | bytes 98312 | tf_op jit(solution)/shard_map/ppermute | solution.py:31
  99.8 2.4 %collective-permute-start.13 = (bf16[128,128]{1,0:T(8,128)(2,1)S(1)}, bf16[128,128]{1,0:T(8,128)(2,1)S(1)}, u32[]{:S(2)}, u32[]{:S(2)}) collective-permute-start(bf16[128,128]{1,0:T(8,128)(2,1)S(1)} %get-tuple-element.72), channel_id=1, source_target_pairs={{0,28},{4,24},{8,20},{12,16},{16,12},{20,8},{24,4},{28,0},{1,29},{... | collective-permute-start | bytes 98312 | tf_op jit(solution)/shard_map/ppermute | solution.py:31
  104.0 9.1 %attend_all.1 = bf16[32,128,128]{2,1,0:T(8,128)(2,1)} custom-call(s32[448]{0:T(512)S(1)} %pad_add_fusion.table_ref, bf16[32,384,128]{2,1,0:T(8,128)(2,1)S(1)} %all-to-all-done.buf), custom_call_target="tpu_custom_call" | custom-call | flops 3221225472 | bytes 3145728 | tf_op jit(solution)/shard_map/attend_all/pallas_call | solution.py:201
  113.1 4.6 %all-to-all-start.1 = ((bf16[32,128,128]{2,1,0:T(8,128)(2,1)}), bf16[32,128,128]{2,1,0:T(8,128)(2,1)S(1)}, u32[]{:S(2)}, u32[]{:S(2)}) async-start(bf16[32,128,128]{2,1,0:T(8,128)(2,1)} %attend_all.1), calls=%async_computation.1 | async-start | bytes 2097152 | tf_op jit(solution)/shard_map/all_to_all | solution.py:430
  117.7 1.8 %collective-permute-start.15 = (bf16[128,128]{1,0:T(8,128)(2,1)S(1)}, bf16[128,128]{1,0:T(8,128)(2,1)S(1)}, u32[]{:S(2)}, u32[]{:S(2)}) collective-permute-start(bf16[128,128]{1,0:T(8,128)(2,1)S(1)} %get-tuple-element.66), channel_id=1, source_target_pairs={{0,4},{4,0},{8,12},{12,8},{16,20},{20,16},{24,28},{28,24},{1,5},{5... | collective-permute-start | bytes 98312 | tf_op jit(solution)/shard_map/ppermute | solution.py:31
  121.0 4.4 %collective-permute-done.15.refs_2_ = bf16[128,128]{1,0:T(8,128)(2,1)S(1)} collective-permute-done((bf16[128,128]{1,0:T(8,128)(2,1)S(1)}, bf16[128,128]{1,0:T(8,128)(2,1)S(1)}, u32[]{:S(2)}, u32[]{:S(2)}) %collective-permute-start.15) | collective-permute-done | bytes 32800 | tf_op jit(solution)/shard_map/ppermute | solution.py:31
  125.4 10.6 %collective-permute-done.16.refs_3_ = bf16[128,128]{1,0:T(8,128)(2,1)S(1)} collective-permute-done((bf16[128,128]{1,0:T(8,128)(2,1)S(1)}, bf16[128,128]{1,0:T(8,128)(2,1)S(1)}, u32[]{:S(2)}, u32[]{:S(2)}) %collective-permute-start.16) | collective-permute-done | bytes 32800 | tf_op jit(solution)/shard_map/ppermute | solution.py:31
  136.1 7.9 %all-to-all-done.1.refs_0_ = bf16[32,128,128]{2,1,0:T(8,128)(2,1)S(1)} async-done(((bf16[32,128,128]{2,1,0:T(8,128)(2,1)}), bf16[32,128,128]{2,1,0:T(8,128)(2,1)S(1)}, u32[]{:S(2)}, u32[]{:S(2)}) %all-to-all-start.1) | async-done | bytes 1048608 | tf_op jit(solution)/shard_map/all_to_all | solution.py:430
  (54 shorter events, 12.8 us)
Async XLA Ops:
  1.8 11.2 %collective-permute-start = (bf16[400,128]{1,0:T(8,128)(2,1)S(1)}, bf16[400,128]{1,0:T(8,128)(2,1)S(1)}, u32[]{:S(2)}, u32[]{:S(2)}) collective-permute-start(bf16[400,128]{1,0:T(8,128)(2,1)S(1)} %get-tuple-element.54), channel_id=1, source_target_pairs={{0,16},{4,20},{8,24},{12,28},{16,0},{20,4},{24,8},{28,12},{1,17},{... | collective-permute-start | bytes 307208 | tf_op jit(solution)/shard_map/ppermute | solution.py:31
  5.9 9.8 %collective-permute-start.1 = (bf16[400,128]{1,0:T(8,128)(2,1)S(1)}, bf16[400,128]{1,0:T(8,128)(2,1)S(1)}, u32[]{:S(2)}, u32[]{:S(2)}) collective-permute-start(bf16[400,128]{1,0:T(8,128)(2,1)S(1)} %get-tuple-element.55), channel_id=1, source_target_pairs={{0,4},{4,0},{8,12},{12,8},{16,20},{20,16},{24,28},{28,24},{1,5},{5... | collective-permute-start | bytes 307208 | tf_op jit(solution)/shard_map/ppermute | solution.py:31
  7.4 16.9 %collective-permute-start.2 = (bf16[400,128]{1,0:T(8,128)(2,1)S(1)}, bf16[400,128]{1,0:T(8,128)(2,1)S(1)}, u32[]{:S(2)}, u32[]{:S(2)}) collective-permute-start(bf16[400,128]{1,0:T(8,128)(2,1)S(1)} %get-tuple-element.56), channel_id=1, source_target_pairs={{0,20},{4,16},{8,28},{12,24},{16,4},{20,0},{24,12},{28,8},{1,21},{... | collective-permute-start | bytes 307208 | tf_op jit(solution)/shard_map/ppermute | solution.py:31
  7.5 16.9 %collective-permute-start.3 = (bf16[400,128]{1,0:T(8,128)(2,1)S(1)}, bf16[400,128]{1,0:T(8,128)(2,1)S(1)}, u32[]{:S(2)}, u32[]{:S(2)}) collective-permute-start(bf16[400,128]{1,0:T(8,128)(2,1)S(1)} %get-tuple-element.57), channel_id=1, source_target_pairs={{0,8},{4,12},{8,0},{12,4},{16,24},{20,28},{24,16},{28,20},{1,9},{5... | collective-permute-start | bytes 307208 | tf_op jit(solution)/shard_map/ppermute | solution.py:31
  9.3 15.1 %collective-permute-start.4 = (bf16[400,128]{1,0:T(8,128)(2,1)S(1)}, bf16[400,128]{1,0:T(8,128)(2,1)S(1)}, u32[]{:S(2)}, u32[]{:S(2)}) collective-permute-start(bf16[400,128]{1,0:T(8,128)(2,1)S(1)} %get-tuple-element.58), channel_id=1, source_target_pairs={{0,24},{4,28},{8,16},{12,20},{16,8},{20,12},{24,0},{28,4},{1,25},{... | collective-permute-start | bytes 307208 | tf_op jit(solution)/shard_map/ppermute | solution.py:31
  13.1 11.3 %copy-start.1 = (bf16[400,128]{1,0:T(8,128)(2,1)}, bf16[400,128]{1,0:T(8,128)(2,1)S(1)}, u32[]{:S(2)}) copy-start(bf16[400,128]{1,0:T(8,128)(2,1)S(1)} %collective-permute-done.refs_4_) | copy-start | bytes 307204
  13.1 11.4 %collective-permute-start.5 = (bf16[400,128]{1,0:T(8,128)(2,1)S(1)}, bf16[400,128]{1,0:T(8,128)(2,1)S(1)}, u32[]{:S(2)}, u32[]{:S(2)}) collective-permute-start(bf16[400,128]{1,0:T(8,128)(2,1)S(1)} %get-tuple-element.59), channel_id=1, source_target_pairs={{0,12},{4,8},{8,4},{12,0},{16,28},{20,24},{24,20},{28,16},{1,13},{... | collective-permute-start | bytes 307208 | tf_op jit(solution)/shard_map/ppermute | solution.py:31
  15.8 8.6 %copy-start.2 = (bf16[400,128]{1,0:T(8,128)(2,1)}, bf16[400,128]{1,0:T(8,128)(2,1)S(1)}, u32[]{:S(2)}) copy-start(bf16[400,128]{1,0:T(8,128)(2,1)S(1)} %collective-permute-done.1.refs_1_) | copy-start | bytes 307204
  15.8 8.7 %collective-permute-start.6 = (bf16[400,128]{1,0:T(8,128)(2,1)S(1)}, bf16[400,128]{1,0:T(8,128)(2,1)S(1)}, u32[]{:S(2)}, u32[]{:S(2)}) collective-permute-start(bf16[400,128]{1,0:T(8,128)(2,1)S(1)} %get-tuple-element.60), channel_id=1, source_target_pairs={{0,28},{4,24},{8,20},{12,16},{16,12},{20,8},{24,4},{28,0},{1,29},{... | collective-permute-start | bytes 307208 | tf_op jit(solution)/shard_map/ppermute | solution.py:31
  24.4 0.8 copy-start.3
  24.4 0.7 copy-start.6
  24.5 0.7 copy-start.7
  25.2 78.8 %all-to-all-start = ((bf16[32,384,128]{2,1,0:T(8,128)(2,1)}), bf16[32,384,128]{2,1,0:T(8,128)(2,1)S(1)}, u32[]{:S(2)}, u32[]{:S(2)}) async-start(bf16[32,384,128]{2,1,0:T(8,128)(2,1)} %pack_all.1), calls=%async_computation | async-start | bytes 6291456 | tf_op jit(solution)/shard_map/all_to_all | solution.py:405
  32.6 2.3 %collective-permute-start.7 = (bf16[8,272,128]{2,1,0:T(8,128)(2,1)}, bf16[8,272,128]{2,1,0:T(8,128)(2,1)}, u32[]{:S(2)}, u32[]{:S(2)}) collective-permute-start(bf16[8,272,128]{2,1,0:T(8,128)(2,1)} %get-tuple-element.63.refs_1_), channel_id=1, source_target_pairs={{0,1},{1,0},{2,3},{3,2},{4,5},{5,4},{6,7},{7,6},{8,9},{9,8},{10,11... | collective-permute-start | bytes 1671176 | tf_op jit(solution)/shard_map/ppermute | solution.py:31
  32.8 41.8 %collective-permute-start.8 = (bf16[8,272,128]{2,1,0:T(8,128)(2,1)}, bf16[8,272,128]{2,1,0:T(8,128)(2,1)}, u32[]{:S(2)}, u32[]{:S(2)}) collective-permute-start(bf16[8,272,128]{2,1,0:T(8,128)(2,1)} %get-tuple-element.63.refs_1_), channel_id=1, source_target_pairs={{0,2},{1,3},{2,0},{3,1},{4,6},{5,7},{6,4},{7,5},{8,10},{9,11},{10,... | collective-permute-start | bytes 1671176 | tf_op jit(solution)/shard_map/ppermute | solution.py:31
  34.9 51.2 %collective-permute-start.9 = (bf16[8,272,128]{2,1,0:T(8,128)(2,1)}, bf16[8,272,128]{2,1,0:T(8,128)(2,1)}, u32[]{:S(2)}, u32[]{:S(2)}) collective-permute-start(bf16[8,272,128]{2,1,0:T(8,128)(2,1)} %collective-permute-done.7.refs_2_), channel_id=1, source_target_pairs={{0,2},{1,3},{2,0},{3,1},{4,6},{5,7},{6,4},{7,5},{8,10},{9,11},{10,... | collective-permute-start | bytes 1671176 | tf_op jit(solution)/shard_map/ppermute | solution.py:31
  92.6 20.4 %collective-permute-start.10 = (bf16[128,128]{1,0:T(8,128)(2,1)}, bf16[128,128]{1,0:T(8,128)(2,1)S(1)}, u32[]{:S(2)}, u32[]{:S(2)}) collective-permute-start(bf16[128,128]{1,0:T(8,128)(2,1)} %get-tuple-element.69), channel_id=1, source_target_pairs={{0,16},{4,20},{8,24},{12,28},{16,0},{20,4},{24,8},{28,12},{1,17},{... | collective-permute-start | bytes 98312 | tf_op jit(solution)/shard_map/ppermute | solution.py:31
  96.5 16.5 %collective-permute-start.11 = (bf16[128,128]{1,0:T(8,128)(2,1)S(1)}, bf16[128,128]{1,0:T(8,128)(2,1)S(1)}, u32[]{:S(2)}, u32[]{:S(2)}) collective-permute-start(bf16[128,128]{1,0:T(8,128)(2,1)S(1)} %get-tuple-element.70), channel_id=1, source_target_pairs={{0,20},{4,16},{8,28},{12,24},{16,4},{20,0},{24,12},{28,8},{1,21},{... | collective-permute-start | bytes 98312 | tf_op jit(solution)/shard_map/ppermute | solution.py:31
  98.5 14.5 %collective-permute-start.12 = (bf16[128,128]{1,0:T(8,128)(2,1)S(1)}, bf16[128,128]{1,0:T(8,128)(2,1)S(1)}, u32[]{:S(2)}, u32[]{:S(2)}) collective-permute-start(bf16[128,128]{1,0:T(8,128)(2,1)S(1)} %get-tuple-element.71), channel_id=1, source_target_pairs={{0,24},{4,28},{8,16},{12,20},{16,8},{20,12},{24,0},{28,4},{1,25},{... | collective-permute-start | bytes 98312 | tf_op jit(solution)/shard_map/ppermute | solution.py:31
  99.8 13.2 %collective-permute-start.13 = (bf16[128,128]{1,0:T(8,128)(2,1)S(1)}, bf16[128,128]{1,0:T(8,128)(2,1)S(1)}, u32[]{:S(2)}, u32[]{:S(2)}) collective-permute-start(bf16[128,128]{1,0:T(8,128)(2,1)S(1)} %get-tuple-element.72), channel_id=1, source_target_pairs={{0,28},{4,24},{8,20},{12,16},{16,12},{20,8},{24,4},{28,0},{1,29},{... | collective-permute-start | bytes 98312 | tf_op jit(solution)/shard_map/ppermute | solution.py:31
  102.3 10.8 %collective-permute-start.14 = (bf16[128,128]{1,0:T(8,128)(2,1)S(1)}, bf16[128,128]{1,0:T(8,128)(2,1)S(1)}, u32[]{:S(2)}, u32[]{:S(2)}) collective-permute-start(bf16[128,128]{1,0:T(8,128)(2,1)S(1)} %get-tuple-element.68), channel_id=1, source_target_pairs={{0,12},{4,8},{8,4},{12,0},{16,28},{20,24},{24,20},{28,16},{1,13},{... | collective-permute-start | bytes 98312 | tf_op jit(solution)/shard_map/ppermute | solution.py:31
  113.1 30.9 %all-to-all-start.1 = ((bf16[32,128,128]{2,1,0:T(8,128)(2,1)}), bf16[32,128,128]{2,1,0:T(8,128)(2,1)S(1)}, u32[]{:S(2)}, u32[]{:S(2)}) async-start(bf16[32,128,128]{2,1,0:T(8,128)(2,1)} %attend_all.1), calls=%async_computation.1 | async-start | bytes 2097152 | tf_op jit(solution)/shard_map/all_to_all | solution.py:430
  117.7 7.7 %collective-permute-start.15 = (bf16[128,128]{1,0:T(8,128)(2,1)S(1)}, bf16[128,128]{1,0:T(8,128)(2,1)S(1)}, u32[]{:S(2)}, u32[]{:S(2)}) collective-permute-start(bf16[128,128]{1,0:T(8,128)(2,1)S(1)} %get-tuple-element.66), channel_id=1, source_target_pairs={{0,4},{4,0},{8,12},{12,8},{16,20},{20,16},{24,28},{28,24},{1,5},{5... | collective-permute-start | bytes 98312 | tf_op jit(solution)/shard_map/ppermute | solution.py:31
  119.6 16.5 %collective-permute-start.16 = (bf16[128,128]{1,0:T(8,128)(2,1)S(1)}, bf16[128,128]{1,0:T(8,128)(2,1)S(1)}, u32[]{:S(2)}, u32[]{:S(2)}) collective-permute-start(bf16[128,128]{1,0:T(8,128)(2,1)S(1)} %get-tuple-element.67), channel_id=1, source_target_pairs={{0,8},{4,12},{8,0},{12,4},{16,24},{20,28},{24,16},{28,20},{1,9},{5... | collective-permute-start | bytes 98312 | tf_op jit(solution)/shard_map/ppermute | solution.py:31
  (3 other events, 2.0 us)

commit v5 on v4

--- a/solution.py
+++ b/solution.py
@@ -18,7 +18,7 @@
 TOGETHER = 8
 REST_TOGETHER = 4
 TABLE_ROWS = 16
-IN_FLIGHT = 5
+IN_FLIGHT = 4
 TIED = 7
 SCORE_FACTOR = HEAD_DIM**-0.5 * math.log2(math.e)
 ANY = pl.BlockSpec(memory_space=pl.ANY)
@@ -155,11 +155,8 @@
         pl.when((most == entries) | (most == entries - 1))(functools.partial(run, entries))
 
 
-def attend_all_kernel(full, place, table_ref, buf, out_ref, table, o_buf, in_sem, out_sem):
+def attend_all_kernel(full, place, table, buf, out_ref, o_buf, out_sem):
     devices = buf.shape[0]
-    copy = pltpu.make_async_copy(table_ref, table, in_sem)
-    copy.start()
-    copy.wait()
 
     def step(j, carry):
         blocks = [table[devices * ROW + j * TOGETHER + t] for t in range(TOGETHER)]
@@ -201,18 +198,16 @@
     return pl.pallas_call(
         functools.partial(attend_all_kernel, full, place),
         out_shape=pltpu.HBM(shape, jnp.bfloat16),
-        in_specs=[HBM, pl.BlockSpec(memory_space=pltpu.VMEM)],
+        in_specs=[SMEM, pl.BlockSpec(memory_space=pltpu.VMEM)],
         out_specs=HBM,
         scratch_shapes=[
-            pltpu.SMEM(table.shape, jnp.int32),
             pltpu.VMEM(shape, jnp.bfloat16),
-            pltpu.SemaphoreType.DMA,
             pltpu.SemaphoreType.DMA,
         ],
         compiler_params=pltpu.CompilerParams(vmem_limit_bytes=16 * MIB),
         cost_estimate=attend_cost(devices, full, arrived.size * 2),
         name="attend_all",
-    )(table, arrived)
+    )(pltpu.with_memory_space_constraint(table, pltpu.SMEM), arrived)
 
 
 def by_count(counts, blocks):

time: 146 us -> 145 us (level)
  starting transfers between devices: 43.4 us -> 41.5 us
    all_to_all x1, starting transfers between devices: 4.64 us -> 3.05 us  [body(): lax.all_to_all(blended, DEVICES, split_axis=0, concat_axis=0, tiled=True)]
  transfers between devices with their start and end apart: 19 -> 19, of which waited for: 8 -> 9; matrix products, arithmetic and copies ran while one was open for 3% -> 3% of each run, Pallas kernels for 15% -> 14%
where the time goes in v5:
time: 145 us; the launch traced here: 144 us
  waiting for transfers between devices  72.7 us (50%)
  starting transfers between devices  41.5 us (29%)
  Pallas kernels  23.3 us (16%)
  local copies, waits for them, and re-layouts  4.51 us (3%)
    ppermute x17, waiting for transfers between devices, swap(): lax.ppermute(x, axis, [(i, i ^ bit) for i in range(lax.axis_size(axis))])  63.6 us
    ppermute x17, starting transfers between devices, swap(): lax.ppermute(x, axis, [(i, i ^ bit) for i in range(lax.axis_size(axis))])  33.8 us
    pallas_call x1, Pallas kernels, attend_all(): pl.pallas_call(functools.partial(attend_all_kernel, full, place), out_sha...  8.72 us
    all_to_all x1, waiting for transfers between devices, body(): lax.all_to_all(blended, DEVICES, split_axis=0, concat_axis=0, tiled=True)  7.19 us
    pallas_call x1, Pallas kernels, attend_rest(): pl.pallas_call(functools.partial(attend_rest_kernel, head_axis, gather_ax...  5.24 us
    all_to_all x1, starting transfers between devices, body(): lax.all_to_all(sent, DEVICES, split_axis=0, concat_axis=0, tiled=True)  4.56 us
    pallas_call x1, Pallas kernels, pack_all(): pl.pallas_call(functools.partial(pack_all_kernel, full, step), grid=(devi...  4.32 us
    all_to_all x1, starting transfers between devices, body(): lax.all_to_all(blended, DEVICES, split_axis=0, concat_axis=0, tiled=True)  3.05 us
  transfers between devices with their start and end apart: 19, of which 9 were waited for; matrix products, arithmetic and copies ran while one was open for 3% of the time, Pallas kernels for 14%

profile of v5, /device:TPU:0, one launch (start us, length us, event | category | flops | bytes accessed | tf_op | source)
XLA Modules:
  0.0 143.6 jit_solution(10171432445753086304)
XLA Ops:
  0.0 1.8 %pack_rest.1 = (bf16[400,128]{1,0:T(8,128)(2,1)S(1)}, bf16[400,128]{1,0:T(8,128)(2,1)S(1)}, bf16[400,128]{1,0:T(8,128)(2,1)S(1)}, bf16[400,128]{1,0:T(8,128)(2,1...) custom-call(s32[4,12]{1,0:T(4,128)} %lists.1, ...), custom_call_target="tpu_custom_call" | custom-call | bytes 1638400 | tf_op jit(solution)/shard_map/pack_rest/pallas_call | solution.py:109
  1.8 4.1 %collective-permute-start = (bf16[400,128]{1,0:T(8,128)(2,1)S(1)}, bf16[400,128]{1,0:T(8,128)(2,1)S(1)}, u32[]{:S(2)}, u32[]{:S(2)}) collective-permute-start(bf16[400,128]{1,0:T(8,128)(2,1)S(1)} %get-tuple-element.53), channel_id=1, source_target_pairs={{0,16},{4,20},{8,24},{12,28},{16,0},{20,4},{24,8},{28,12},{1,17},{... | collective-permute-start | bytes 307208 | tf_op jit(solution)/shard_map/ppermute | solution.py:31
  7.5 1.8 %collective-permute-start.3 = (bf16[400,128]{1,0:T(8,128)(2,1)S(1)}, bf16[400,128]{1,0:T(8,128)(2,1)S(1)}, u32[]{:S(2)}, u32[]{:S(2)}) collective-permute-start(bf16[400,128]{1,0:T(8,128)(2,1)S(1)} %get-tuple-element.56), channel_id=1, source_target_pairs={{0,8},{4,12},{8,0},{12,4},{16,24},{20,28},{24,16},{28,20},{1,9},{5... | collective-permute-start | bytes 307208 | tf_op jit(solution)/shard_map/ppermute | solution.py:31
  9.3 2.5 %collective-permute-start.4 = (bf16[400,128]{1,0:T(8,128)(2,1)S(1)}, bf16[400,128]{1,0:T(8,128)(2,1)S(1)}, u32[]{:S(2)}, u32[]{:S(2)}) collective-permute-start(bf16[400,128]{1,0:T(8,128)(2,1)S(1)} %get-tuple-element.57), channel_id=1, source_target_pairs={{0,24},{4,28},{8,16},{12,20},{16,8},{20,12},{24,0},{28,4},{1,25},{... | collective-permute-start | bytes 307208 | tf_op jit(solution)/shard_map/ppermute | solution.py:31
  13.1 2.7 %collective-permute-start.5 = (bf16[400,128]{1,0:T(8,128)(2,1)S(1)}, bf16[400,128]{1,0:T(8,128)(2,1)S(1)}, u32[]{:S(2)}, u32[]{:S(2)}) collective-permute-start(bf16[400,128]{1,0:T(8,128)(2,1)S(1)} %get-tuple-element.58), channel_id=1, source_target_pairs={{0,12},{4,8},{8,4},{12,0},{16,28},{20,24},{24,20},{28,16},{1,13},{... | collective-permute-start | bytes 307208 | tf_op jit(solution)/shard_map/ppermute | solution.py:31
  15.8 4.3 %collective-permute-start.6 = (bf16[400,128]{1,0:T(8,128)(2,1)S(1)}, bf16[400,128]{1,0:T(8,128)(2,1)S(1)}, u32[]{:S(2)}, u32[]{:S(2)}) collective-permute-start(bf16[400,128]{1,0:T(8,128)(2,1)S(1)} %get-tuple-element.59), channel_id=1, source_target_pairs={{0,28},{4,24},{8,20},{12,16},{16,12},{20,8},{24,4},{28,0},{1,29},{... | collective-permute-start | bytes 307208 | tf_op jit(solution)/shard_map/ppermute | solution.py:31
  20.1 4.3 %pack_all.1 = bf16[32,384,128]{2,1,0:T(8,128)(2,1)} custom-call(bf16[128,5120]{1,0:T(8,128)(2,1)} %k_ref.2, bf16[128,5120]{1,0:T(8,128)(2,1)} %v_ref.2, bf16[128,5120]{1,0:T(8,128)(2,1)} %q_ref.2), custom_call_target="tpu_custom_call" | custom-call | bytes 6291456 | tf_op jit(solution)/shard_map/pack_all/pallas_call | solution.py:64
  25.2 4.6 %all-to-all-start = ((bf16[32,384,128]{2,1,0:T(8,128)(2,1)}), bf16[32,384,128]{2,1,0:T(8,128)(2,1)S(1)}, u32[]{:S(2)}, u32[]{:S(2)}) async-start(bf16[32,384,128]{2,1,0:T(8,128)(2,1)} %pack_all.1), calls=%async_computation | async-start | bytes 6291456 | tf_op jit(solution)/shard_map/all_to_all | solution.py:400
  29.8 2.1 %stack.1 = (bf16[8,272,128]{2,1,0:T(8,128)(2,1)}, bf16[8,128,128]{2,1,0:T(8,128)(2,1)S(1)}) custom-call(bf16[400,128]{1,0:T(8,128)(2,1)S(1)} %get-tuple-element.61.refs_0_, bf16[400,128]{1,0:T(8,128)(2,1)} %copy-done.2, bf16[400,128]{1,0:T(8,128)(2,1)} %copy-done.4, bf16[400,128]{1,0:T(8,128)(2,1)} %copy-done.6, bf16[400,128]{1,0:T(8,128)(2,1)} %copy-done.1, ...), custom_call_target="tpu_custom_call" | custom-call | bytes 1638400 | tf_op jit(solution)/shard_map/stack/pallas_call | solution.py:244
  32.8 1.7 %collective-permute-start.8 = (bf16[8,272,128]{2,1,0:T(8,128)(2,1)}, bf16[8,272,128]{2,1,0:T(8,128)(2,1)}, u32[]{:S(2)}, u32[]{:S(2)}) collective-permute-start(bf16[8,272,128]{2,1,0:T(8,128)(2,1)} %get-tuple-element.62.refs_1_), channel_id=1, source_target_pairs={{0,2},{1,3},{2,0},{3,1},{4,6},{5,7},{6,4},{7,5},{8,10},{9,11},{10,... | collective-permute-start | bytes 1671176 | tf_op jit(solution)/shard_map/ppermute | solution.py:31
  34.9 1.8 %collective-permute-start.9 = (bf16[8,272,128]{2,1,0:T(8,128)(2,1)}, bf16[8,272,128]{2,1,0:T(8,128)(2,1)}, u32[]{:S(2)}, u32[]{:S(2)}) collective-permute-start(bf16[8,272,128]{2,1,0:T(8,128)(2,1)} %collective-permute-done.7.refs_2_), channel_id=1, source_target_pairs={{0,2},{1,3},{2,0},{3,1},{4,6},{5,7},{6,4},{7,5},{8,10},{9,11},{10,... | collective-permute-start | bytes 1671176 | tf_op jit(solution)/shard_map/ppermute | solution.py:31
  38.9 35.7 %collective-permute-done.8.refs_3_ = bf16[8,272,128]{2,1,0:T(8,128)(2,1)} collective-permute-done((bf16[8,272,128]{2,1,0:T(8,128)(2,1)}, bf16[8,272,128]{2,1,0:T(8,128)(2,1)}, u32[]{:S(2)}, u32[]{:S(2)}) %collective-permute-start.8) | collective-permute-done | bytes 557088 | tf_op jit(solution)/shard_map/ppermute | solution.py:31
  75.4 10.7 %collective-permute-done.9.refs_4_ = bf16[8,272,128]{2,1,0:T(8,128)(2,1)} collective-permute-done((bf16[8,272,128]{2,1,0:T(8,128)(2,1)}, bf16[8,272,128]{2,1,0:T(8,128)(2,1)}, u32[]{:S(2)}, u32[]{:S(2)}) %collective-permute-start.9) | collective-permute-done | bytes 557088 | tf_op jit(solution)/shard_map/ppermute | solution.py:31
  86.9 5.2 %attend_rest.1 = (bf16[128,128]{1,0:T(8,128)(2,1)S(1)}, bf16[128,128]{1,0:T(8,128)(2,1)S(1)}, bf16[128,128]{1,0:T(8,128)(2,1)S(1)}, bf16[128,128]{1,0:T(8,128)(2...) custom-call(s32[104]{0:T(128)S(1)} %reshape.46.table, ...), custom_call_target="tpu_custom_call" | custom-call | flops 805306368 | bytes 2097152 | tf_op jit(solution)/shard_map/attend_rest/pallas_call | solution.py:304
  92.2 4.0 %collective-permute-start.10 = (bf16[128,128]{1,0:T(8,128)(2,1)S(1)}, bf16[128,128]{1,0:T(8,128)(2,1)S(1)}, u32[]{:S(2)}, u32[]{:S(2)}) collective-permute-start(bf16[128,128]{1,0:T(8,128)(2,1)S(1)} %get-tuple-element.68), channel_id=1, source_target_pairs={{0,16},{4,20},{8,24},{12,28},{16,0},{20,4},{24,8},{28,12},{1,17},{... | collective-permute-start | bytes 98312 | tf_op jit(solution)/shard_map/ppermute | solution.py:31
  96.2 2.0 %collective-permute-start.11 = (bf16[128,128]{1,0:T(8,128)(2,1)S(1)}, bf16[128,128]{1,0:T(8,128)(2,1)S(1)}, u32[]{:S(2)}, u32[]{:S(2)}) collective-permute-start(bf16[128,128]{1,0:T(8,128)(2,1)S(1)} %get-tuple-element.69), channel_id=1, source_target_pairs={{0,20},{4,16},{8,28},{12,24},{16,4},{20,0},{24,12},{28,8},{1,21},{... | collective-permute-start | bytes 98312 | tf_op jit(solution)/shard_map/ppermute | solution.py:31
  99.5 2.4 %collective-permute-start.13 = (bf16[128,128]{1,0:T(8,128)(2,1)S(1)}, bf16[128,128]{1,0:T(8,128)(2,1)S(1)}, u32[]{:S(2)}, u32[]{:S(2)}) collective-permute-start(bf16[128,128]{1,0:T(8,128)(2,1)S(1)} %get-tuple-element.71), channel_id=1, source_target_pairs={{0,28},{4,24},{8,20},{12,16},{16,12},{20,8},{24,4},{28,0},{1,29},{... | collective-permute-start | bytes 98312 | tf_op jit(solution)/shard_map/ppermute | solution.py:31
  102.4 1.9 %all-to-all-done.buf = bf16[32,384,128]{2,1,0:T(8,128)(2,1)S(1)} async-done(((bf16[32,384,128]{2,1,0:T(8,128)(2,1)}), bf16[32,384,128]{2,1,0:T(8,128)(2,1)S(1)}, u32[]{:S(2)}, u32[]{:S(2)}) %all-to-all-start) | async-done | bytes 3145760 | tf_op jit(solution)/shard_map/all_to_all | solution.py:400
  104.3 8.7 %attend_all.1 = bf16[32,128,128]{2,1,0:T(8,128)(2,1)} custom-call(s32[448]{0:T(512)S(1)} %pad_add_fusion.table, bf16[32,384,128]{2,1,0:T(8,128)(2,1)S(1)} %all-to-all-done.buf), custom_call_target="tpu_custom_call" | custom-call | flops 3221225472 | bytes 3145728 | tf_op jit(solution)/shard_map/attend_all/pallas_call | solution.py:198
  113.1 3.1 %all-to-all-start.1 = ((bf16[32,128,128]{2,1,0:T(8,128)(2,1)}), bf16[32,128,128]{2,1,0:T(8,128)(2,1)S(1)}, u32[]{:S(2)}, u32[]{:S(2)}) async-start(bf16[32,128,128]{2,1,0:T(8,128)(2,1)} %attend_all.1), calls=%async_computation.1 | async-start | bytes 2097152 | tf_op jit(solution)/shard_map/all_to_all | solution.py:425
  116.1 1.8 %collective-permute-start.14 = (bf16[128,128]{1,0:T(8,128)(2,1)S(1)}, bf16[128,128]{1,0:T(8,128)(2,1)S(1)}, u32[]{:S(2)}, u32[]{:S(2)}) collective-permute-start(bf16[128,128]{1,0:T(8,128)(2,1)S(1)} %get-tuple-element.65), channel_id=1, source_target_pairs={{0,4},{4,0},{8,12},{12,8},{16,20},{20,16},{24,28},{28,24},{1,5},{5... | collective-permute-start | bytes 98312 | tf_op jit(solution)/shard_map/ppermute | solution.py:31
  119.7 4.2 %collective-permute-done.14.refs_2_ = bf16[128,128]{1,0:T(8,128)(2,1)S(1)} collective-permute-done((bf16[128,128]{1,0:T(8,128)(2,1)S(1)}, bf16[128,128]{1,0:T(8,128)(2,1)S(1)}, u32[]{:S(2)}, u32[]{:S(2)}) %collective-permute-start.14) | collective-permute-done | bytes 32800 | tf_op jit(solution)/shard_map/ppermute | solution.py:31
  123.8 10.9 %collective-permute-done.15.refs_3_ = bf16[128,128]{1,0:T(8,128)(2,1)S(1)} collective-permute-done((bf16[128,128]{1,0:T(8,128)(2,1)S(1)}, bf16[128,128]{1,0:T(8,128)(2,1)S(1)}, u32[]{:S(2)}, u32[]{:S(2)}) %collective-permute-start.15) | collective-permute-done | bytes 32800 | tf_op jit(solution)/shard_map/ppermute | solution.py:31
  135.2 7.2 %all-to-all-done.1.refs_0_ = bf16[32,128,128]{2,1,0:T(8,128)(2,1)S(1)} async-done(((bf16[32,128,128]{2,1,0:T(8,128)(2,1)}), bf16[32,128,128]{2,1,0:T(8,128)(2,1)S(1)}, u32[]{:S(2)}, u32[]{:S(2)}) %all-to-all-start.1) | async-done | bytes 1048608 | tf_op jit(solution)/shard_map/all_to_all | solution.py:425
  (54 shorter events, 13.8 us)
Async XLA Ops:
  1.8 11.2 %collective-permute-start = (bf16[400,128]{1,0:T(8,128)(2,1)S(1)}, bf16[400,128]{1,0:T(8,128)(2,1)S(1)}, u32[]{:S(2)}, u32[]{:S(2)}) collective-permute-start(bf16[400,128]{1,0:T(8,128)(2,1)S(1)} %get-tuple-element.53), channel_id=1, source_target_pairs={{0,16},{4,20},{8,24},{12,28},{16,0},{20,4},{24,8},{28,12},{1,17},{... | collective-permute-start | bytes 307208 | tf_op jit(solution)/shard_map/ppermute | solution.py:31
  5.9 9.8 %collective-permute-start.1 = (bf16[400,128]{1,0:T(8,128)(2,1)S(1)}, bf16[400,128]{1,0:T(8,128)(2,1)S(1)}, u32[]{:S(2)}, u32[]{:S(2)}) collective-permute-start(bf16[400,128]{1,0:T(8,128)(2,1)S(1)} %get-tuple-element.54), channel_id=1, source_target_pairs={{0,4},{4,0},{8,12},{12,8},{16,20},{20,16},{24,28},{28,24},{1,5},{5... | collective-permute-start | bytes 307208 | tf_op jit(solution)/shard_map/ppermute | solution.py:31
  7.4 16.9 %collective-permute-start.2 = (bf16[400,128]{1,0:T(8,128)(2,1)S(1)}, bf16[400,128]{1,0:T(8,128)(2,1)S(1)}, u32[]{:S(2)}, u32[]{:S(2)}) collective-permute-start(bf16[400,128]{1,0:T(8,128)(2,1)S(1)} %get-tuple-element.55), channel_id=1, source_target_pairs={{0,20},{4,16},{8,28},{12,24},{16,4},{20,0},{24,12},{28,8},{1,21},{... | collective-permute-start | bytes 307208 | tf_op jit(solution)/shard_map/ppermute | solution.py:31
  7.5 16.9 %collective-permute-start.3 = (bf16[400,128]{1,0:T(8,128)(2,1)S(1)}, bf16[400,128]{1,0:T(8,128)(2,1)S(1)}, u32[]{:S(2)}, u32[]{:S(2)}) collective-permute-start(bf16[400,128]{1,0:T(8,128)(2,1)S(1)} %get-tuple-element.56), channel_id=1, source_target_pairs={{0,8},{4,12},{8,0},{12,4},{16,24},{20,28},{24,16},{28,20},{1,9},{5... | collective-permute-start | bytes 307208 | tf_op jit(solution)/shard_map/ppermute | solution.py:31
  9.3 15.1 %collective-permute-start.4 = (bf16[400,128]{1,0:T(8,128)(2,1)S(1)}, bf16[400,128]{1,0:T(8,128)(2,1)S(1)}, u32[]{:S(2)}, u32[]{:S(2)}) collective-permute-start(bf16[400,128]{1,0:T(8,128)(2,1)S(1)} %get-tuple-element.57), channel_id=1, source_target_pairs={{0,24},{4,28},{8,16},{12,20},{16,8},{20,12},{24,0},{28,4},{1,25},{... | collective-permute-start | bytes 307208 | tf_op jit(solution)/shard_map/ppermute | solution.py:31
  13.1 11.3 %copy-start.1 = (bf16[400,128]{1,0:T(8,128)(2,1)}, bf16[400,128]{1,0:T(8,128)(2,1)S(1)}, u32[]{:S(2)}) copy-start(bf16[400,128]{1,0:T(8,128)(2,1)S(1)} %collective-permute-done.refs_4_) | copy-start | bytes 307204
  13.1 11.4 %collective-permute-start.5 = (bf16[400,128]{1,0:T(8,128)(2,1)S(1)}, bf16[400,128]{1,0:T(8,128)(2,1)S(1)}, u32[]{:S(2)}, u32[]{:S(2)}) collective-permute-start(bf16[400,128]{1,0:T(8,128)(2,1)S(1)} %get-tuple-element.58), channel_id=1, source_target_pairs={{0,12},{4,8},{8,4},{12,0},{16,28},{20,24},{24,20},{28,16},{1,13},{... | collective-permute-start | bytes 307208 | tf_op jit(solution)/shard_map/ppermute | solution.py:31
  15.8 8.6 %copy-start.2 = (bf16[400,128]{1,0:T(8,128)(2,1)}, bf16[400,128]{1,0:T(8,128)(2,1)S(1)}, u32[]{:S(2)}) copy-start(bf16[400,128]{1,0:T(8,128)(2,1)S(1)} %collective-permute-done.1.refs_1_) | copy-start | bytes 307204
  15.8 8.7 %collective-permute-start.6 = (bf16[400,128]{1,0:T(8,128)(2,1)S(1)}, bf16[400,128]{1,0:T(8,128)(2,1)S(1)}, u32[]{:S(2)}, u32[]{:S(2)}) collective-permute-start(bf16[400,128]{1,0:T(8,128)(2,1)S(1)} %get-tuple-element.59), channel_id=1, source_target_pairs={{0,28},{4,24},{8,20},{12,16},{16,12},{20,8},{24,4},{28,0},{1,29},{... | collective-permute-start | bytes 307208 | tf_op jit(solution)/shard_map/ppermute | solution.py:31
  24.4 0.8 copy-start.3
  24.4 0.7 copy-start.6
  24.5 0.7 copy-start.7
  25.2 79.1 %all-to-all-start = ((bf16[32,384,128]{2,1,0:T(8,128)(2,1)}), bf16[32,384,128]{2,1,0:T(8,128)(2,1)S(1)}, u32[]{:S(2)}, u32[]{:S(2)}) async-start(bf16[32,384,128]{2,1,0:T(8,128)(2,1)} %pack_all.1), calls=%async_computation | async-start | bytes 6291456 | tf_op jit(solution)/shard_map/all_to_all | solution.py:400
  32.6 2.3 %collective-permute-start.7 = (bf16[8,272,128]{2,1,0:T(8,128)(2,1)}, bf16[8,272,128]{2,1,0:T(8,128)(2,1)}, u32[]{:S(2)}, u32[]{:S(2)}) collective-permute-start(bf16[8,272,128]{2,1,0:T(8,128)(2,1)} %get-tuple-element.62.refs_1_), channel_id=1, source_target_pairs={{0,1},{1,0},{2,3},{3,2},{4,5},{5,4},{6,7},{7,6},{8,9},{9,8},{10,11... | collective-permute-start | bytes 1671176 | tf_op jit(solution)/shard_map/ppermute | solution.py:31
  32.8 41.8 %collective-permute-start.8 = (bf16[8,272,128]{2,1,0:T(8,128)(2,1)}, bf16[8,272,128]{2,1,0:T(8,128)(2,1)}, u32[]{:S(2)}, u32[]{:S(2)}) collective-permute-start(bf16[8,272,128]{2,1,0:T(8,128)(2,1)} %get-tuple-element.62.refs_1_), channel_id=1, source_target_pairs={{0,2},{1,3},{2,0},{3,1},{4,6},{5,7},{6,4},{7,5},{8,10},{9,11},{10,... | collective-permute-start | bytes 1671176 | tf_op jit(solution)/shard_map/ppermute | solution.py:31
  34.9 51.2 %collective-permute-start.9 = (bf16[8,272,128]{2,1,0:T(8,128)(2,1)}, bf16[8,272,128]{2,1,0:T(8,128)(2,1)}, u32[]{:S(2)}, u32[]{:S(2)}) collective-permute-start(bf16[8,272,128]{2,1,0:T(8,128)(2,1)} %collective-permute-done.7.refs_2_), channel_id=1, source_target_pairs={{0,2},{1,3},{2,0},{3,1},{4,6},{5,7},{6,4},{7,5},{8,10},{9,11},{10,... | collective-permute-start | bytes 1671176 | tf_op jit(solution)/shard_map/ppermute | solution.py:31
  92.2 20.8 %collective-permute-start.10 = (bf16[128,128]{1,0:T(8,128)(2,1)S(1)}, bf16[128,128]{1,0:T(8,128)(2,1)S(1)}, u32[]{:S(2)}, u32[]{:S(2)}) collective-permute-start(bf16[128,128]{1,0:T(8,128)(2,1)S(1)} %get-tuple-element.68), channel_id=1, source_target_pairs={{0,16},{4,20},{8,24},{12,28},{16,0},{20,4},{24,8},{28,12},{1,17},{... | collective-permute-start | bytes 98312 | tf_op jit(solution)/shard_map/ppermute | solution.py:31
  96.2 16.9 %collective-permute-start.11 = (bf16[128,128]{1,0:T(8,128)(2,1)S(1)}, bf16[128,128]{1,0:T(8,128)(2,1)S(1)}, u32[]{:S(2)}, u32[]{:S(2)}) collective-permute-start(bf16[128,128]{1,0:T(8,128)(2,1)S(1)} %get-tuple-element.69), channel_id=1, source_target_pairs={{0,20},{4,16},{8,28},{12,24},{16,4},{20,0},{24,12},{28,8},{1,21},{... | collective-permute-start | bytes 98312 | tf_op jit(solution)/shard_map/ppermute | solution.py:31
  98.1 14.9 %collective-permute-start.12 = (bf16[128,128]{1,0:T(8,128)(2,1)S(1)}, bf16[128,128]{1,0:T(8,128)(2,1)S(1)}, u32[]{:S(2)}, u32[]{:S(2)}) collective-permute-start(bf16[128,128]{1,0:T(8,128)(2,1)S(1)} %get-tuple-element.70), channel_id=1, source_target_pairs={{0,24},{4,28},{8,16},{12,20},{16,8},{20,12},{24,0},{28,4},{1,25},{... | collective-permute-start | bytes 98312 | tf_op jit(solution)/shard_map/ppermute | solution.py:31
  99.5 13.6 %collective-permute-start.13 = (bf16[128,128]{1,0:T(8,128)(2,1)S(1)}, bf16[128,128]{1,0:T(8,128)(2,1)S(1)}, u32[]{:S(2)}, u32[]{:S(2)}) collective-permute-start(bf16[128,128]{1,0:T(8,128)(2,1)S(1)} %get-tuple-element.71), channel_id=1, source_target_pairs={{0,28},{4,24},{8,20},{12,16},{16,12},{20,8},{24,4},{28,0},{1,29},{... | collective-permute-start | bytes 98312 | tf_op jit(solution)/shard_map/ppermute | solution.py:31
  113.1 29.3 %all-to-all-start.1 = ((bf16[32,128,128]{2,1,0:T(8,128)(2,1)}), bf16[32,128,128]{2,1,0:T(8,128)(2,1)S(1)}, u32[]{:S(2)}, u32[]{:S(2)}) async-start(bf16[32,128,128]{2,1,0:T(8,128)(2,1)} %attend_all.1), calls=%async_computation.1 | async-start | bytes 2097152 | tf_op jit(solution)/shard_map/all_to_all | solution.py:425
  116.1 7.7 %collective-permute-start.14 = (bf16[128,128]{1,0:T(8,128)(2,1)S(1)}, bf16[128,128]{1,0:T(8,128)(2,1)S(1)}, u32[]{:S(2)}, u32[]{:S(2)}) collective-permute-start(bf16[128,128]{1,0:T(8,128)(2,1)S(1)} %get-tuple-element.65), channel_id=1, source_target_pairs={{0,4},{4,0},{8,12},{12,8},{16,20},{20,16},{24,28},{28,24},{1,5},{5... | collective-permute-start | bytes 98312 | tf_op jit(solution)/shard_map/ppermute | solution.py:31
  118.0 16.8 %collective-permute-start.15 = (bf16[128,128]{1,0:T(8,128)(2,1)S(1)}, bf16[128,128]{1,0:T(8,128)(2,1)S(1)}, u32[]{:S(2)}, u32[]{:S(2)}) collective-permute-start(bf16[128,128]{1,0:T(8,128)(2,1)S(1)} %get-tuple-element.66), channel_id=1, source_target_pairs={{0,8},{4,12},{8,0},{12,4},{16,24},{20,28},{24,16},{28,20},{1,9},{5... | collective-permute-start | bytes 98312 | tf_op jit(solution)/shard_map/ppermute | solution.py:31
  119.4 15.7 %collective-permute-start.16 = (bf16[128,128]{1,0:T(8,128)(2,1)S(1)}, bf16[128,128]{1,0:T(8,128)(2,1)S(1)}, u32[]{:S(2)}, u32[]{:S(2)}) collective-permute-start(bf16[128,128]{1,0:T(8,128)(2,1)S(1)} %get-tuple-element.67), channel_id=1, source_target_pairs={{0,12},{4,8},{8,4},{12,0},{16,28},{20,24},{24,20},{28,16},{1,13},{... | collective-permute-start | bytes 98312 | tf_op jit(solution)/shard_map/ppermute | solution.py:31
  (3 other events, 2.0 us)
